TPU v7x, 256 devices: a whole 4x4x8 slice. The times are simulated.
256 devices in a mesh: lat: 32 (over z_hi, x, core), lon: 8 (over y, z_lo).
Axes of the slice: x: 4, y: 4, z: 8 (z_hi: 4, z_lo: 2; z = z_hi * 2 + z_lo), core: 2. Of those that a mesh axis runs over, the one named last changes fastest.
Arguments:
- elevation: float32 [16, 2048, 4096], P(None, 'lat', 'lon'), may hold values from -6 to 6
- depth: float32 [2048, 4096], P('lat', 'lon'), may hold values from 0.3 to 3
- friction: float32 [2048, 4096], P('lat', 'lon'), may hold values from 0.05 to 1
- land_mask: int32 [2048, 4096], P('lat', 'lon'), may hold values 0 or 1
- order_map: int32 [128], replicated, may hold values from 0 to 127, each once
- legendre: bfloat16 [128, 2048, 2048], P('lon', 'lat'), may hold values from -0.125 to 0.125
- load: float32 [2048], replicated, may hold values from 0.25 to 4
Outputs:
- elevation_new: float32 [16, 2048, 4096], P(None, 'lat', 'lon')
- sal: float32 [16, 2048, 4096], P(None, 'lat', 'lon')
- friction_new: float32 [2048, 4096], P('lat', 'lon')
Inputs may be any that keep to these rules, and one draw needn't show every extreme that they name: `order_map`: each order 0 to 127 stands in exactly one slot. `land_mask`: 1 marks sea and 0 land.
All inputs are finite; a program needn't handle non-finite values. No bound on the sum of `land_mask` on one device may be relied on, other than what follows from the above.
Results may differ from a plain program's by a relative error of at most 0.0037.
Values may be sent and summed in bfloat16 or wider, within the bound.
No kernel may reach another device: no remote copies, remote signals or barrier semaphores. Data moves between devices by JAX's collectives and lax.ppermute only.
A program may use at most 64 MiB of HBM per device.

v0:
```python
import math

import jax
import jax.numpy as jnp
from jax import lax
from jax.sharding import PartitionSpec as P

SAMPLES = 64


FREQUENCIES = (1.0, 1.0347, 0.9582, 1.0379, 0.5018, 0.4651, 0.4986, 0.4482)
EQ_AMPS = (0.73, 0.34, 0.14, 0.09, 0.42, 0.3, 0.14, 0.06)
LAT_EDGE = 1.3614
RELAX_RATE = 0.1
BASE_FRICTION = 0.05
DRAG_COEFF = 0.5
SPEED_EPS = 0.001
STEP_TIME = 3.0
PRECISE = lax.Precision.HIGHEST


def with_halo(value, sides, width):
    for axis, dim in sides:
        size, length = (lax.axis_size(axis), value.shape[dim])
        up = [(i, (i + 1) % size) for i in range(size)]
        down = [(j, i) for i, j in up]
        last = lax.slice_in_dim(value, length - width, length, axis=dim)
        initial = lax.slice_in_dim(value, 0, width, axis=dim)
        before = lax.ppermute(last, axis, up)
        after = lax.ppermute(initial, axis, down)
        value = jnp.concatenate([before, value, after], axis=dim)
    return value


def fourier_basis(order_map, col_start, lon_cols, lon_count):
    columns = col_start + jnp.arange(lon_cols, dtype=jnp.int32)
    product = order_map[:, None] * columns[None, :] % lon_count
    angles = product.astype(jnp.float32) * (2.0 * math.pi / lon_count)
    scaling = jnp.where(
        order_map > 0, math.sqrt(2.0 / lon_count), math.sqrt(1.0 / lon_count)
    ).astype(jnp.float32)[:, None]
    harmonics = jnp.stack([jnp.cos(angles) * scaling, jnp.sin(angles) * scaling], axis=1)
    return harmonics.reshape(2 * order_map.shape[0], lon_cols)


def equilibrium(lat_start, lat_rows, col_start, lon_cols, lat_count, lon_count):
    lat_step = 2.0 * LAT_EDGE / lat_count
    lat_offset = jnp.asarray(lat_start).astype(jnp.float32)
    latitude = (
        -LAT_EDGE + (lat_offset + jnp.arange(lat_rows, dtype=jnp.float32) + 0.5) * lat_step
    )[:, None]
    columns = jnp.asarray(col_start).astype(jnp.float32) + jnp.arange(lon_cols, dtype=jnp.float32)
    longitude = (columns * (2.0 * math.pi / lon_count))[None, :]
    fields = []
    for member in range(len(EQ_AMPS)):
        if member < 4:
            shape_lat = EQ_AMPS[member] * jnp.cos(latitude) ** 2
            wave_angle = 2.0 * longitude
        else:
            shape_lat = EQ_AMPS[member] * jnp.sin(2.0 * latitude)
            wave_angle = longitude
        fields.append(shape_lat * jnp.cos(wave_angle))
        fields.append(shape_lat * jnp.sin(wave_angle))
    return jnp.stack(fields, axis=0)


def face_flux(depths, drags, diffs, omegas):
    constit = omegas.shape[0]
    pairs = diffs.reshape((constit, 2) + diffs.shape[1:])
    denominator = drags * drags + omegas * omegas * depths * depths
    real_coef = depths * depths * drags / denominator
    imag_coef = depths * depths * depths * omegas / denominator
    flux_real = -(real_coef * pairs[:, 0] - imag_coef * pairs[:, 1])
    flux_imag = -(real_coef * pairs[:, 1] + imag_coef * pairs[:, 0])
    return jnp.stack([flux_real, flux_imag], axis=1).reshape(diffs.shape)


def relax_sweep(padded, elevation, sea_mask, lat_start, lat_count):
    channels, lat_rows, lon_cols = elevation.shape
    surface = padded[:channels]
    sea_depth = padded[channels]
    drag_field = padded[channels + 1]
    lat_step = 2.0 * LAT_EDGE / lat_count
    lat_offset = jnp.asarray(lat_start).astype(jnp.float32)
    cos_center = jnp.cos(
        -LAT_EDGE + (lat_offset + jnp.arange(lat_rows, dtype=jnp.float32) + 0.5) * lat_step
    )[:, None]
    cos_face = jnp.cos(
        -LAT_EDGE + (lat_offset + jnp.arange(lat_rows + 1, dtype=jnp.float32)) * lat_step
    )[:, None]
    omegas = jnp.asarray(FREQUENCIES, dtype=jnp.float32)[:, None, None]
    east_depth = jnp.sqrt(sea_depth[1:-1, :-1] * sea_depth[1:-1, 1:])
    east_drag = 0.5 * (drag_field[1:-1, :-1] + drag_field[1:-1, 1:])
    east_diff = (surface[:, 1:-1, 1:] - surface[:, 1:-1, :-1]) / cos_center
    north_depth = jnp.sqrt(sea_depth[:-1, 1:-1] * sea_depth[1:, 1:-1])
    north_drag = 0.5 * (drag_field[:-1, 1:-1] + drag_field[1:, 1:-1])
    north_diff = (surface[:, 1:, 1:-1] - surface[:, :-1, 1:-1]) * cos_face
    east_flux = face_flux(east_depth, east_drag, east_diff, omegas)
    north_flux = face_flux(north_depth, north_drag, north_diff, omegas)
    divergence = (
        east_flux[:, :, 1:] - east_flux[:, :, :-1] + north_flux[:, 1:] - north_flux[:, :-1]
    ) / cos_center
    constit = omegas.shape[0]
    current = elevation.reshape(constit, 2, lat_rows, lon_cols)
    div_pairs = divergence.reshape(constit, 2, lat_rows, lon_cols)
    resid_real = div_pairs[:, 0] + omegas * current[:, 1]
    resid_imag = div_pairs[:, 1] - omegas * current[:, 0]
    residual = jnp.stack([resid_real, resid_imag], axis=1).reshape(channels, lat_rows, lon_cols)
    elevation_new = (elevation - RELAX_RATE * residual) * sea_mask
    east_cell = 0.5 * (east_flux[:, :, 1:] + east_flux[:, :, :-1])
    north_cell = 0.5 * (north_flux[:, 1:] + north_flux[:, :-1])
    return (elevation_new, east_cell, north_cell)


def sample_table():
    sample_time = STEP_TIME * jnp.arange(SAMPLES, dtype=jnp.float32)[:, None]
    omegas = jnp.asarray(FREQUENCIES, dtype=jnp.float32)[None, :]
    phases = sample_time * omegas
    return jnp.stack([jnp.cos(phases), jnp.sin(phases)], axis=2).reshape(
        SAMPLES, 2 * len(FREQUENCIES)
    )


def clear_poles(padded, band_count):
    band_index = lax.axis_index("lat")
    row_ids = jnp.arange(padded.shape[1])
    dropped = (row_ids == 0) & (band_index == 0) | (row_ids == padded.shape[1] - 1) & (
        band_index == band_count - 1
    )
    return jnp.where(dropped[None, :, None], 0.0, padded)


def on_device(elevation, depth, friction, land_mask, order_map, legendre, load):
    channels, lat_rows, lon_cols = elevation.shape
    slot_count = legendre.shape[0]
    band_count = lax.axis_size("lat")
    sector_count = lax.axis_size("lon")
    lat_count = lat_rows * band_count
    lon_count = lon_cols * sector_count
    lat_start = lax.axis_index("lat") * lat_rows
    col_start = lax.axis_index("lon") * lon_cols
    sea_mask = land_mask.astype(jnp.float32)
    equil_tide = equilibrium(lat_start, lat_rows, col_start, lon_cols, lat_count, lon_count)
    sea_depth = depth * sea_mask
    harmonics = fourier_basis(order_map, col_start, lon_cols, lon_count)
    flat_field = (elevation * sea_mask).reshape(channels * lat_rows, lon_cols)
    part_basis = harmonics
    product = lax.dot_general(
        part_basis,
        flat_field,
        (((1,), (1,)), ((), ())),
        precision=PRECISE,
        preferred_element_type=jnp.float32,
    )
    owned = lax.psum_scatter(
        product.reshape(slot_count * lax.axis_size("lon"), 2 * channels * lat_rows),
        "lon",
        scatter_dimension=0,
        tiled=True,
    )
    fourier = owned.reshape(slot_count, 2 * channels, lat_rows).astype(jnp.bfloat16)
    coeffs = jnp.einsum("sjn,sqj->sqn", legendre, fourier, preferred_element_type=jnp.float32)
    summed = lax.psum(coeffs, "lat")
    scaled = (summed * load[None, None, :]).astype(jnp.bfloat16)
    synthesis = jnp.einsum("sjn,sqn->sqj", legendre, scaled, preferred_element_type=jnp.float32)
    blocks = lax.all_gather(synthesis, "lon", axis=0, tiled=True)
    number = blocks.shape[0]
    part_basis = harmonics
    left_side = blocks.reshape(2 * number, channels * lat_rows)
    sal = lax.dot_general(
        left_side,
        part_basis,
        (((0,), (0,)), ((), ())),
        precision=PRECISE,
        preferred_element_type=jnp.float32,
    ).reshape(channels, lat_rows, lon_cols)
    stacked = jnp.concatenate(
        [elevation - equil_tide - sal, sea_depth[None], friction[None]], axis=0
    )
    padded = clear_poles(with_halo(stacked, (("lat", 1), ("lon", 2)), 1), band_count)
    elevation_new, east_cell, north_cell = relax_sweep(
        padded, elevation, sea_mask, lat_start, lat_count
    )
    weights_all = sample_table()
    east_time = jnp.einsum("sc,cjl->sjl", weights_all, east_cell, precision=PRECISE)
    north_time = jnp.einsum("sc,cjl->sjl", weights_all, north_cell, precision=PRECISE)
    speeds = jnp.sqrt(east_time * east_time + north_time * north_time + SPEED_EPS * SPEED_EPS)
    friction_new = BASE_FRICTION + DRAG_COEFF * jnp.sum(speeds, axis=0) / SAMPLES
    return (elevation_new, sal, friction_new)


def solution(mesh):
    return jax.shard_map(
        on_device,
        mesh=mesh,
        in_specs=(
            P(None, "lat", "lon"),
            P("lat", "lon"),
            P("lat", "lon"),
            P("lat", "lon"),
            P(),
            P("lon", "lat", None),
            P(),
        ),
        out_specs=(P(None, "lat", "lon"), P(None, "lat", "lon"), P("lat", "lon")),
        check_vma=False,
    )
```

profile of v0, /device:TPU:71, one launch (start us, length us, event | category | flops | bytes accessed | tf_op | source)
XLA Modules:
  0.0 512.9 jit_solution(1118835266222028482)
XLA Ops:
  9.0 1.8 cosine_multiply_fusion
  11.9 2.9 fusion.42
  14.8 2.5 reshape.1127
  17.4 41.1 %reduce-scatter.2.cloned.1.call-done = f32[16,2048]{1,0:T(8,128)} async-done(((f32[128,2048]{1,0:T(8,128)}), f32[16,2048]{1,0:T(8,128)}) %reduce-scatter.2.cloned.1.call-update) | async-done | bytes 131088 | tf_op jit(solution)/shard_map/reduce_scatter | solution.py:155
  59.5 4.9 fusion.43
  72.4 296.3 %all-reduce.2.cloned.1.call-done = f32[16,32,2048]{2,1,0:T(8,128)} async-done(((f32[16,32,2048]{2,1,0:T(8,128)}), f32[16,32,2048]{2,1,0:T(8,128)}) %all-reduce.2.cloned.1.call-update) | async-done | bytes 4194320 | tf_op jit(solution)/shard_map/psum | solution.py:163
  368.7 5.4 %fusion.2 = f32[16,32,64]{2,1,0:T(8,128)} fusion(bf16[16,64,2048]{2,1,0:T(8,128)(2,1)} %param.14, f32[16,32,2048]{2,1,0:T(8,128)} %all-reduce.2.cloned.1.call-done, f32[2048]{0:T(1024)S(1)} %copy-done.9), kind=kOutput, calls=%fused_computation.9 | convolution fusion | flops 136314880 | bytes 8527872 | tf_op jit(solution)/shard_map/sjn,sqn->sqj/dot_general | solution.py:165
  381.0 49.0 %all-gather.2.cloned.1.call-done = f32[128,32,64]{2,1,0:T(8,128)} async-done(((f32[16,32,64]{2,1,0:T(8,128)}), f32[128,32,64]{2,1,0:T(8,128)}) %all-gather.2.cloned.1.call-update) | async-done | bytes 1048592 | tf_op jit(solution)/shard_map/all_gather | solution.py:166
  430.1 2.7 reshape.1128
  432.8 1.6 copy.41
  434.4 5.1 subtract_subtract_fusion
  439.5 1.3 copy-done.1
  440.9 3.4 collective-permute-start
  446.0 6.6 %collective-permute-done.1 = f32[18,1,512]{2,1,0:T(1,128)} collective-permute-done((f32[18,1,512]{2,1,0:T(1,128)S(1)}, f32[18,1,512]{2,1,0:T(1,128)}, u32[]{:S(2)}, u32[]{:S(2)}) %collective-permute-start.1) | collective-permute-done | bytes 36896 | tf_op jit(solution)/shard_map/ppermute | solution.py:30
  452.6 1.6 pad_maximum_fusion.6
  457.7 1.3 copy.50
  459.0 2.7 collective-permute-done.2
  463.1 3.2 maximum_select_fusion
  467.0 1.5 fusion.1
  472.6 6.1 %subtract_divide_fusion = f32[16,64,512]{2,0,1:T(8,128)S(1)} fusion(f32[16,64,512]{2,1,0:T(8,128)S(1)} %get-tuple-element.20, f32[16,64,512]{2,1,0:T(8,128)S(1)} %get-tuple-element.19, f32[16,64,512]{2,1,0:T(8,128)S(1)} %get-tuple-element.16, f32[16,64,512]{2,1,0:T(8,128)S(1)} %get-tuple-element.15, f32[64]{0:T(128)S(1)} %copy-done.13), kind=kLoop, calls=%fused_computation.18 | loop fusion | flops 2097152 | bytes 10486016 | tf_op jit(solution)/shard_map/div | solution.py:100
  478.7 1.2 copy.53
  481.4 1.8 fusion.3
  483.2 9.6 %fusion.6 = f32[64,64,512]{2,0,1:T(8,128)S(1)} fusion(f32[64,16,1]{0,1,2:T(8,128)S(1)} %bitcast.44, f32[16,64,512]{2,1,0:T(8,128)S(1)} %get-tuple-element.16, f32[16,64,512]{2,1,0:T(8,128)S(1)} %get-tuple-element.15), kind=kOutput, calls=%fused_computation.15 | convolution fusion | flops 403701760 | bytes 12587008 | tf_op jit(solution)/shard_map/sc,cjl->sjl/dot_general | solution.py:185
  492.9 12.6 %sqrt_reduce_fusion = f32[64,512]{1,0:T(8,128)S(1)} fusion(f32[64,64,512]{2,0,1:T(8,128)S(1)} %fusion.6, f32[64,16,1]{0,1,2:T(8,128)S(1)} %bitcast.45, f32[16,64,512]{2,1,0:T(8,128)S(1)} %get-tuple-element.20, f32[16,64,512]{2,1,0:T(8,128)S(1)} %get-tuple-element.19), kind=kOutput, calls=%fused_computation | convolution fusion | flops 414154752 | bytes 12718080 | tf_op jit(solution)/shard_map/sc,cjl->sjl/dot_general | solution.py:186
  (99 shorter events, 32.2 us)
Async XLA Ops:
  7.2 4.4 copy-start
  7.2 51.3 %reduce-scatter.2.cloned.1.call-start = ((), (), s32[]{:S(2)}) async-start(), calls=%async_computation.1 | async-start | bytes 1179648 | tf_op jit(solution)/shard_map/reduce_scatter | solution.py:155
  8.9 2.9 copy-start.3
  17.3 351.4 %all-reduce.2.cloned.1.call-start = ((), (), s32[]{:S(2)}) async-start(), calls=%async_computation.2 | async-start | bytes 8388608 | tf_op jit(solution)/shard_map/psum | solution.py:163
  64.4 0.7 copy-start.10
  64.4 304.3 %copy-start.9 = (f32[2048]{0:T(1024)S(1)}, f32[2048]{0:T(1024)}, u32[]{:S(2)}) copy-start(f32[2048]{0:T(1024)} %param.15) | copy-start | bytes 24580
  64.5 365.6 %all-gather.2.cloned.1.call-start = ((), (), s32[]{:S(2)}) async-start(), calls=%async_computation.3 | async-start | bytes 2359296 | tf_op jit(solution)/shard_map/all_gather | solution.py:166
  374.1 6.9 %copy-start.5 = (s32[64,512]{1,0:T(8,128)S(1)}, s32[64,512]{1,0:T(8,128)}, u32[]{:S(2)}) copy-start(s32[64,512]{1,0:T(8,128)} %param.12) | copy-start | bytes 393220
  374.1 6.9 %copy-start.7 = (f32[64,512]{1,0:T(8,128)S(1)}, f32[64,512]{1,0:T(8,128)}, u32[]{:S(2)}) copy-start(f32[64,512]{1,0:T(8,128)} %param.10) | copy-start | bytes 393220
  434.4 6.5 %copy-start.2 = (f32[64,512]{1,0:T(8,128)S(1)}, f32[64,512]{1,0:T(8,128)}, u32[]{:S(2)}) copy-start(f32[64,512]{1,0:T(8,128)} %param.11) | copy-start | bytes 393220
  439.5 1.3 copy-start.1
  440.9 4.5 collective-permute-start
  444.3 8.3 %collective-permute-start.1 = (f32[18,1,512]{2,1,0:T(1,128)S(1)}, f32[18,1,512]{2,1,0:T(1,128)}, u32[]{:S(2)}, u32[]{:S(2)}) collective-permute-start(f32[18,1,512]{2,1,0:T(1,128)S(1)} %get-tuple-element.22), channel_id=1, source_target_pairs={{8,0},{16,8},{24,16},{32,24},{40,32},{48,40},{56,48},{64,56},{72,6... | collective-permute-start | bytes 110600 | tf_op jit(solution)/shard_map/ppermute | solution.py:30
  445.3 0.6 copy-start.6
  455.3 6.7 %collective-permute-start.3 = (f32[18,66,1]{1,2,0:T(1,128)S(1)}, f32[18,66,1]{1,2,0:T(1,128)}, u32[]{:S(2)}, u32[]{:S(2)}) collective-permute-start(f32[18,66,1]{1,2,0:T(1,128)S(1)} %copy.43), channel_id=1, source_target_pairs={{1,0},{2,1},{3,2},{4,3},{5,4},{6,5},{7,6},{0,7},{9,8},{10,9},{11,1... | collective-permute-start | bytes 14264 | tf_op jit(solution)/shard_map/ppermute | solution.py:30
  456.4 5.2 %collective-permute-start.2 = (f32[18,66,1]{1,2,0:T(1,128)}, f32[18,66,1]{1,2,0:T(1,128)S(1)}, u32[]{:S(2)}, u32[]{:S(2)}) collective-permute-start(f32[18,66,1]{1,2,0:T(1,128)} %copy.42), channel_id=1, source_target_pairs={{0,1},{1,2},{2,3},{3,4},{4,5},{5,6},{6,7},{7,0},{8,9},{9,10},{10,1... | collective-permute-start | bytes 14264 | tf_op jit(solution)/shard_map/ppermute | solution.py:29
  466.3 0.7 copy-start.14
  467.0 1.5 copy-start.13
  468.5 1.0 copy-start.11
  468.5 1.0 copy-start.12
  480.5 0.9 copy-start.4
  481.4 1.8 copy-start.8
Sparse Core Ops, SparseCore 0:
  17.5 40.9 reduce-scatter.1
  64.6 304.0 all-reduce.1
  374.3 55.7 all-gather.1
where the time goes:
time: 522 us; the launch traced here: 513 us
  waiting for transfers between devices  396 us (76%)
  matrix products  40.6 us (8%)
  other arithmetic  38.2 us (7%)
  local copies, waits for them, and re-layouts  18.3 us (4%)
  between operations  14.3 us (3%)
  starting transfers between devices  5.64 us (1%)
    psum x1, waiting for transfers between devices, on_device(): summed = lax.psum(coeffs, 'lat')  296 us
    all_gather x1, waiting for transfers between devices, on_device(): blocks = lax.all_gather(synthesis, 'lon', axis=0, tiled=True)  49 us
    reduce_scatter x1, waiting for transfers between devices, on_device(): lax.psum_scatter(product.reshape(slot_count * lax.axis_size('lon'), 2 * c...  41.1 us
    dot_general x1, matrix products, on_device(): jnp.einsum('sc,cjl->sjl', weights_all, north_cell, precision=PRECISE)  12.6 us
    unnamed x15, other arithmetic  11 us
  transfers between devices with their start and end apart: 7, of which 6 were waited for; matrix products, arithmetic and copies ran while one was open for 3% of the time, Pallas kernels for 0%

commit v1 on v0

v1 whole, which is shorter than its diff:
```python
import functools
import math

import jax
import jax.numpy as jnp
import numpy as np
from jax import lax
from jax.experimental import pallas as pl
from jax.experimental.pallas import tpu as pltpu
from jax.sharding import Mesh, PartitionSpec as P

SAMPLES = 64
FREQUENCIES = (1.0, 1.0347, 0.9582, 1.0379, 0.5018, 0.4651, 0.4986, 0.4482)
EQ_AMPS = (0.73, 0.34, 0.14, 0.09, 0.42, 0.3, 0.14, 0.06)
LAT_EDGE = 1.3614
RELAX_RATE = 0.1
BASE_FRICTION = 0.05
DRAG_COEFF = 0.5
SPEED_EPS = 0.001
STEP_TIME = 3.0
NLAT = 2048
NLON = 4096
LAT_STEP = 2.0 * LAT_EDGE / NLAT
ROWS = 64
COLS = 512
CH = 16
DEG = 2048
F32 = jnp.float32
BF16 = jnp.bfloat16
VMEM_LIMIT = 52 * 1024 * 1024


def params():
    return pltpu.CompilerParams(vmem_limit_bytes=VMEM_LIMIT)


def unit_circle(k):
    k = k & (NLON - 1)
    quad = (k + 512) >> 10
    t = (k - (quad << 10)).astype(F32) * (2.0 * math.pi / NLON)
    q = quad & 3
    t2 = t * t
    s = t * (1.0 + t2 * (-1.0 / 6 + t2 * (1.0 / 120 + t2 * (-1.0 / 5040 + t2 * (1.0 / 362880)))))
    c = 1.0 + t2 * (-0.5 + t2 * (1.0 / 24 + t2 * (-1.0 / 720 + t2 * (1.0 / 40320))))
    swap = (q & 1) == 1
    cos = jnp.where(swap, s, c)
    sin = jnp.where(swap, c, s)
    cos = jnp.where((q == 1) | (q == 2), -cos, cos)
    sin = jnp.where(q >= 2, -sin, sin)
    return cos, sin


def split(x):
    hi = x.astype(BF16)
    lo = (x - hi.astype(F32)).astype(BF16)
    return hi, lo


NT = (((1,), (1,)), ((), ()))
TN = (((0,), (0,)), ((), ()))


def dft_kernel(idx, om_ref, elev_ref, mask_ref, part_ref, harm_ref):
    @pl.when(pl.program_id(0) == 0)
    def _():
        lane = lax.broadcasted_iota(jnp.int32, (8, COLS + 128), 1)
        off = jnp.where(lane < COLS, lane, jnp.where(lane < COLS + 64, -1, COLS))
        col = idx[1] * COLS + off
        for g in range(16):
            m = om_ref[8 * g : 8 * g + 8, :]
            cos, sin = unit_circle(m * col)
            scale = jnp.where(m > 0, math.sqrt(2.0 / NLON), math.sqrt(1.0 / NLON)).astype(F32)
            hi, lo = split(jnp.concatenate([cos * scale, sin * scale], axis=0))
            harm_ref[16 * g : 16 * g + 16, :] = hi
            harm_ref[256 + 16 * g : 256 + 16 * g + 16, :] = lo

    mask = mask_ref[...].astype(F32)
    field = jnp.concatenate([elev_ref[c] * mask for c in range(4)], axis=0)
    hi, lo = split(field)
    both = lax.dot_general(harm_ref[:, :COLS], hi, NT, preferred_element_type=F32)
    small = lax.dot_general(harm_ref[:256, :COLS], lo, NT, preferred_element_type=F32)
    out = both[:256] + (both[256:] + small)
    part_ref[...] = out.reshape(16, 16, 256).astype(part_ref.dtype)


def dft(idx, om, elevation, mask, dtype):
    return pl.pallas_call(
        dft_kernel,
        grid_spec=pltpu.PrefetchScalarGridSpec(
            num_scalar_prefetch=1,
            grid=(4,),
            in_specs=[
                pl.BlockSpec((128, 1), lambda i, x: (0, 0)),
                pl.BlockSpec((4, ROWS, COLS), lambda i, x: (i, 0, 0)),
                pl.BlockSpec((ROWS, COLS), lambda i, x: (0, 0)),
            ],
            out_specs=[
                pl.BlockSpec((16, 16, 256), lambda i, x: (0, 0, i)),
                pl.BlockSpec((512, COLS + 128), lambda i, x: (0, 0)),
            ],
        ),
        out_shape=[
            jax.ShapeDtypeStruct((16, 16, 1024), dtype),
            jax.ShapeDtypeStruct((512, COLS + 128), BF16),
        ],
        compiler_params=params(),
        name="dft",
    )(idx, om, elevation, mask)


def analyse_kernel(idx, r_ref, own_ref, rcv_ref, out_ref, a_ref):
    @pl.when(pl.program_id(0) == 0)
    def _():
        me = idx[2]
        lane = lax.broadcasted_iota(jnp.int32, (16, 128), 1)
        low = lane < 64
        for t in range(8):
            tiles = []
            for which in (me, 1 - me):
                acc = r_ref[which, :, 128 * t : 128 * t + 128].astype(F32)
                for d in range(1, 8):
                    acc = acc + r_ref[2 * d + which, :, 128 * t : 128 * t + 128].astype(F32)
                tiles.append(acc)
            f0, f1 = tiles
            even = jnp.where(low, f0, pltpu.roll(f1, 64, 1))
            odd = jnp.where(low, pltpu.roll(f0, 64, 1), f1)
            for ch, val in ((2 * t, even), (2 * t + 1, odd)):
                for p in range(2):
                    for s in range(8):
                        a_ref[s, 16 * p + ch : 16 * p + ch + 1, :] = val[8 * p + s : 8 * p + s + 1, :]

    i = pl.program_id(0)
    for s in range(2):
        a = a_ref[2 * i + s].astype(BF16)
        table = jnp.concatenate([own_ref[s], rcv_ref[s]], axis=0)
        out_ref[s] = jnp.dot(a, table, preferred_element_type=F32).astype(out_ref.dtype)


def analyse(idx, received, legendre, swapped, dtype):
    return pl.pallas_call(
        analyse_kernel,
        grid_spec=pltpu.PrefetchScalarGridSpec(
            num_scalar_prefetch=1,
            grid=(4,),
            in_specs=[
                pl.BlockSpec((16, 16, 1024), lambda i, x: (0, 0, 0)),
                pl.BlockSpec((2, ROWS, DEG), lambda i, x: (4 * x[2] + i, 0, 0)),
                pl.BlockSpec((2, ROWS, DEG), lambda i, x: (i, 0, 0)),
            ],
            out_specs=pl.BlockSpec((2, 32, DEG), lambda i, x: (i, 0, 0)),
            scratch_shapes=[pltpu.VMEM((8, 32, 128), F32)],
        ),
        out_shape=jax.ShapeDtypeStruct((8, 32, DEG), dtype),
        compiler_params=params(),
        name="analyse",
    )(idx, received, legendre, swapped)


def synth_kernel(idx, sc_ref, own_ref, rcv_ref, out_ref, t_ref):
    i = pl.program_id(0)
    for s in range(2):
        table = jnp.concatenate([own_ref[s], rcv_ref[s]], axis=0)
        t_ref[2 * i + s] = lax.dot_general(sc_ref[s], table, NT, preferred_element_type=F32)

    @pl.when(i == 3)
    def _():
        me = idx[2]
        lane = lax.broadcasted_iota(jnp.int32, (8, 128), 1)
        low = lane < 64
        for t in range(8):
            own, oth = [], []
            for p in range(2):
                r0 = 16 * p + 2 * t
                v0 = jnp.concatenate([t_ref[s, r0 : r0 + 1, :] for s in range(8)], axis=0)
                v1 = jnp.concatenate([t_ref[s, r0 + 1 : r0 + 2, :] for s in range(8)], axis=0)
                own.append(jnp.where(low, v0, pltpu.roll(v1, 64, 1)))
                oth.append(jnp.where(low, pltpu.roll(v0, 64, 1), v1))
            own = jnp.concatenate(own, axis=0).astype(out_ref.dtype)
            oth = jnp.concatenate(oth, axis=0).astype(out_ref.dtype)
            for d in range(8):
                out_ref[2 * d + me, :, 128 * t : 128 * t + 128] = own
                out_ref[2 * d + 1 - me, :, 128 * t : 128 * t + 128] = oth


def synthesise(idx, scaled, legendre, swapped, dtype):
    return pl.pallas_call(
        synth_kernel,
        grid_spec=pltpu.PrefetchScalarGridSpec(
            num_scalar_prefetch=1,
            grid=(4,),
            in_specs=[
                pl.BlockSpec((2, 32, DEG), lambda i, x: (i, 0, 0)),
                pl.BlockSpec((2, ROWS, DEG), lambda i, x: (4 * x[2] + i, 0, 0)),
                pl.BlockSpec((2, ROWS, DEG), lambda i, x: (i, 0, 0)),
            ],
            out_specs=pl.BlockSpec((16, 16, 1024), lambda i, x: (0, 0, 0)),
            scratch_shapes=[pltpu.VMEM((8, 32, 128), F32)],
        ),
        out_shape=jax.ShapeDtypeStruct((16, 16, 1024), dtype),
        compiler_params=params(),
        name="synthesise",
    )(idx, scaled, legendre, swapped)


def sal_kernel(g_ref, harm_ref, sal_ref, halo_ref):
    g = g_ref[...]
    hi = lax.dot_general(g, harm_ref[:256, :], TN, preferred_element_type=F32)
    lo = lax.dot_general(g, harm_ref[256:, :], TN, preferred_element_type=F32)
    out = hi + lo
    for c in range(4):
        sal_ref[c] = out[64 * c : 64 * c + 64, :COLS]
        halo_ref[c] = out[64 * c : 64 * c + 64, COLS:]


def inverse(g, harm):
    return pl.pallas_call(
        sal_kernel,
        grid=(4,),
        in_specs=[
            pl.BlockSpec((256, 256), lambda i: (0, i)),
            pl.BlockSpec((512, COLS + 128), lambda i: (0, 0)),
        ],
        out_specs=[
            pl.BlockSpec((4, ROWS, COLS), lambda i: (i, 0, 0)),
            pl.BlockSpec((4, ROWS, 128), lambda i: (i, 0, 0)),
        ],
        out_shape=[
            jax.ShapeDtypeStruct((CH, ROWS, COLS), F32),
            jax.ShapeDtypeStruct((CH, ROWS, 128), F32),
        ],
        compiler_params=params(),
        name="inverse",
    )(g, harm)


def lat_of(row):
    return -LAT_EDGE + row * LAT_STEP


def sweep_kernel(
    idx, elev_ref, sal_ref, salh_ref, salr_ref, depth_ref, fric_ref, mask_ref, rows_ref, lonh_ref, w_ref,
    new_ref, fnew_ref, spad, dpad, fpad, nf,
):
    b = pl.program_id(0)
    lat0 = idx[0] * ROWS

    @pl.when(b == 0)
    def _():
        lane = lax.broadcasted_iota(jnp.int32, (8, COLS), 1)
        col = idx[1] * COLS + lane
        c1, s1 = unit_circle(col)
        c2, s2 = unit_circle(2 * col)
        waves = (c2[:1], s2[:1], c1[:1], s1[:1])

        def shapes(first, count):
            row = first.astype(F32) + lax.broadcasted_iota(jnp.int32, (count, COLS), 0).astype(F32)
            phi = lat_of(row + 0.5)
            cosphi = jnp.cos(phi)
            return cosphi * cosphi, jnp.sin(2.0 * phi)

        sq, s2phi = shapes(lat0, ROWS)
        up_sq, up_s2 = shapes(lat0 - 1, 8)
        dn_sq, dn_s2 = shapes(lat0 + ROWS, 8)
        for ch in range(CH):
            k = ch // 2
            wave = waves[(0 if k < 4 else 2) + ch % 2]
            eq = EQ_AMPS[k] * (sq if k < 4 else s2phi) * wave
            spad[ch, 8 : 8 + ROWS, :] = elev_ref[ch] - eq - sal_ref[ch]
            up = EQ_AMPS[k] * (up_sq if k < 4 else up_s2)[:1] * wave
            dn = EQ_AMPS[k] * (dn_sq if k < 4 else dn_s2)[:1] * wave
            spad[ch, 7:8, :] = rows_ref[0, ch : ch + 1, :] - up - salr_ref[0, ch : ch + 1, :]
            spad[ch, 8 + ROWS : 9 + ROWS, :] = rows_ref[1, ch : ch + 1, :] - dn - salr_ref[1, ch : ch + 1, :]
        dpad[8 : 8 + ROWS, :] = depth_ref[...] * mask_ref[...].astype(F32)
        fpad[8 : 8 + ROWS, :] = fric_ref[...]
        top = jnp.where(idx[0] == 0, 0.0, 1.0)
        bottom = jnp.where(idx[0] == 31, 0.0, 1.0)
        dpad[7:8, :] = rows_ref[0, 16:17, :] * top
        dpad[8 + ROWS : 9 + ROWS, :] = rows_ref[1, 16:17, :] * bottom
        fpad[7:8, :] = rows_ref[0, 17:18, :]
        fpad[8 + ROWS : 9 + ROWS, :] = rows_ref[1, 17:18, :]

        for blk in range(9):
            lo = 8 * blk
            row = (lat0 + lo).astype(F32) + lax.broadcasted_iota(jnp.int32, (8, 128), 0).astype(F32)
            cosf = jnp.tile(jnp.cos(lat_of(row)), (1, 4))
            hh = dpad[8 + lo : 16 + lo, :] * dpad[7 + lo : 15 + lo, :]
            h = jnp.sqrt(hh)
            r = 0.5 * (fpad[8 + lo : 16 + lo, :] + fpad[7 + lo : 15 + lo, :])
            for k in range(8):
                om = FREQUENCIES[k]
                inv = -hh / (r * r + (om * om) * hh)
                rc = inv * r * cosf
                ic = inv * h * om * cosf
                dr = spad[2 * k, 8 + lo : 16 + lo, :] - spad[2 * k, 7 + lo : 15 + lo, :]
                di = spad[2 * k + 1, 8 + lo : 16 + lo, :] - spad[2 * k + 1, 7 + lo : 15 + lo, :]
                nf[2 * k, lo : lo + 8, :] = rc * dr - ic * di
                nf[2 * k + 1, lo : lo + 8, :] = rc * di + ic * dr

    base = pl.multiple_of(8 * b, 8)
    own = pl.ds(base + 8, 8)
    row = (lat0 + base).astype(F32) + lax.broadcasted_iota(jnp.int32, (8, 128), 0).astype(F32)
    phi = lat_of(row + 0.5)
    rcos1 = 1.0 / jnp.cos(phi)
    rcos = jnp.tile(rcos1, (1, 4))
    lane = lax.broadcasted_iota(jnp.int32, (8, COLS), 1)
    last = lane == COLS - 1
    first = lane == 0
    tile_lane = lax.broadcasted_iota(jnp.int32, (8, 128), 1)
    col = idx[1] * COLS + jnp.where(tile_lane < 64, -1, COLS)
    c1, s1 = unit_circle(col)
    c2, s2 = unit_circle(2 * col)
    waves = (c2, s2, c1, s1)
    cosphi = jnp.cos(phi)
    sq, s2phi = cosphi * cosphi, jnp.sin(2.0 * phi)

    def east_of(x, halo):
        wide = jnp.tile(halo, (1, 4))
        return jnp.where(last, wide, pltpu.roll(x, COLS - 1, 1))

    d = dpad[own, :]
    f = fpad[own, :]
    dh = lonh_ref[16]
    fh = lonh_ref[17]
    hh = d * east_of(d, dh)
    h = jnp.sqrt(hh)
    r = 0.5 * (f + east_of(f, fh))
    hhw = d[:, :128] * dh
    hw = jnp.sqrt(hhw)
    rw = 0.5 * (f[:, :128] + fh)
    mask = mask_ref[pl.ds(base, 8), :].astype(F32)
    ecell, ncell = [], []
    for k in range(8):
        om = FREQUENCIES[k]
        inv = -hh / (r * r + (om * om) * hh)
        rc = inv * r * rcos
        ic = inv * h * om * rcos
        invw = -hhw / (rw * rw + (om * om) * hhw)
        rcw = invw * rw * rcos1
        icw = invw * hw * om * rcos1
        diffs, wdiffs = [], []
        for ch in (2 * k, 2 * k + 1):
            s = spad[ch, own, :]
            eq = EQ_AMPS[k] * (sq if k < 4 else s2phi) * waves[(0 if k < 4 else 2) + ch % 2]
            sh = lonh_ref[ch] - eq - salh_ref[ch]
            diffs.append(east_of(s, sh) - s)
            wdiffs.append(s[:, :128] - sh)
        flux = (rc * diffs[0] - ic * diffs[1], rc * diffs[1] + ic * diffs[0])
        fluxw = (rcw * wdiffs[0] - icw * wdiffs[1], rcw * wdiffs[1] + icw * wdiffs[0])
        div = []
        for p in range(2):
            ch = 2 * k + p
            west = jnp.where(first, jnp.tile(fluxw[p], (1, 4)), pltpu.roll(flux[p], 1, 1))
            south = nf[ch, pl.ds(base, 8), :]
            below = nf[ch, pl.ds(base + 8, 8), :]
            sub = lax.broadcasted_iota(jnp.int32, (8, COLS), 0)
            north = pltpu.roll(jnp.where(sub == 0, below, south), 7, 0)
            div.append((flux[p] - west + (north - south)) * rcos)
            ecell.append(0.5 * (flux[p] + west))
            ncell.append(0.5 * (north + south))
        cr = elev_ref[2 * k, pl.ds(base, 8), :]
        ci = elev_ref[2 * k + 1, pl.ds(base, 8), :]
        new_ref[2 * k] = (cr - RELAX_RATE * (div[0] + om * ci)) * mask
        new_ref[2 * k + 1] = (ci - RELAX_RATE * (div[1] - om * cr)) * mask

    def stacked(parts):
        hi, lo = split(jnp.concatenate(parts, axis=0))
        return jnp.concatenate([hi, lo, hi], axis=0)

    xe, xn = stacked(ecell), stacked(ncell)
    total = jnp.zeros((8, COLS), F32)
    for q in range(4):
        w = w_ref[128 * q : 128 * q + 128, :]
        u = jnp.dot(w, xe, preferred_element_type=F32)
        v = jnp.dot(w, xn, preferred_element_type=F32)
        x = u * u + v * v + SPEED_EPS * SPEED_EPS
        speed = x * lax.rsqrt(x)
        for s in range(16):
            total = total + speed[8 * s : 8 * s + 8, :]
    fnew_ref[...] = BASE_FRICTION + DRAG_COEFF * total / SAMPLES


def sample_matrix():
    time = (STEP_TIME * np.arange(SAMPLES, dtype=np.float32))[:, None]
    phases = time * np.asarray(FREQUENCIES, np.float32)[None, :]
    table = np.stack([np.cos(phases), np.sin(phases)], axis=2).reshape(SAMPLES, CH).astype(np.float32)
    hi = table.astype(jnp.bfloat16)
    lo = (table - hi.astype(np.float32)).astype(jnp.bfloat16)
    eye = np.eye(8, dtype=np.float32)
    wide = [np.kron(x.astype(np.float32), eye) for x in (hi, hi, lo)]
    return jnp.asarray(np.concatenate(wide, axis=1), BF16)


def sweep(idx, elevation, sal, salh, salr, depth, friction, mask, rows, lonh, w):
    def whole(shape):
        return pl.BlockSpec(shape, lambda i, x: (0,) * len(shape))

    return pl.pallas_call(
        sweep_kernel,
        grid_spec=pltpu.PrefetchScalarGridSpec(
            num_scalar_prefetch=1,
            grid=(8,),
            in_specs=[
                whole((CH, ROWS, COLS)),
                whole((CH, ROWS, COLS)),
                pl.BlockSpec((CH, 8, 128), lambda i, x: (0, i, 0)),
                whole((2, CH, COLS)),
                whole((ROWS, COLS)),
                whole((ROWS, COLS)),
                whole((ROWS, COLS)),
                whole((2, 18, COLS)),
                pl.BlockSpec((18, 8, 128), lambda i, x: (0, i, 0)),
                whole((512, 384)),
            ],
            out_specs=[
                pl.BlockSpec((CH, 8, COLS), lambda i, x: (0, i, 0)),
                pl.BlockSpec((8, COLS), lambda i, x: (i, 0)),
            ],
            scratch_shapes=[
                pltpu.VMEM((CH, 80, COLS), F32),
                pltpu.VMEM((80, COLS), F32),
                pltpu.VMEM((80, COLS), F32),
                pltpu.VMEM((CH, 72, COLS), F32),
            ],
        ),
        out_shape=[
            jax.ShapeDtypeStruct((CH, ROWS, COLS), F32),
            jax.ShapeDtypeStruct((ROWS, COLS), F32),
        ],
        compiler_params=params(),
        name="sweep",
    )(idx, elevation, sal, salh, salr, depth, friction, mask, rows, lonh, w)


LAT = ("zh", "x", "c")
LON = ("y", "zl")


def shift(value, axes, size, step):
    return lax.ppermute(value, axes, [(i, (i + step) % size) for i in range(size)])


def swap(x, axis):
    return lax.all_to_all(x, axis, 0, 0, tiled=True)


def on_device(elevation, depth, friction, land_mask, order_map, legendre, load):
    lat = lax.axis_index(LAT)
    lon = lax.axis_index(LON)
    core = lax.axis_index("c")
    idx = jnp.stack([lat, lon, core, core]).astype(jnp.int32)

    sent = lax.dynamic_slice_in_dim(legendre, (1 - core) * 8, 8, axis=0)
    swapped = shift(sent, "c", 2, 1)

    sea_depth = depth * land_mask.astype(F32)
    last_row = jnp.concatenate([elevation[:, -1, :], sea_depth[-1:], friction[-1:]], axis=0)
    first_row = jnp.concatenate([elevation[:, 0, :], sea_depth[:1], friction[:1]], axis=0)
    rows = jnp.stack([shift(last_row, LAT, 32, 1), shift(first_row, LAT, 32, -1)])
    last_col = jnp.concatenate([elevation[:, :, -1], sea_depth[None, :, -1], friction[None, :, -1]], axis=0)
    first_col = jnp.concatenate([elevation[:, :, 0], sea_depth[None, :, 0], friction[None, :, 0]], axis=0)
    west = shift(last_col, LON, 8, 1)
    east = shift(first_col, LON, 8, -1)
    half = jnp.arange(128) < 64
    lonh = jnp.where(half, west[:, :, None], east[:, :, None])

    part, harm = dft(idx, order_map[:, None], elevation, land_mask, F32)
    received = swap(part, ("y", "zl", "c"))
    coeffs = analyse(idx, received, legendre, swapped, BF16)
    by_x = swap(coeffs.reshape(4, 64, DEG), "x")
    sum_x = jnp.sum(by_x.astype(F32), axis=0)
    by_z = swap(sum_x.reshape(4, 16, DEG), "zh")
    total = jnp.sum(by_z.astype(F32), axis=0)
    scaled = (total * load[None, :]).astype(BF16)
    all_z = swap(jnp.broadcast_to(scaled[None], (4, 16, DEG)), "zh")
    all_x = swap(jnp.broadcast_to(all_z.reshape(1, 64, DEG), (4, 64, DEG)), "x")
    spread = synthesise(idx, all_x.reshape(8, 32, DEG), legendre, swapped, BF16)
    g = swap(spread, ("y", "zl", "c"))
    sal, salh = inverse(g.reshape(256, 1024), harm)
    salr = jnp.stack([shift(sal[:, -1, :], LAT, 32, 1), shift(sal[:, 0, :], LAT, 32, -1)])
    new, fnew = sweep(idx, elevation, sal, salh, salr, depth, friction, land_mask, rows, lonh, sample_matrix())
    return new, sal, fnew


def solution(mesh):
    fine = Mesh(mesh.devices.reshape(4, 4, 2, 4, 2), ("zh", "x", "c", "y", "zl"))
    return jax.shard_map(
        on_device,
        mesh=fine,
        in_specs=(
            P(None, LAT, LON),
            P(LAT, LON),
            P(LAT, LON),
            P(LAT, LON),
            P(),
            P(LON, LAT, None),
            P(),
        ),
        out_specs=(P(None, LAT, LON), P(None, LAT, LON), P(LAT, LON)),
        check_vma=False,
    )
```

time: 522 us -> 162 us (0.31)
  the two profiles are of different devices: /device:TPU:71 before, /device:TPU:7 now
where the time goes in v1:
time: 162 us; the launch traced here: 161 us
  blocking collectives  54.9 us (34%)
  starting transfers between devices  39 us (24%)
  Pallas kernels  31.9 us (20%)
  waiting for transfers between devices  19.1 us (12%)
  local copies, waits for them, and re-layouts  12.4 us (8%)
  other arithmetic  2.61 us (2%)
    all_to_all x3, blocking collectives, swap(): return lax.all_to_all(x, axis, 0, 0, tiled=True)  54.9 us
    all_to_all x3, starting transfers between devices, swap(): return lax.all_to_all(x, axis, 0, 0, tiled=True)  24.5 us
    pallas_call x1, Pallas kernels, sweep(): pl.pallas_call(sweep_kernel, grid_spec=pltpu.PrefetchScalarGridSpec(num_s...  14.7 us
    ppermute x7, starting transfers between devices, shift(): lax.ppermute(value, axes, [(i, (i + step) % size) for i in range(size)])  14.6 us
    all_to_all x3, waiting for transfers between devices, swap(): return lax.all_to_all(x, axis, 0, 0, tiled=True)  12.7 us
    ppermute x7, waiting for transfers between devices, shift(): lax.ppermute(value, axes, [(i, (i + step) % size) for i in range(size)])  6.39 us
    pallas_call x1, Pallas kernels, synthesise(): pl.pallas_call(synth_kernel, grid_spec=pltpu.PrefetchScalarGridSpec(num_s...  5.42 us
    pallas_call x1, Pallas kernels, dft(): pl.pallas_call(dft_kernel, grid_spec=pltpu.PrefetchScalarGridSpec(num_sca...  4.56 us
  transfers between devices with their start and end apart: 10, of which 5 were waited for; matrix products, arithmetic and copies ran while one was open for 5% of the time, Pallas kernels for 8%

profile of v1, /device:TPU:7, one launch (start us, length us, event | category | flops | bytes accessed | tf_op | source)
XLA Modules:
  0.0 160.8 jit_solution(12430647645291330482)
XLA Ops:
  0.7 3.2 %constant_dynamic-slice_fusion = bf16[8,64,2048]{2,1,0:T(8,128)(2,1)} fusion(bf16[16,64,2048]{2,1,0:T(8,128)(2,1)} %own_ref.3, s32[]{:T(128)S(6)} %select_n.7), kind=kLoop, calls=%fused_computation.20 | loop fusion | bytes 4194308 | tf_op jit(solution)/shard_map/dynamic_slice | solution.py:452
  4.7 4.6 %dft.1 = (f32[16,16,1024]{2,1,0:T(8,128)S(1)}, bf16[512,640]{1,0:T(8,128)(2,1)S(1)}) custom-call(s32[4]{0:T(128)S(1)} %pad_add_fusion.idx, s32[128,1]{1,0:T(8,128)S(1)} %copy.23.om_ref, f32[16,64,512]{2,1,0:T(8,128)} %elev_ref.3, s32[64,512]{1,0:T(8,128)S(1)} %copy-done), custom_call_target="tpu_custom_call" | custom-call | tf_op jit(solution)/shard_map/dft/pallas_call | solution.py:87
  9.3 21.3 %all_to_all.30.r_ref = f32[16,16,1024]{2,1,0:T(8,128)} all-to-all(f32[16,16,1024]{2,1,0:T(8,128)S(1)} %get-tuple-element.9), channel_id=1, replica_groups=mesh['zh'=4,'x'=4,'c'=2,'y'=4,'zl'=2] {'y','zl','c'}, dimensions={0} | all-to-all | bytes 2097152 | tf_op jit(solution)/shard_map/all_to_all | solution.py:443
  30.6 1.3 copy-done.5
  31.9 4.4 %analyse.1 = bf16[8,32,2048]{2,1,0:T(8,128)(2,1)S(1)} custom-call(s32[4]{0:T(128)S(1)} %pad_add_fusion.idx, f32[16,16,1024]{2,1,0:T(8,128)} %all_to_all.30.r_ref, bf16[16,64,2048]{2,1,0:T(8,128)(2,1)} %own_ref.3, bf16[8,64,2048]{2,1,0:T(8,128)(2,1)} %copy-done.5), custom_call_target="tpu_custom_call" | custom-call | tf_op jit(solution)/shard_map/analyse/pallas_call | solution.py:140
  36.3 15.6 %all_to_all.31 = bf16[4,64,2048]{2,1,0:T(8,128)(2,1)S(1)} all-to-all(bf16[4,64,2048]{2,1,0:T(8,128)(2,1)S(1)} %bitcast.30), channel_id=1, replica_groups=mesh['zh'=4,'x'=4,'c'=2,'y'=4,'zl'=2] {'x'}, dimensions={0} | all-to-all | bytes 2097152 | tf_op jit(solution)/shard_map/all_to_all | solution.py:443
  52.1 18.0 %all_to_all.32 = f32[4,16,2048]{2,1,0:T(8,128)} all-to-all(f32[4,16,2048]{2,1,0:T(8,128)S(1)} %bitcast.32), channel_id=1, replica_groups=mesh['zh'=4,'x'=4,'c'=2,'y'=4,'zl'=2] {'zh'}, dimensions={0} | all-to-all | bytes 1048576 | tf_op jit(solution)/shard_map/all_to_all | solution.py:443
  71.9 5.4 %all-to-all-start.3 = ((bf16[4,16,2048]{2,1,0:T(8,128)(2,1)}), bf16[4,16,2048]{2,1,0:T(8,128)(2,1)S(1)}, u32[]{:S(2)}, u32[]{:S(2)}) async-start(bf16[4,16,2048]{2,1,0:T(8,128)(2,1)} %broadcast_in_dim.40), calls=%async_computation.3 | async-start | bytes 524288 | tf_op jit(solution)/shard_map/all_to_all | solution.py:443
  77.3 1.1 fusion
  78.5 6.8 %all-to-all-done.3 = bf16[4,16,2048]{2,1,0:T(8,128)(2,1)S(1)} async-done(((bf16[4,16,2048]{2,1,0:T(8,128)(2,1)}), bf16[4,16,2048]{2,1,0:T(8,128)(2,1)S(1)}, u32[]{:S(2)}, u32[]{:S(2)}) %all-to-all-start.3) | async-done | bytes 262176 | tf_op jit(solution)/shard_map/all_to_all | solution.py:443
  85.3 1.1 broadcast_in_dim.42
  86.3 5.3 %all-to-all-start.4 = ((bf16[4,64,2048]{2,1,0:T(8,128)(2,1)}), bf16[4,64,2048]{2,1,0:T(8,128)(2,1)S(1)}, u32[]{:S(2)}, u32[]{:S(2)}) async-start(bf16[4,64,2048]{2,1,0:T(8,128)(2,1)} %broadcast_in_dim.42), calls=%async_computation.4 | async-start | bytes 2097152 | tf_op jit(solution)/shard_map/all_to_all | solution.py:443
  92.3 4.4 %collective-permute-start.5 = (f32[18,64]{1,0:T(8,128)S(1)}, f32[18,64]{1,0:T(8,128)S(1)}, u32[]{:S(2)}, u32[]{:S(2)}) collective-permute-start(f32[18,64]{1,0:T(8,128)S(1)} %pad_maximum_fusion.4), channel_id=1, source_target_pairs={{0,1},{1,2},{2,3},{3,4},{4,5},{5,6},{6,7},{7,0},{8,9},{9,10},{10,1... | collective-permute-start | bytes 13832 | tf_op jit(solution)/shard_map/ppermute | solution.py:439
  98.3 1.2 all-to-all-done.4
  99.6 5.4 %synthesise.1 = bf16[16,16,1024]{2,1,0:T(8,128)(2,1)} custom-call(s32[4]{0:T(128)S(1)} %pad_add_fusion.idx, bf16[8,32,2048]{2,1,0:T(8,128)(2,1)S(1)} %bitcast.29, bf16[16,64,2048]{2,1,0:T(8,128)(2,1)} %own_ref.3, bf16[8,64,2048]{2,1,0:T(8,128)(2,1)} %copy-done.5), custom_call_target="tpu_custom_call" | custom-call | tf_op jit(solution)/shard_map/synthesise/pallas_call | solution.py:186
  105.0 13.8 %all-to-all-start.5 = ((bf16[16,16,1024]{2,1,0:T(8,128)(2,1)}), bf16[16,16,1024]{2,1,0:T(8,128)(2,1)S(1)}, u32[]{:S(2)}, u32[]{:S(2)}) async-start(bf16[16,16,1024]{2,1,0:T(8,128)(2,1)} %synthesise.1), calls=%async_computation.5 | async-start | bytes 1048576 | tf_op jit(solution)/shard_map/all_to_all | solution.py:443
  118.8 3.7 %collective-permute-start.3 = (f32[18,512]{1,0:T(8,128)S(1)}, f32[18,512]{1,0:T(8,128)S(1)}, u32[]{:S(2)}, u32[]{:S(2)}) collective-permute-start(f32[18,512]{1,0:T(8,128)S(1)} %pad_maximum_fusion.2), channel_id=1, source_target_pairs={{0,8},{8,16},{16,24},{24,32},{32,40},{40,48},{48,56},{56,64},{64,7... | collective-permute-start | bytes 110600 | tf_op jit(solution)/shard_map/ppermute | solution.py:439
  122.7 1.2 broadcast_select_fusion.lonh_ref
  123.9 4.7 %all-to-all-done.5 = bf16[16,16,1024]{2,1,0:T(8,128)(2,1)S(1)} async-done(((bf16[16,16,1024]{2,1,0:T(8,128)(2,1)}), bf16[16,16,1024]{2,1,0:T(8,128)(2,1)S(1)}, u32[]{:S(2)}, u32[]{:S(2)}) %all-to-all-start.5) | async-done | bytes 524320 | tf_op jit(solution)/shard_map/all_to_all | solution.py:443
  128.6 2.9 %inverse.1 = (f32[16,64,512]{2,1,0:T(8,128)}, f32[16,64,128]{2,1,0:T(8,128)S(1)}) custom-call(bf16[256,1024]{1,0:T(8,128)(2,1)S(1)} %bitcast.31, bf16[512,640]{1,0:T(8,128)(2,1)S(1)} %get-tuple-element.10.harm_ref), custom_call_target="tpu_custom_call" | custom-call | tf_op jit(solution)/shard_map/inverse/pallas_call | solution.py:216
  131.5 2.9 %copy.24 = f32[16,64,512]{2,0,1:T(8,128)S(1)} copy(f32[16,64,512]{2,1,0:T(8,128)} %get-tuple-element.7.sal_ref) | data formatting | bytes 4194304 | tf_op jit(solution)/shard_map/inverse/pallas_call | solution.py:216
  134.3 5.3 %collective-permute-start.1 = (f32[16,512]{1,0:T(8,128)S(1)}, f32[16,512]{1,0:T(8,128)S(1)}, u32[]{:S(2)}, u32[]{:S(2)}) collective-permute-start(f32[16,512]{1,0:T(8,128)S(1)} %get-tuple-element.23), channel_id=1, source_target_pairs={{0,8},{8,16},{16,24},{24,32},{32,40},{40,48},{48,56},{56,64},{64,7... | collective-permute-start | bytes 98312 | tf_op jit(solution)/shard_map/ppermute | solution.py:439
  140.8 5.3 %collective-permute-done.2 = f32[16,512]{1,0:T(8,128)S(1)} collective-permute-done((f32[16,512]{1,0:T(8,128)S(1)}, f32[16,512]{1,0:T(8,128)S(1)}, u32[]{:S(2)}, u32[]{:S(2)}) %collective-permute-start.2) | collective-permute-done | bytes 32800 | tf_op jit(solution)/shard_map/ppermute | solution.py:439
  146.1 14.7 %sweep.1 = (f32[16,64,512]{2,1,0:T(8,128)}, f32[64,512]{1,0:T(8,128)}) custom-call(s32[4]{0:T(128)S(1)} %pad_add_fusion.idx, f32[16,64,512]{2,1,0:T(8,128)} %elev_ref.3, f32[16,64,512]{2,1,0:T(8,128)} %get-tuple-element.7.sal_ref, f32[16,64,128]{2,1,0:T(8,128)S(1)} %get-tuple-element.12.salh_ref, f32[2,16,512]{2,1,0:T(8,128)S(1)} %pad_maximum_fusion.1.salr_ref, ...), custom_call_target="tpu_custom_call" | custom-call | tf_op jit(solution)/shard_map/sweep/pallas_call | solution.py:397
  (53 shorter events, 6.4 us)
Async XLA Ops:
  0.6 3.9 %copy-start.9 = (s32[128]{0:T(128)S(1)}, s32[128]{0:T(128)}, u32[]{:S(2)}) copy-start(s32[128]{0:T(128)} %param.12) | copy-start | bytes 1540
  0.6 4.1 %copy-start = (s32[64,512]{1,0:T(8,128)S(1)}, s32[64,512]{1,0:T(8,128)}, u32[]{:S(2)}) copy-start(s32[64,512]{1,0:T(8,128)} %mask_ref.3) | copy-start | bytes 393220
  3.9 26.7 %collective-permute-start = (bf16[8,64,2048]{2,1,0:T(8,128)(2,1)}, bf16[8,64,2048]{2,1,0:T(8,128)(2,1)S(1)}, u32[]{:S(2)}, u32[]{:S(2)}) collective-permute-start(bf16[8,64,2048]{2,1,0:T(8,128)(2,1)} %constant_dynamic-slice_fusion), channel_id=1, source_target_pairs={{0,8},{8,0},{1,9},{9,1},{2,10},{10,2},{3,11},{11,3},{4,12},{12,4},... | collective-permute-start | bytes 6291464 | tf_op jit(solution)/shard_map/ppermute | solution.py:439
  30.6 1.3 copy-start.5
  51.9 19.2 %copy-start.8 = (f32[2048]{0:T(1024)S(1)}, f32[2048]{0:T(1024)}, u32[]{:S(2)}) copy-start(f32[2048]{0:T(1024)} %param.14) | copy-start | bytes 24580
  51.9 25.4 %copy-start.4 = (f32[16,64,512]{2,1,0:T(8,128)S(1)}, f32[16,64,512]{2,1,0:T(8,128)}, u32[]{:S(2)}) copy-start(f32[16,64,512]{2,1,0:T(8,128)} %elev_ref.3) | copy-start | bytes 6291460
  71.9 13.3 %all-to-all-start.3 = ((bf16[4,16,2048]{2,1,0:T(8,128)(2,1)}), bf16[4,16,2048]{2,1,0:T(8,128)(2,1)S(1)}, u32[]{:S(2)}, u32[]{:S(2)}) async-start(bf16[4,16,2048]{2,1,0:T(8,128)(2,1)} %broadcast_in_dim.40), calls=%async_computation.3 | async-start | bytes 524288 | tf_op jit(solution)/shard_map/all_to_all | solution.py:443
  78.5 13.2 %copy-start.1 = (f32[64,512]{1,0:T(8,128)S(1)}, f32[64,512]{1,0:T(8,128)}, u32[]{:S(2)}) copy-start(f32[64,512]{1,0:T(8,128)} %depth_ref.1) | copy-start | bytes 393220
  78.5 13.2 %copy-start.7 = (f32[16,64,1]{2,1,0:T(8,128)S(1)}, f32[16,64,1]{2,1,0:T(8,128)}, u32[]{:S(2)}) copy-start(f32[16,64,1]{2,1,0:T(8,128)} %get-tuple-element.19) | copy-start | bytes 12292
  85.2 6.8 %copy-start.3 = (f32[64,512]{1,0:T(8,128)S(1)}, f32[64,512]{1,0:T(8,128)}, u32[]{:S(2)}) copy-start(f32[64,512]{1,0:T(8,128)} %fric_ref.1) | copy-start | bytes 393220
  85.2 11.4 %copy-start.6 = (f32[16,64,1]{2,1,0:T(8,128)S(1)}, f32[16,64,1]{2,1,0:T(8,128)}, u32[]{:S(2)}) copy-start(f32[16,64,1]{2,1,0:T(8,128)} %get-tuple-element.20) | copy-start | bytes 12292
  86.3 13.2 %all-to-all-start.4 = ((bf16[4,64,2048]{2,1,0:T(8,128)(2,1)}), bf16[4,64,2048]{2,1,0:T(8,128)(2,1)S(1)}, u32[]{:S(2)}, u32[]{:S(2)}) async-start(bf16[4,64,2048]{2,1,0:T(8,128)(2,1)} %broadcast_in_dim.42), calls=%async_computation.4 | async-start | bytes 2097152 | tf_op jit(solution)/shard_map/all_to_all | solution.py:443
  92.3 30.4 %collective-permute-start.5 = (f32[18,64]{1,0:T(8,128)S(1)}, f32[18,64]{1,0:T(8,128)S(1)}, u32[]{:S(2)}, u32[]{:S(2)}) collective-permute-start(f32[18,64]{1,0:T(8,128)S(1)} %pad_maximum_fusion.4), channel_id=1, source_target_pairs={{0,1},{1,2},{2,3},{3,4},{4,5},{5,6},{6,7},{7,0},{8,9},{9,10},{10,1... | collective-permute-start | bytes 13832 | tf_op jit(solution)/shard_map/ppermute | solution.py:439
  96.9 25.8 %collective-permute-start.6 = (f32[18,64]{1,0:T(8,128)S(1)}, f32[18,64]{1,0:T(8,128)S(1)}, u32[]{:S(2)}, u32[]{:S(2)}) collective-permute-start(f32[18,64]{1,0:T(8,128)S(1)} %pad_maximum_fusion.5), channel_id=1, source_target_pairs={{0,7},{1,0},{2,1},{3,2},{4,3},{5,4},{6,5},{7,6},{8,15},{9,8},{10,9... | collective-permute-start | bytes 13832 | tf_op jit(solution)/shard_map/ppermute | solution.py:439
  105.0 23.6 %all-to-all-start.5 = ((bf16[16,16,1024]{2,1,0:T(8,128)(2,1)}), bf16[16,16,1024]{2,1,0:T(8,128)(2,1)S(1)}, u32[]{:S(2)}, u32[]{:S(2)}) async-start(bf16[16,16,1024]{2,1,0:T(8,128)(2,1)} %synthesise.1), calls=%async_computation.5 | async-start | bytes 1048576 | tf_op jit(solution)/shard_map/all_to_all | solution.py:443
  118.8 20.8 %collective-permute-start.3 = (f32[18,512]{1,0:T(8,128)S(1)}, f32[18,512]{1,0:T(8,128)S(1)}, u32[]{:S(2)}, u32[]{:S(2)}) collective-permute-start(f32[18,512]{1,0:T(8,128)S(1)} %pad_maximum_fusion.2), channel_id=1, source_target_pairs={{0,8},{8,16},{16,24},{24,32},{32,40},{40,48},{48,56},{56,64},{64,7... | collective-permute-start | bytes 110600 | tf_op jit(solution)/shard_map/ppermute | solution.py:439
  122.6 17.1 %collective-permute-start.4 = (f32[18,512]{1,0:T(8,128)S(1)}, f32[18,512]{1,0:T(8,128)S(1)}, u32[]{:S(2)}, u32[]{:S(2)}) collective-permute-start(f32[18,512]{1,0:T(8,128)S(1)} %pad_maximum_fusion.3), channel_id=1, source_target_pairs={{0,248},{8,0},{16,8},{24,16},{32,24},{40,32},{48,40},{56,48},{64,5... | collective-permute-start | bytes 110600 | tf_op jit(solution)/shard_map/ppermute | solution.py:439
  131.5 14.6 %copy-start.2 = (bf16[512,384]{1,0:T(8,128)(2,1)S(1)}, bf16[512,384]{1,0:T(8,128)(2,1)}, u32[]{:S(2)}) copy-start(bf16[512,384]{1,0:T(8,128)(2,1)} %constant.35.clone.w_ref) | copy-start | bytes 1179652
  134.3 6.4 %collective-permute-start.1 = (f32[16,512]{1,0:T(8,128)S(1)}, f32[16,512]{1,0:T(8,128)S(1)}, u32[]{:S(2)}, u32[]{:S(2)}) collective-permute-start(f32[16,512]{1,0:T(8,128)S(1)} %get-tuple-element.23), channel_id=1, source_target_pairs={{0,8},{8,16},{16,24},{24,32},{32,40},{40,48},{48,56},{56,64},{64,7... | collective-permute-start | bytes 98312 | tf_op jit(solution)/shard_map/ppermute | solution.py:439
  139.7 6.4 %collective-permute-start.2 = (f32[16,512]{1,0:T(8,128)S(1)}, f32[16,512]{1,0:T(8,128)S(1)}, u32[]{:S(2)}, u32[]{:S(2)}) collective-permute-start(f32[16,512]{1,0:T(8,128)S(1)} %get-tuple-element.24), channel_id=1, source_target_pairs={{0,248},{8,0},{16,8},{24,16},{32,24},{40,32},{48,40},{56,48},{64,5... | collective-permute-start | bytes 98312 | tf_op jit(solution)/shard_map/ppermute | solution.py:439

commit v2 on v1

v2 whole, which is shorter than its diff:
```python
import functools
import math

import jax
import jax.numpy as jnp
import numpy as np
from jax import lax
from jax.experimental import pallas as pl
from jax.experimental.pallas import tpu as pltpu
from jax.sharding import Mesh, PartitionSpec as P

SAMPLES = 64
FREQUENCIES = (1.0, 1.0347, 0.9582, 1.0379, 0.5018, 0.4651, 0.4986, 0.4482)
EQ_AMPS = (0.73, 0.34, 0.14, 0.09, 0.42, 0.3, 0.14, 0.06)
LAT_EDGE = 1.3614
RELAX_RATE = 0.1
BASE_FRICTION = 0.05
DRAG_COEFF = 0.5
SPEED_EPS = 0.001
STEP_TIME = 3.0
NLAT = 2048
NLON = 4096
LAT_STEP = 2.0 * LAT_EDGE / NLAT
ROWS = 64
COLS = 512
CH = 16
DEG = 2048
F32 = jnp.float32
BF16 = jnp.bfloat16
PART_SCALE = 512.0


def params(mib=52):
    return pltpu.CompilerParams(vmem_limit_bytes=mib * 1024 * 1024)


def unit_circle(k):
    k = k & (NLON - 1)
    quad = (k + 512) >> 10
    t = (k - (quad << 10)).astype(F32) * (2.0 * math.pi / NLON)
    q = quad & 3
    t2 = t * t
    s = t * (1.0 + t2 * (-1.0 / 6 + t2 * (1.0 / 120 + t2 * (-1.0 / 5040 + t2 * (1.0 / 362880)))))
    c = 1.0 + t2 * (-0.5 + t2 * (1.0 / 24 + t2 * (-1.0 / 720 + t2 * (1.0 / 40320))))
    swap = (q & 1) == 1
    cos = jnp.where(swap, s, c)
    sin = jnp.where(swap, c, s)
    cos = jnp.where((q == 1) | (q == 2), -cos, cos)
    sin = jnp.where(q >= 2, -sin, sin)
    return cos, sin


def split(x):
    hi = x.astype(BF16)
    lo = (x - hi.astype(F32)).astype(BF16)
    return hi, lo


NT = (((1,), (1,)), ((), ()))
TN = (((0,), (0,)), ((), ()))


def dft_kernel(
    idx, om_ref, elev_ref, mask_ref, depth_ref, fric_ref, leg_ref,
    part_ref, harm_ref, half_ref, first_ref, last_ref, cols_ref,
):
    i = pl.program_id(0)
    half_ref[...] = leg_ref[...]
    mask = mask_ref[...].astype(F32)
    sub = lax.broadcasted_iota(jnp.int32, (8, 128), 0)
    lane = lax.broadcasted_iota(jnp.int32, (8, 128), 1)
    pick_first = jnp.where((sub == 0) & (lane == 0), 1.0, 0.0).astype(F32)
    pick_last = jnp.where((sub == 1) & (lane == 127), 1.0, 0.0).astype(F32)

    def ends(x):
        def pick(sel, tile):
            return lax.dot_general(sel, tile, NT, precision=lax.Precision.HIGHEST, preferred_element_type=F32)

        return pick(pick_first, x[:, :128]) + pick(pick_last, x[:, COLS - 128 :])

    @pl.when(i == 0)
    def _():
        diag = lax.broadcasted_iota(jnp.int32, (128, 128), 0) == lax.broadcasted_iota(jnp.int32, (128, 128), 1)
        orders = jnp.broadcast_to(om_ref[...].astype(F32), (128, 128))
        orders = jnp.sum(jnp.where(diag, orders, 0.0), axis=1, keepdims=True).astype(jnp.int32)
        lane = lax.broadcasted_iota(jnp.int32, (8, COLS + 128), 1)
        off = jnp.where(lane < COLS, lane, jnp.where(lane < COLS + 64, -1, COLS))
        col = idx[1] * COLS + off
        for g in range(16):
            m = orders[8 * g : 8 * g + 8, :]
            cos, sin = unit_circle(m * col)
            scale = jnp.where(m > 0, math.sqrt(2.0 / NLON), math.sqrt(1.0 / NLON)).astype(F32)
            hi, lo = split(jnp.concatenate([cos * scale, sin * scale], axis=0))
            harm_ref[16 * g : 16 * g + 16, :] = hi
            harm_ref[256 + 16 * g : 256 + 16 * g + 16, :] = lo
        sea = depth_ref[...] * mask
        for r, x in ((16, sea), (17, fric_ref[...])):
            first_ref[r : r + 1, :] = x[:1]
            last_ref[r : r + 1, :] = x[ROWS - 1 :]
        first_ref[18:, :] = jnp.zeros((6, COLS), F32)
        last_ref[18:, :] = jnp.zeros((6, COLS), F32)
        cols_ref[:, 1024:] = ends(jnp.concatenate([sea, fric_ref[...]], axis=0))

    field = jnp.concatenate([elev_ref[c] * mask for c in range(4)], axis=0)
    hi, lo = split(field)
    both = lax.dot_general(harm_ref[:, :COLS], hi, NT, preferred_element_type=F32)
    small = lax.dot_general(harm_ref[:256, :COLS], lo, NT, preferred_element_type=F32)
    out = both[:256] + (both[256:] + small)
    part_ref[...] = (out * PART_SCALE).reshape(16, 16, 256).astype(part_ref.dtype)
    for c in range(4):
        first_ref[pl.ds(4 * i + c, 1), :] = field[64 * c : 64 * c + 1]
        last_ref[pl.ds(4 * i + c, 1), :] = field[64 * c + 63 : 64 * c + 64]
    cols_ref[:, pl.ds(pl.multiple_of(256 * i, 256), 256)] = ends(field)


def dft(idx, om, elevation, mask, depth, friction, legendre):
    def whole(shape):
        return pl.BlockSpec(shape, lambda i, x: (0,) * len(shape))

    return pl.pallas_call(
        dft_kernel,
        grid_spec=pltpu.PrefetchScalarGridSpec(
            num_scalar_prefetch=1,
            grid=(4,),
            in_specs=[
                whole((1, 128)),
                pl.BlockSpec((4, ROWS, COLS), lambda i, x: (i, 0, 0)),
                whole((ROWS, COLS)),
                whole((ROWS, COLS)),
                whole((ROWS, COLS)),
                pl.BlockSpec((2, ROWS, DEG), lambda i, x: (4 - 4 * x[2] + i, 0, 0)),
            ],
            out_specs=[
                pl.BlockSpec((16, 16, 256), lambda i, x: (0, 0, i)),
                whole((512, COLS + 128)),
                pl.BlockSpec((2, ROWS, DEG), lambda i, x: (i, 0, 0)),
                whole((24, COLS)),
                whole((24, COLS)),
                whole((8, 1152)),
            ],
        ),
        out_shape=[
            jax.ShapeDtypeStruct((16, 16, 1024), F32),
            jax.ShapeDtypeStruct((512, COLS + 128), BF16),
            jax.ShapeDtypeStruct((8, ROWS, DEG), BF16),
            jax.ShapeDtypeStruct((24, COLS), F32),
            jax.ShapeDtypeStruct((24, COLS), F32),
            jax.ShapeDtypeStruct((8, 1152), F32),
        ],
        compiler_params=params(60),
        name="dft",
    )(idx, om, elevation, mask, depth, friction, legendre)


def analyse_kernel(idx, r_ref, own_ref, rcv_ref, *rest):
    out_ref, mid_ref, outer_ref, a_ref, e_ref = rest[-5:]

    @pl.when(pl.program_id(0) == 0)
    def _():
        me = idx[2]
        low = lax.broadcasted_iota(jnp.int32, (16, 128), 1) < 64
        for t in range(8):
            tiles = [r_ref[which, :, 128 * t : 128 * t + 128] for which in (me, 1 - me)]
            f0, f1 = tiles
            even = jnp.where(low, f0, pltpu.roll(f1, 64, 1))
            odd = jnp.where(low, pltpu.roll(f0, 64, 1), f1)
            for ch, val in ((2 * t, even), (2 * t + 1, odd)):
                for p in range(2):
                    a_ref[pl.ds(16 * p + ch, 8, stride=32), :] = val[8 * p : 8 * p + 8, :]

    i = pl.program_id(0)
    for s in range(2):
        a = a_ref[pl.ds(pl.multiple_of(64 * i, 64) + 32 * s, 32), :].astype(BF16)
        table = jnp.concatenate([own_ref[s], rcv_ref[s]], axis=0)
        out_ref[s] = jnp.dot(a, table, preferred_element_type=F32).astype(out_ref.dtype)
        low = idx[2] == 0
        own_first, own_last = own_ref[s, :16].astype(F32)[:1], own_ref[s, ROWS - 16 :].astype(F32)[15:]
        rcv_first, rcv_last = rcv_ref[s, :16].astype(F32)[:1], rcv_ref[s, ROWS - 16 :].astype(F32)[15:]
        e_ref[pl.ds(2 * i + s, 1), :] = jnp.where(low, rcv_first, own_first)
        e_ref[pl.ds(8 + 2 * i + s, 1), :] = jnp.where(low, own_last, rcv_last)
        e_ref[pl.ds(16 + 2 * i + s, 1), :] = jnp.where(low, own_first, rcv_first)
        e_ref[pl.ds(24 + 2 * i + s, 1), :] = jnp.where(low, rcv_last, own_last)

    @pl.when(i == 3)
    def _():
        mid_ref[...] = e_ref[:16, :].astype(BF16)
        outer_ref[...] = e_ref[16:, :].astype(BF16)


def analyse(idx, received, legendre, other, after, dtype):
    table = pl.BlockSpec((2, ROWS, DEG), lambda i, x: (4 * x[2] + i, 0, 0))
    return pl.pallas_call(
        analyse_kernel,
        grid_spec=pltpu.PrefetchScalarGridSpec(
            num_scalar_prefetch=1,
            grid=(4,),
            in_specs=[
                pl.BlockSpec((2, 16, 1024), lambda i, x: (0, 0, 0)),
                table,
                pl.BlockSpec((2, ROWS, DEG), lambda i, x: (i, 0, 0)),
            ]
            + [pl.BlockSpec(memory_space=pl.ANY)] * len(after),
            out_specs=[
                pl.BlockSpec((2, 32, DEG), lambda i, x: (i, 0, 0)),
                pl.BlockSpec((16, DEG), lambda i, x: (0, 0)),
                pl.BlockSpec((16, DEG), lambda i, x: (0, 0)),
            ],
            scratch_shapes=[pltpu.VMEM((256, 128), F32), pltpu.VMEM((32, DEG), F32)],
        ),
        out_shape=[
            jax.ShapeDtypeStruct((8, 32, DEG), dtype),
            jax.ShapeDtypeStruct((16, DEG), BF16),
            jax.ShapeDtypeStruct((16, DEG), BF16),
        ],
        compiler_params=params(),
        name="analyse",
    )(idx, received, legendre, other, *after)


def synth_kernel(idx, sc_ref, own_ref, rcv_ref, mid_ref, prev_ref, next_ref, *rest):
    out_ref, t_ref, u_ref = rest[-3:]
    edges = jnp.concatenate([mid_ref[...], prev_ref[...], next_ref[...]], axis=0)
    i = pl.program_id(0)
    for s in range(2):
        table = jnp.concatenate([own_ref[s], rcv_ref[s]], axis=0)
        row = pl.multiple_of(64 * i, 64) + 32 * s
        t_ref[pl.ds(row, 32), :] = lax.dot_general(sc_ref[s], table, NT, preferred_element_type=F32)
        u_ref[2 * i + s, :, :32] = lax.dot_general(edges, sc_ref[s], NT, preferred_element_type=F32)

    @pl.when(i == 3)
    def _():
        me = idx[2]
        lane = lax.broadcasted_iota(jnp.int32, (8, 128), 1)
        sub = lax.broadcasted_iota(jnp.int32, (8, 128), 0)
        low = lane < 64
        for t in range(8):
            own, oth = [], []
            for p in range(2):
                v0 = t_ref[pl.ds(16 * p + 2 * t, 8, stride=32), :]
                v1 = t_ref[pl.ds(16 * p + 2 * t + 1, 8, stride=32), :]
                own.append(jnp.where(low, v0, pltpu.roll(v1, 64, 1)))
                oth.append(jnp.where(low, pltpu.roll(v0, 64, 1), v1))
            own = jnp.concatenate(own, axis=0).astype(out_ref.dtype)
            oth = jnp.concatenate(oth, axis=0).astype(out_ref.dtype)
            for d in range(8):
                out_ref[2 * d + me, :, 128 * t : 128 * t + 128] = own
                out_ref[2 * d + 1 - me, :, 128 * t : 128 * t + 128] = oth
        for half in range(2):
            sides = []
            for side in range(2):
                g = 8 * ((3, 0), (1, 4))[half][side]
                v = jnp.zeros((8, 128), F32)
                for s in range(8):
                    v = jnp.where(sub == s, u_ref[s, g : g + 8, :], v)
                sides.append(v)
            top, bottom = sides
            rows = [
                jnp.where(lane < 16, top, pltpu.roll(bottom, 16, 1)),
                jnp.where(lane < 16, pltpu.roll(top, 112, 1), bottom),
            ]
            rows = [jnp.where(lane < 32, x, 0.0) for x in rows]
            edge = jnp.concatenate(rows, axis=0).astype(out_ref.dtype)
            for d in range(8):
                out_ref[2 * d + half, :, 1024:] = edge


def synthesise(idx, scaled, legendre, other, edges, after, dtype):
    table = pl.BlockSpec((2, ROWS, DEG), lambda i, x: (4 * x[2] + i, 0, 0))
    return pl.pallas_call(
        synth_kernel,
        grid_spec=pltpu.PrefetchScalarGridSpec(
            num_scalar_prefetch=1,
            grid=(4,),
            in_specs=[
                pl.BlockSpec((2, 32, DEG), lambda i, x: (i, 0, 0)),
                table,
                pl.BlockSpec((2, ROWS, DEG), lambda i, x: (i, 0, 0)),
            ]
            + [pl.BlockSpec((16, DEG), lambda i, x: (0, 0))] * 3
            + [pl.BlockSpec(memory_space=pl.ANY)] * len(after),
            out_specs=pl.BlockSpec((16, 16, 1152), lambda i, x: (0, 0, 0)),
            scratch_shapes=[pltpu.VMEM((256, 128), F32), pltpu.VMEM((8, 48, 128), F32)],
        ),
        out_shape=jax.ShapeDtypeStruct((16, 16, 1152), dtype),
        compiler_params=params(),
        name="synthesise",
    )(idx, scaled, legendre, other, *edges, *after)


def lat_of(row):
    return -LAT_EDGE + row * LAT_STEP


def sweep_kernel(
    idx, g_ref, harm_ref, elev_ref, depth_ref, fric_ref, mask_ref, before_ref, after_ref, west_ref, east_ref, w_ref,
    new_ref, sal_ref, fnew_ref, spad, dpad, fpad, nf, salbuf, lonh_all, sem,
):
    b = pl.program_id(0)
    lat0 = idx[0] * ROWS

    def send(c):
        part = pl.ds(4 * c, 4)
        return pltpu.make_async_copy(salbuf.at[part], sal_ref.at[part], sem.at[c])

    @pl.when(b == 0)
    def _():
        lane = lax.broadcasted_iota(jnp.int32, (8, COLS), 1)
        col = idx[1] * COLS + lane
        c1, s1 = unit_circle(col)
        c2, s2 = unit_circle(2 * col)
        waves = (c2[:1], s2[:1], c1[:1], s1[:1])

        def shapes(first, count):
            row = first.astype(F32) + lax.broadcasted_iota(jnp.int32, (count, 128), 0).astype(F32)
            phi = lat_of(row + 0.5)
            cosphi = jnp.cos(phi)
            return jnp.tile(cosphi * cosphi, (1, 4)), jnp.tile(jnp.sin(2.0 * phi), (1, 4))

        sq, s2phi = shapes(lat0, ROWS)
        up_sq, up_s2 = shapes(lat0 - 1, 8)
        dn_sq, dn_s2 = shapes(lat0 + ROWS, 8)

        def invert(cols):
            part = g_ref[:, cols]
            hi = lax.dot_general(part, harm_ref[:256, :], TN, preferred_element_type=F32)
            lo = lax.dot_general(part, harm_ref[256:, :], TN, preferred_element_type=F32)
            return hi + lo

        sub = lax.broadcasted_iota(jnp.int32, (8, 128), 0)
        lane = lax.broadcasted_iota(jnp.int32, (8, 128), 1)
        to_low = jnp.where((sub == 1) & (lane < 64), 1.0, 0.0).astype(F32)
        to_high = jnp.where((sub == 0) & (lane >= 64), 1.0, 0.0).astype(F32)

        def place(x, sel):
            return lax.dot_general(x, sel, TN, precision=lax.Precision.HIGHEST, preferred_element_type=F32)

        beside = place(west_ref[...], to_low) + place(east_ref[...], to_high)
        for ch in range(18):
            lonh_all[ch] = beside[64 * ch : 64 * ch + 64]
        edge = invert(slice(1024, 1152))
        for ch in range(CH):
            if ch % 4 == 0:
                quarter = invert(slice(64 * ch, 64 * ch + 256))
                for c in range(4):
                    salbuf[ch + c] = quarter[64 * c : 64 * c + 64, :COLS]
                    lonh_all[ch + c] = lonh_all[ch + c] - quarter[64 * c : 64 * c + 64, COLS:]
                send(ch // 4).start()
            k = ch // 2
            wave = waves[(0 if k < 4 else 2) + ch % 2]
            eq = EQ_AMPS[k] * (sq if k < 4 else s2phi) * wave
            spad[ch, 8 : 8 + ROWS, :] = elev_ref[ch] - eq - salbuf[ch]
            up = EQ_AMPS[k] * (up_sq if k < 4 else up_s2)[:1] * wave
            dn = EQ_AMPS[k] * (dn_sq if k < 4 else dn_s2)[:1] * wave
            spad[ch, 7:8, :] = before_ref[ch : ch + 1, :] - up - edge[ch : ch + 1, :COLS]
            spad[ch, 8 + ROWS : 9 + ROWS, :] = after_ref[ch : ch + 1, :] - dn - edge[16 + ch : 17 + ch, :COLS]
        dpad[8 : 8 + ROWS, :] = depth_ref[...] * mask_ref[...].astype(F32)
        fpad[8 : 8 + ROWS, :] = fric_ref[...]
        top = jnp.where(idx[0] == 0, 0.0, 1.0)
        bottom = jnp.where(idx[0] == 31, 0.0, 1.0)
        dpad[7:8, :] = before_ref[16:17, :] * top
        dpad[8 + ROWS : 9 + ROWS, :] = after_ref[16:17, :] * bottom
        fpad[7:8, :] = before_ref[17:18, :]
        fpad[8 + ROWS : 9 + ROWS, :] = after_ref[17:18, :]

        for blk in range(9):
            lo = 8 * blk
            row = (lat0 + lo).astype(F32) + lax.broadcasted_iota(jnp.int32, (8, 128), 0).astype(F32)
            cosf = jnp.tile(jnp.cos(lat_of(row)), (1, 4))
            hh = dpad[8 + lo : 16 + lo, :] * dpad[7 + lo : 15 + lo, :]
            h = jnp.sqrt(hh)
            r = 0.5 * (fpad[8 + lo : 16 + lo, :] + fpad[7 + lo : 15 + lo, :])
            for k in range(8):
                om = FREQUENCIES[k]
                inv = -hh / (r * r + (om * om) * hh)
                rc = inv * r * cosf
                ic = inv * h * om * cosf
                dr = spad[2 * k, 8 + lo : 16 + lo, :] - spad[2 * k, 7 + lo : 15 + lo, :]
                di = spad[2 * k + 1, 8 + lo : 16 + lo, :] - spad[2 * k + 1, 7 + lo : 15 + lo, :]
                nf[2 * k, lo : lo + 8, :] = rc * dr - ic * di
                nf[2 * k + 1, lo : lo + 8, :] = rc * di + ic * dr

    base = pl.multiple_of(8 * b, 8)
    own = pl.ds(base + 8, 8)
    row = (lat0 + base).astype(F32) + lax.broadcasted_iota(jnp.int32, (8, 128), 0).astype(F32)
    phi = lat_of(row + 0.5)
    rcos1 = 1.0 / jnp.cos(phi)
    rcos = jnp.tile(rcos1, (1, 4))
    lane = lax.broadcasted_iota(jnp.int32, (8, COLS), 1)
    last = lane == COLS - 1
    first = lane == 0
    tile_lane = lax.broadcasted_iota(jnp.int32, (8, 128), 1)
    col = idx[1] * COLS + jnp.where(tile_lane < 64, -1, COLS)
    c1, s1 = unit_circle(col)
    c2, s2 = unit_circle(2 * col)
    waves = (c2, s2, c1, s1)
    cosphi = jnp.cos(phi)
    sq, s2phi = cosphi * cosphi, jnp.sin(2.0 * phi)

    def east_of(x, halo):
        wide = jnp.tile(halo, (1, 4))
        return jnp.where(last, wide, pltpu.roll(x, COLS - 1, 1))

    d = dpad[own, :]
    f = fpad[own, :]
    dh = lonh_all[16, pl.ds(base, 8), :]
    fh = lonh_all[17, pl.ds(base, 8), :]
    hh = d * east_of(d, dh)
    h = jnp.sqrt(hh)
    r = 0.5 * (f + east_of(f, fh))
    hhw = d[:, :128] * dh
    hw = jnp.sqrt(hhw)
    rw = 0.5 * (f[:, :128] + fh)
    mask = mask_ref[pl.ds(base, 8), :].astype(F32)
    ecell, ncell = [], []
    for k in range(8):
        om = FREQUENCIES[k]
        inv = -hh / (r * r + (om * om) * hh)
        rc = inv * r * rcos
        ic = inv * h * om * rcos
        invw = -hhw / (rw * rw + (om * om) * hhw)
        rcw = invw * rw * rcos1
        icw = invw * hw * om * rcos1
        diffs, wdiffs = [], []
        for ch in (2 * k, 2 * k + 1):
            s = spad[ch, own, :]
            eq = EQ_AMPS[k] * (sq if k < 4 else s2phi) * waves[(0 if k < 4 else 2) + ch % 2]
            sh = lonh_all[ch, pl.ds(base, 8), :] - eq
            diffs.append(east_of(s, sh) - s)
            wdiffs.append(s[:, :128] - sh)
        flux = (rc * diffs[0] - ic * diffs[1], rc * diffs[1] + ic * diffs[0])
        fluxw = (rcw * wdiffs[0] - icw * wdiffs[1], rcw * wdiffs[1] + icw * wdiffs[0])
        div = []
        for p in range(2):
            ch = 2 * k + p
            west = jnp.where(first, jnp.tile(fluxw[p], (1, 4)), pltpu.roll(flux[p], 1, 1))
            south = nf[ch, pl.ds(base, 8), :]
            below = nf[ch, pl.ds(base + 8, 8), :]
            sub = lax.broadcasted_iota(jnp.int32, (8, COLS), 0)
            north = pltpu.roll(jnp.where(sub == 0, below, south), 7, 0)
            div.append((flux[p] - west + (north - south)) * rcos)
            ecell.append(0.5 * (flux[p] + west))
            ncell.append(0.5 * (north + south))
        cr = elev_ref[2 * k, pl.ds(base, 8), :]
        ci = elev_ref[2 * k + 1, pl.ds(base, 8), :]
        new_ref[2 * k] = (cr - RELAX_RATE * (div[0] + om * ci)) * mask
        new_ref[2 * k + 1] = (ci - RELAX_RATE * (div[1] - om * cr)) * mask

    def stacked(parts):
        hi, lo = split(jnp.concatenate(parts, axis=0))
        return jnp.concatenate([hi, lo, hi], axis=0)

    xe, xn = stacked(ecell), stacked(ncell)
    total = jnp.zeros((8, COLS), F32)
    for q in range(4):
        w = w_ref[128 * q : 128 * q + 128, :]
        u = jnp.dot(w, xe, preferred_element_type=F32)
        v = jnp.dot(w, xn, preferred_element_type=F32)
        x = u * u + v * v + SPEED_EPS * SPEED_EPS
        speed = x * lax.rsqrt(x)
        for s in range(16):
            total = total + speed[8 * s : 8 * s + 8, :]
    fnew_ref[...] = BASE_FRICTION + DRAG_COEFF * total / SAMPLES

    @pl.when(b == 7)
    def _():
        for c in range(4):
            send(c).wait()


def sample_matrix():
    time = (STEP_TIME * np.arange(SAMPLES, dtype=np.float32))[:, None]
    phases = time * np.asarray(FREQUENCIES, np.float32)[None, :]
    table = np.stack([np.cos(phases), np.sin(phases)], axis=2).reshape(SAMPLES, CH).astype(np.float32)
    hi = table.astype(jnp.bfloat16)
    lo = (table - hi.astype(np.float32)).astype(jnp.bfloat16)
    eye = np.eye(8, dtype=np.float32)
    wide = [np.kron(x.astype(np.float32), eye) for x in (hi, hi, lo)]
    return jnp.asarray(np.concatenate(wide, axis=1), BF16)


def sweep(idx, g, harm, elevation, depth, friction, mask, before, after, west, east, w):
    def whole(shape):
        return pl.BlockSpec(shape, lambda i, x: (0,) * len(shape))

    return pl.pallas_call(
        sweep_kernel,
        grid_spec=pltpu.PrefetchScalarGridSpec(
            num_scalar_prefetch=1,
            grid=(8,),
            in_specs=[
                whole((256, 1152)),
                whole((512, COLS + 128)),
                whole((CH, ROWS, COLS)),
                whole((ROWS, COLS)),
                whole((ROWS, COLS)),
                whole((ROWS, COLS)),
                whole((24, COLS)),
                whole((24, COLS)),
                whole((8, 1152)),
                whole((8, 1152)),
                whole((512, 384)),
            ],
            out_specs=[
                pl.BlockSpec((CH, 8, COLS), lambda i, x: (0, i, 0)),
                pl.BlockSpec(memory_space=pl.ANY),
                pl.BlockSpec((8, COLS), lambda i, x: (i, 0)),
            ],
            scratch_shapes=[
                pltpu.VMEM((CH, 80, COLS), F32),
                pltpu.VMEM((80, COLS), F32),
                pltpu.VMEM((80, COLS), F32),
                pltpu.VMEM((CH, 72, COLS), F32),
                pltpu.VMEM((CH, ROWS, COLS), F32),
                pltpu.VMEM((CH + 2, ROWS, 128), F32),
                pltpu.SemaphoreType.DMA((4,)),
            ],
        ),
        out_shape=[
            jax.ShapeDtypeStruct((CH, ROWS, COLS), F32),
            jax.ShapeDtypeStruct((CH, ROWS, COLS), F32),
            jax.ShapeDtypeStruct((ROWS, COLS), F32),
        ],
        compiler_params=params(),
        name="sweep",
    )(idx, g, harm, elevation, depth, friction, mask, before, after, west, east, w)


LAT = ("zh", "x", "c")
LON = ("y", "zl")


def shift(value, axes, size, step):
    return lax.ppermute(value, axes, [(i, (i + step) % size) for i in range(size)])


def swap(x, axis):
    return lax.all_to_all(x, axis, 0, 0, tiled=True)


def on_device(elevation, depth, friction, land_mask, order_map, legendre, load):
    lat = lax.axis_index(LAT)
    lon = lax.axis_index(LON)
    core = lax.axis_index("c")
    idx = jnp.stack([lat, lon, core, core]).astype(jnp.int32)

    part, harm, half, first_row, last_row, ends = dft(
        idx, order_map[None, :], elevation, land_mask, depth, friction, legendre
    )
    received = swap(part.astype(jnp.float16), ("y", "zl", "c"))
    other = shift(half, "c", 2, 1)
    before = shift(last_row, LAT, 32, 1)
    after = shift(first_row, LAT, 32, -1)
    west = shift(ends, LON, 8, 1)
    east = shift(ends, LON, 8, -1)
    fourier = jnp.sum(received.reshape(8, 2, 16, 1024).astype(F32), axis=0) * (1.0 / PART_SCALE)
    coeffs, mid, outer = analyse(idx, fourier, legendre, other, (before, after), BF16)
    prior = shift(outer, LAT, 32, 2)
    later = shift(outer, LAT, 32, -2)

    by_band = swap(coeffs.reshape(16, 16, DEG), ("zh", "x"))
    total = jnp.sum(by_band.astype(F32), axis=0)
    scaled = (total * load[None, :]).astype(BF16)
    every = swap(jnp.broadcast_to(scaled[None], (16, 16, DEG)), ("zh", "x"))
    spread = synthesise(idx, every.reshape(8, 32, DEG), legendre, other, (mid, prior, later), (west, east), BF16)
    g = swap(spread, ("y", "zl", "c"))
    new, sal, fnew = sweep(
        idx, g.reshape(256, 1152), harm, elevation, depth, friction, land_mask,
        before, after, west, east, sample_matrix(),
    )
    return new, sal, fnew


def solution(mesh):
    fine = Mesh(mesh.devices.reshape(4, 4, 2, 4, 2), ("zh", "x", "c", "y", "zl"))
    return jax.shard_map(
        on_device,
        mesh=fine,
        in_specs=(
            P(None, LAT, LON),
            P(LAT, LON),
            P(LAT, LON),
            P(LAT, LON),
            P(),
            P(LON, LAT, None),
            P(),
        ),
        out_specs=(P(None, LAT, LON), P(None, LAT, LON), P(LAT, LON)),
        check_vma=False,
    )
```

time: 162 us -> 140 us (0.86)
  the two profiles are of different devices: /device:TPU:7 before, /device:TPU:65 now
where the time goes in v2:
time: 140 us; the launch traced here: 137 us
  blocking collectives  45 us (32%)
  Pallas kernels  31.8 us (23%)
  waiting for transfers between devices  28 us (20%)
  starting transfers between devices  27.4 us (20%)
  other arithmetic  3.03 us (2%)
    all_to_all x2, blocking collectives, swap(): return lax.all_to_all(x, axis, 0, 0, tiled=True)  45 us
    ppermute x7, waiting for transfers between devices, shift(): lax.ppermute(value, axes, [(i, (i + step) % size) for i in range(size)])  19.5 us
    pallas_call x1, Pallas kernels, sweep(): pl.pallas_call(sweep_kernel, grid_spec=pltpu.PrefetchScalarGridSpec(num_s...  15.6 us
    all_to_all x2, starting transfers between devices, swap(): return lax.all_to_all(x, axis, 0, 0, tiled=True)  14.7 us
    ppermute x7, starting transfers between devices, shift(): lax.ppermute(value, axes, [(i, (i + step) % size) for i in range(size)])  12.7 us
    all_to_all x2, waiting for transfers between devices, swap(): return lax.all_to_all(x, axis, 0, 0, tiled=True)  8.51 us
    pallas_call x1, Pallas kernels, dft(): pl.pallas_call(dft_kernel, grid_spec=pltpu.PrefetchScalarGridSpec(num_sca...  7.18 us
    pallas_call x1, Pallas kernels, synthesise(): pl.pallas_call(synth_kernel, grid_spec=pltpu.PrefetchScalarGridSpec(num_s...  4.85 us
  transfers between devices with their start and end apart: 9, of which 3 were waited for; matrix products, arithmetic and copies ran while one was open for 2% of the time, Pallas kernels for 0%

profile of v2, /device:TPU:65, one launch (start us, length us, event | category | flops | bytes accessed | tf_op | source)
XLA Modules:
  0.0 137.3 jit_solution(7228041948547661046)
XLA Ops:
  0.6 0.7 pad_add_fusion.idx
  1.3 7.2 %dft.1 = (f32[16,16,1024]{2,1,0:T(8,128)}, bf16[512,640]{1,0:T(8,128)(2,1)}, bf16[8,64,2048]{2,1,0:T(8,128)(2,1)}, f32[24,512]{1,0:T(8,128)}, f32[24,512]{1,0:T(8,128)}, /*index=5*/f32[8,1152]{1,0:T(8,128)}) custom-call(s32[4]{0:T(128)} %pad_add_fusion.idx, s32[1,128]{1,0:T(1,128)} %bitcast.13, f32[16,64,512]{2,1,0:T(8,128)} %elev_ref.3, ...), custom_call_target="tpu_custom_call" | custom-call | tf_op jit(solution)/shard_map/dft/pallas_call | solution.py:120
  8.5 0.0 copy-start.6
  8.5 0.8 collective-permute-start
  9.3 2.1 %convert_element_type.19 = f16[16,16,1024]{2,1,0:T(8,128)(2,1)} convert(f32[16,16,1024]{2,1,0:T(8,128)} %get-tuple-element.12) | non-fusion elementwise | flops 262144 | bytes 1572864 | tf_op jit(solution)/shard_map/convert_element_type | solution.py:549
  11.4 6.0 %all-to-all-start = ((f16[16,16,1024]{2,1,0:T(8,128)(2,1)}), f16[16,16,1024]{2,1,0:T(8,128)(2,1)S(1)}, u32[]{:S(2)}, u32[]{:S(2)}) async-start(f16[16,16,1024]{2,1,0:T(8,128)(2,1)} %convert_element_type.19), calls=%async_computation | async-start | bytes 1048576 | tf_op jit(solution)/shard_map/all_to_all | solution.py:537
  17.3 1.3 collective-permute-start.1
  18.6 8.5 %all-to-all-done = f16[16,16,1024]{2,1,0:T(8,128)(2,1)S(1)} async-done(((f16[16,16,1024]{2,1,0:T(8,128)(2,1)}), f16[16,16,1024]{2,1,0:T(8,128)(2,1)S(1)}, u32[]{:S(2)}, u32[]{:S(2)}) %all-to-all-start) | async-done | bytes 524320 | tf_op jit(solution)/shard_map/all_to_all | solution.py:537
  27.1 0.1 convert_reduce_fusion.1
  27.3 4.2 %analyse.1 = (bf16[8,32,2048]{2,1,0:T(8,128)(2,1)S(1)}, bf16[16,2048]{1,0:T(8,128)(2,1)S(1)}, bf16[16,2048]{1,0:T(8,128)(2,1)S(1)}) custom-call(s32[4]{0:T(128)S(1)} %copy-done.4, f32[2,16,1024]{2,1,0:T(8,128)S(1)} %broadcast_multiply_fusion.r_ref, bf16[16,64,2048]{2,1,0:T(8,128)(2,1)} %own_ref.3, bf16[8,64,2048]{2,1,0:T(8,128)(2,1)} %collective-permute-done.rcv_ref, ...), custom_call_target="tpu_custom_call" | custom-call | tf_op jit(solution)/shard_map/analyse/pallas_call | solution.py:192
  31.5 0.0 copy-start.5
  31.5 27.1 %all_to_all.20 = bf16[16,16,2048]{2,1,0:T(8,128)(2,1)S(1)} all-to-all(bf16[16,16,2048]{2,1,0:T(8,128)(2,1)S(1)} %bitcast.11), channel_id=1, replica_groups=mesh['zh'=4,'x'=4,'c'=2,'y'=4,'zl'=2] {'zh','x'}, dimensions={0} | all-to-all | bytes 2097152 | tf_op jit(solution)/shard_map/all_to_all | solution.py:537
  58.5 0.1 convert_reduce_fusion
  58.7 1.1 broadcast_in_dim.5
  59.8 8.7 %all-to-all-start.2 = ((bf16[16,16,2048]{2,1,0:T(8,128)(2,1)}), bf16[16,16,2048]{2,1,0:T(8,128)(2,1)S(1)}, u32[]{:S(2)}, u32[]{:S(2)}) async-start(bf16[16,16,2048]{2,1,0:T(8,128)(2,1)} %broadcast_in_dim.5), calls=%async_computation.2 | async-start | bytes 2097152 | tf_op jit(solution)/shard_map/all_to_all | solution.py:537
  68.5 2.4 %collective-permute-start.4 = (bf16[16,2048]{1,0:T(8,128)(2,1)S(1)}, bf16[16,2048]{1,0:T(8,128)(2,1)S(1)}, u32[]{:S(2)}, u32[]{:S(2)}) collective-permute-start(bf16[16,2048]{1,0:T(8,128)(2,1)S(1)} %get-tuple-element.18), channel_id=1, source_target_pairs={{0,240},{8,248},{16,0},{24,8},{32,16},{40,24},{48,32},{56,40},{64,... | collective-permute-start | bytes 196616 | tf_op jit(solution)/shard_map/ppermute | solution.py:533
  70.9 8.3 %collective-permute-start.6 = (f32[8,1152]{1,0:T(8,128)S(1)}, f32[8,1152]{1,0:T(8,128)S(1)}, u32[]{:S(2)}, u32[]{:S(2)}) collective-permute-start(f32[8,1152]{1,0:T(8,128)S(1)} %copy-done.8), channel_id=1, source_target_pairs={{0,7},{1,0},{2,1},{3,2},{4,3},{5,4},{6,5},{7,6},{8,15},{9,8},{10,9... | collective-permute-start | bytes 110600 | tf_op jit(solution)/shard_map/ppermute | solution.py:533
  79.2 16.1 %collective-permute-done.6.rest_1_.east_ref = f32[8,1152]{1,0:T(8,128)S(1)} collective-permute-done((f32[8,1152]{1,0:T(8,128)S(1)}, f32[8,1152]{1,0:T(8,128)S(1)}, u32[]{:S(2)}, u32[]{:S(2)}) %collective-permute-start.6) | collective-permute-done | bytes 36896 | tf_op jit(solution)/shard_map/ppermute | solution.py:533
  95.3 3.4 %collective-permute-done.5.rest_0_.west_ref = f32[8,1152]{1,0:T(8,128)S(1)} collective-permute-done((f32[8,1152]{1,0:T(8,128)S(1)}, f32[8,1152]{1,0:T(8,128)S(1)}, u32[]{:S(2)}, u32[]{:S(2)}) %collective-permute-start.5) | collective-permute-done | bytes 36896 | tf_op jit(solution)/shard_map/ppermute | solution.py:533
  98.7 0.0 copy-start.2
  98.8 0.0 copy-start.3
  98.8 4.8 %synthesise.1 = bf16[16,16,1152]{2,1,0:T(8,128)(2,1)S(1)} custom-call(s32[4]{0:T(128)S(1)} %copy-done.4, bf16[8,32,2048]{2,1,0:T(8,128)(2,1)S(1)} %bitcast.9, bf16[16,64,2048]{2,1,0:T(8,128)(2,1)} %own_ref.3, bf16[8,64,2048]{2,1,0:T(8,128)(2,1)} %collective-permute-done.rcv_ref, bf16[16,2048]{1,0:T(8,128)(2,1)S(1)} %get-tuple-element.17.mid_ref, ...), custom_call_target="tpu_custom_call" | custom-call | tf_op jit(solution)/shard_map/synthesise/pallas_call | solution.py:269
  103.6 17.9 %all_to_all.21 = bf16[16,16,1152]{2,1,0:T(8,128)(2,1)S(1)} all-to-all(bf16[16,16,1152]{2,1,0:T(8,128)(2,1)S(1)} %synthesise.1), channel_id=1, replica_groups=mesh['zh'=4,'x'=4,'c'=2,'y'=4,'zl'=2] {'y','zl','c'}, dimensions={0} | all-to-all | bytes 1179648 | tf_op jit(solution)/shard_map/all_to_all | solution.py:537
  121.6 15.6 %sweep.1 = (f32[16,64,512]{2,1,0:T(8,128)}, f32[16,64,512]{2,1,0:T(8,128)}, f32[64,512]{1,0:T(8,128)}) custom-call(s32[4]{0:T(128)S(1)} %copy-done.4, bf16[256,1152]{1,0:T(8,128)(2,1)S(1)} %bitcast.10, bf16[512,640]{1,0:T(8,128)(2,1)} %get-tuple-element.20.harm_ref, f32[16,64,512]{2,1,0:T(8,128)} %elev_ref.3, f32[64,512]{1,0:T(8,128)S(1)} %copy-done.1, ...), custom_call_target="tpu_custom_call" | custom-call | tf_op jit(solution)/shard_map/sweep/pallas_call | solution.py:485
  (25 shorter events, 0.1 us)
Async XLA Ops:
  8.5 8.8 %copy-start.7 = (f32[24,512]{1,0:T(8,128)S(1)}, f32[24,512]{1,0:T(8,128)}, u32[]{:S(2)}) copy-start(f32[24,512]{1,0:T(8,128)} %get-tuple-element.14) | copy-start | bytes 147460
  8.5 10.1 %copy-start.6 = (f32[24,512]{1,0:T(8,128)S(1)}, f32[24,512]{1,0:T(8,128)}, u32[]{:S(2)}) copy-start(f32[24,512]{1,0:T(8,128)} %get-tuple-element.15) | copy-start | bytes 147460
  8.5 18.8 %copy-start.4 = (s32[4]{0:T(128)S(1)}, s32[4]{0:T(128)}, u32[]{:S(2)}) copy-start(s32[4]{0:T(128)} %pad_add_fusion.idx) | copy-start | bytes 52
  8.5 18.7 %collective-permute-start = (bf16[8,64,2048]{2,1,0:T(8,128)(2,1)}, bf16[8,64,2048]{2,1,0:T(8,128)(2,1)}, u32[]{:S(2)}, u32[]{:S(2)}) collective-permute-start(bf16[8,64,2048]{2,1,0:T(8,128)(2,1)} %get-tuple-element.13), channel_id=1, source_target_pairs={{0,8},{8,0},{1,9},{9,1},{2,10},{10,2},{3,11},{11,3},{4,12},{12,4},... | collective-permute-start | bytes 6291464 | tf_op jit(solution)/shard_map/ppermute | solution.py:533
  11.4 15.7 %all-to-all-start = ((f16[16,16,1024]{2,1,0:T(8,128)(2,1)}), f16[16,16,1024]{2,1,0:T(8,128)(2,1)S(1)}, u32[]{:S(2)}, u32[]{:S(2)}) async-start(f16[16,16,1024]{2,1,0:T(8,128)(2,1)} %convert_element_type.19), calls=%async_computation | async-start | bytes 1048576 | tf_op jit(solution)/shard_map/all_to_all | solution.py:537
  17.3 9.9 %collective-permute-start.1 = (f32[24,512]{1,0:T(8,128)S(1)}, f32[24,512]{1,0:T(8,128)S(1)}, u32[]{:S(2)}, u32[]{:S(2)}) collective-permute-start(f32[24,512]{1,0:T(8,128)S(1)} %copy-done.7), channel_id=1, source_target_pairs={{0,8},{8,16},{16,24},{24,32},{32,40},{40,48},{48,56},{56,64},{64,7... | collective-permute-start | bytes 147464 | tf_op jit(solution)/shard_map/ppermute | solution.py:533
  18.6 8.6 %collective-permute-start.2 = (f32[24,512]{1,0:T(8,128)S(1)}, f32[24,512]{1,0:T(8,128)S(1)}, u32[]{:S(2)}, u32[]{:S(2)}) collective-permute-start(f32[24,512]{1,0:T(8,128)S(1)} %copy-done.6), channel_id=1, source_target_pairs={{0,248},{8,0},{16,8},{24,16},{32,24},{40,32},{48,40},{56,48},{64,5... | collective-permute-start | bytes 147464 | tf_op jit(solution)/shard_map/ppermute | solution.py:533
  31.5 27.2 %copy-start.5 = (f32[2048]{0:T(1024)S(1)}, f32[2048]{0:T(1024)}, u32[]{:S(2)}) copy-start(f32[2048]{0:T(1024)} %param.14) | copy-start | bytes 24580
  58.5 12.4 %copy-start.8 = (f32[8,1152]{1,0:T(8,128)S(1)}, f32[8,1152]{1,0:T(8,128)}, u32[]{:S(2)}) copy-start(f32[8,1152]{1,0:T(8,128)} %get-tuple-element.19) | copy-start | bytes 110596
  59.8 38.9 %all-to-all-start.2 = ((bf16[16,16,2048]{2,1,0:T(8,128)(2,1)}), bf16[16,16,2048]{2,1,0:T(8,128)(2,1)S(1)}, u32[]{:S(2)}, u32[]{:S(2)}) async-start(bf16[16,16,2048]{2,1,0:T(8,128)(2,1)} %broadcast_in_dim.5), calls=%async_computation.2 | async-start | bytes 2097152 | tf_op jit(solution)/shard_map/all_to_all | solution.py:537
  68.5 30.2 %collective-permute-start.4 = (bf16[16,2048]{1,0:T(8,128)(2,1)S(1)}, bf16[16,2048]{1,0:T(8,128)(2,1)S(1)}, u32[]{:S(2)}, u32[]{:S(2)}) collective-permute-start(bf16[16,2048]{1,0:T(8,128)(2,1)S(1)} %get-tuple-element.18), channel_id=1, source_target_pairs={{0,240},{8,248},{16,0},{24,8},{32,16},{40,24},{48,32},{56,40},{64,... | collective-permute-start | bytes 196616 | tf_op jit(solution)/shard_map/ppermute | solution.py:533
  70.9 27.8 %collective-permute-start.3 = (bf16[16,2048]{1,0:T(8,128)(2,1)S(1)}, bf16[16,2048]{1,0:T(8,128)(2,1)S(1)}, u32[]{:S(2)}, u32[]{:S(2)}) collective-permute-start(bf16[16,2048]{1,0:T(8,128)(2,1)S(1)} %get-tuple-element.18), channel_id=1, source_target_pairs={{0,16},{8,24},{16,32},{24,40},{32,48},{40,56},{48,64},{56,72},{64,... | collective-permute-start | bytes 196616 | tf_op jit(solution)/shard_map/ppermute | solution.py:533
  70.9 24.4 %collective-permute-start.6 = (f32[8,1152]{1,0:T(8,128)S(1)}, f32[8,1152]{1,0:T(8,128)S(1)}, u32[]{:S(2)}, u32[]{:S(2)}) collective-permute-start(f32[8,1152]{1,0:T(8,128)S(1)} %copy-done.8), channel_id=1, source_target_pairs={{0,7},{1,0},{2,1},{3,2},{4,3},{5,4},{6,5},{7,6},{8,15},{9,8},{10,9... | collective-permute-start | bytes 110600 | tf_op jit(solution)/shard_map/ppermute | solution.py:533
  79.2 19.5 %collective-permute-start.5 = (f32[8,1152]{1,0:T(8,128)S(1)}, f32[8,1152]{1,0:T(8,128)S(1)}, u32[]{:S(2)}, u32[]{:S(2)}) collective-permute-start(f32[8,1152]{1,0:T(8,128)S(1)} %copy-done.8), channel_id=1, source_target_pairs={{0,1},{1,2},{2,3},{3,4},{4,5},{5,6},{6,7},{7,0},{8,9},{9,10},{10,1... | collective-permute-start | bytes 110600 | tf_op jit(solution)/shard_map/ppermute | solution.py:533
  98.7 22.8 %copy-start = (s32[64,512]{1,0:T(8,128)S(1)}, s32[64,512]{1,0:T(8,128)}, u32[]{:S(2)}) copy-start(s32[64,512]{1,0:T(8,128)} %mask_ref.3) | copy-start | bytes 393220
  98.7 22.8 %copy-start.1 = (f32[64,512]{1,0:T(8,128)S(1)}, f32[64,512]{1,0:T(8,128)}, u32[]{:S(2)}) copy-start(f32[64,512]{1,0:T(8,128)} %depth_ref.3) | copy-start | bytes 393220
  98.7 22.8 %copy-start.2 = (f32[64,512]{1,0:T(8,128)S(1)}, f32[64,512]{1,0:T(8,128)}, u32[]{:S(2)}) copy-start(f32[64,512]{1,0:T(8,128)} %fric_ref.3) | copy-start | bytes 393220
  98.8 22.8 %copy-start.3 = (bf16[512,384]{1,0:T(8,128)(2,1)S(1)}, bf16[512,384]{1,0:T(8,128)(2,1)}, u32[]{:S(2)}) copy-start(bf16[512,384]{1,0:T(8,128)(2,1)} %constant.29.clone.w_ref) | copy-start | bytes 1179652

commit v3 on v2

--- a/solution.py
+++ b/solution.py
@@ -30,7 +30,7 @@
 PART_SCALE = 512.0
 
 
-def params(mib=52):
+def params(mib=24):
     return pltpu.CompilerParams(vmem_limit_bytes=mib * 1024 * 1024)
 
 
@@ -67,17 +67,6 @@
     i = pl.program_id(0)
     half_ref[...] = leg_ref[...]
     mask = mask_ref[...].astype(F32)
-    sub = lax.broadcasted_iota(jnp.int32, (8, 128), 0)
-    lane = lax.broadcasted_iota(jnp.int32, (8, 128), 1)
-    pick_first = jnp.where((sub == 0) & (lane == 0), 1.0, 0.0).astype(F32)
-    pick_last = jnp.where((sub == 1) & (lane == 127), 1.0, 0.0).astype(F32)
-
-    def ends(x):
-        def pick(sel, tile):
-            return lax.dot_general(sel, tile, NT, precision=lax.Precision.HIGHEST, preferred_element_type=F32)
-
-        return pick(pick_first, x[:, :128]) + pick(pick_last, x[:, COLS - 128 :])
-
     @pl.when(i == 0)
     def _():
         diag = lax.broadcasted_iota(jnp.int32, (128, 128), 0) == lax.broadcasted_iota(jnp.int32, (128, 128), 1)
@@ -91,26 +80,34 @@
             cos, sin = unit_circle(m * col)
             scale = jnp.where(m > 0, math.sqrt(2.0 / NLON), math.sqrt(1.0 / NLON)).astype(F32)
             hi, lo = split(jnp.concatenate([cos * scale, sin * scale], axis=0))
-            harm_ref[16 * g : 16 * g + 16, :] = hi
-            harm_ref[256 + 16 * g : 256 + 16 * g + 16, :] = lo
+            harm_ref[16 * g : 16 * g + 16, :] = lo
+            harm_ref[272 + 16 * g : 288 + 16 * g, :] = hi
+        sub = lax.broadcasted_iota(jnp.int32, (16, COLS + 128), 0)
+        lane = lax.broadcasted_iota(jnp.int32, (16, COLS + 128), 1)
+        ends = ((sub == 0) & (lane == 0)) | ((sub == 1) & (lane == COLS - 1))
+        harm_ref[256:272, :] = jnp.where(ends, 1.0, 0.0).astype(BF16)
         sea = depth_ref[...] * mask
         for r, x in ((16, sea), (17, fric_ref[...])):
             first_ref[r : r + 1, :] = x[:1]
             last_ref[r : r + 1, :] = x[ROWS - 1 :]
         first_ref[18:, :] = jnp.zeros((6, COLS), F32)
         last_ref[18:, :] = jnp.zeros((6, COLS), F32)
-        cols_ref[:, 1024:] = ends(jnp.concatenate([sea, fric_ref[...]], axis=0))
+        pick = harm_ref[256:272, :COLS]
+        hi, lo = split(jnp.concatenate([sea, fric_ref[...]], axis=0))
+        edge = lax.dot_general(pick, hi, NT, preferred_element_type=F32)
+        edge = edge + lax.dot_general(pick, lo, NT, preferred_element_type=F32)
+        cols_ref[:, 1024:] = edge[:8]
 
     field = jnp.concatenate([elev_ref[c] * mask for c in range(4)], axis=0)
     hi, lo = split(field)
     both = lax.dot_general(harm_ref[:, :COLS], hi, NT, preferred_element_type=F32)
-    small = lax.dot_general(harm_ref[:256, :COLS], lo, NT, preferred_element_type=F32)
-    out = both[:256] + (both[256:] + small)
+    small = lax.dot_general(harm_ref[256:, :COLS], lo, NT, preferred_element_type=F32)
+    out = both[272:] + (both[:256] + small[16:])
     part_ref[...] = (out * PART_SCALE).reshape(16, 16, 256).astype(part_ref.dtype)
     for c in range(4):
         first_ref[pl.ds(4 * i + c, 1), :] = field[64 * c : 64 * c + 1]
         last_ref[pl.ds(4 * i + c, 1), :] = field[64 * c + 63 : 64 * c + 64]
-    cols_ref[:, pl.ds(pl.multiple_of(256 * i, 256), 256)] = ends(field)
+    cols_ref[:, pl.ds(pl.multiple_of(256 * i, 256), 256)] = both[256:264] + small[:8]
 
 
 def dft(idx, om, elevation, mask, depth, friction, legendre):
@@ -132,7 +129,7 @@
             ],
             out_specs=[
                 pl.BlockSpec((16, 16, 256), lambda i, x: (0, 0, i)),
-                whole((512, COLS + 128)),
+                whole((528, COLS + 128)),
                 pl.BlockSpec((2, ROWS, DEG), lambda i, x: (i, 0, 0)),
                 whole((24, COLS)),
                 whole((24, COLS)),
@@ -141,7 +138,7 @@
         ),
         out_shape=[
             jax.ShapeDtypeStruct((16, 16, 1024), F32),
-            jax.ShapeDtypeStruct((512, COLS + 128), BF16),
+            jax.ShapeDtypeStruct((528, COLS + 128), BF16),
             jax.ShapeDtypeStruct((8, ROWS, DEG), BF16),
             jax.ShapeDtypeStruct((24, COLS), F32),
             jax.ShapeDtypeStruct((24, COLS), F32),
@@ -153,7 +150,7 @@
 
 
 def analyse_kernel(idx, r_ref, own_ref, rcv_ref, *rest):
-    out_ref, mid_ref, outer_ref, a_ref, e_ref = rest[-5:]
+    outs, (mid_ref, outer_ref, a_ref, e_ref) = rest[-8:-4], rest[-4:]
 
     @pl.when(pl.program_id(0) == 0)
     def _():
@@ -169,17 +166,24 @@
                     a_ref[pl.ds(16 * p + ch, 8, stride=32), :] = val[8 * p : 8 * p + 8, :]
 
     i = pl.program_id(0)
+    pair = (idx[3] + i) & 3
     for s in range(2):
-        a = a_ref[pl.ds(pl.multiple_of(64 * i, 64) + 32 * s, 32), :].astype(BF16)
+        a = a_ref[pl.ds(pl.multiple_of(64 * pair, 64) + 32 * s, 32), :].astype(BF16)
         table = jnp.concatenate([own_ref[s], rcv_ref[s]], axis=0)
-        out_ref[s] = jnp.dot(a, table, preferred_element_type=F32).astype(out_ref.dtype)
+        sums = jnp.dot(a, table, preferred_element_type=F32)
+        for k, out_ref in enumerate(outs):
+
+            @pl.when(i == k)
+            def _():
+                out_ref[s] = sums.astype(out_ref.dtype)
+
         low = idx[2] == 0
         own_first, own_last = own_ref[s, :16].astype(F32)[:1], own_ref[s, ROWS - 16 :].astype(F32)[15:]
         rcv_first, rcv_last = rcv_ref[s, :16].astype(F32)[:1], rcv_ref[s, ROWS - 16 :].astype(F32)[15:]
-        e_ref[pl.ds(2 * i + s, 1), :] = jnp.where(low, rcv_first, own_first)
-        e_ref[pl.ds(8 + 2 * i + s, 1), :] = jnp.where(low, own_last, rcv_last)
-        e_ref[pl.ds(16 + 2 * i + s, 1), :] = jnp.where(low, own_first, rcv_first)
-        e_ref[pl.ds(24 + 2 * i + s, 1), :] = jnp.where(low, rcv_last, own_last)
+        e_ref[pl.ds(2 * pair + s, 1), :] = jnp.where(low, rcv_first, own_first)
+        e_ref[pl.ds(8 + 2 * pair + s, 1), :] = jnp.where(low, own_last, rcv_last)
+        e_ref[pl.ds(16 + 2 * pair + s, 1), :] = jnp.where(low, own_first, rcv_first)
+        e_ref[pl.ds(24 + 2 * pair + s, 1), :] = jnp.where(low, rcv_last, own_last)
 
     @pl.when(i == 3)
     def _():
@@ -188,7 +192,7 @@
 
 
 def analyse(idx, received, legendre, other, after, dtype):
-    table = pl.BlockSpec((2, ROWS, DEG), lambda i, x: (4 * x[2] + i, 0, 0))
+    whole = pl.BlockSpec((2, 32, DEG), lambda i, x: (0, 0, 0))
     return pl.pallas_call(
         analyse_kernel,
         grid_spec=pltpu.PrefetchScalarGridSpec(
@@ -196,19 +200,25 @@
             grid=(4,),
             in_specs=[
                 pl.BlockSpec((2, 16, 1024), lambda i, x: (0, 0, 0)),
-                table,
-                pl.BlockSpec((2, ROWS, DEG), lambda i, x: (i, 0, 0)),
+                pl.BlockSpec((2, ROWS, DEG), lambda i, x: (4 * x[2] + ((x[3] + i) & 3), 0, 0)),
+                pl.BlockSpec((2, ROWS, DEG), lambda i, x: ((x[3] + i) & 3, 0, 0)),
             ]
             + [pl.BlockSpec(memory_space=pl.ANY)] * len(after),
             out_specs=[
-                pl.BlockSpec((2, 32, DEG), lambda i, x: (i, 0, 0)),
+                whole,
+                whole,
+                whole,
+                whole,
                 pl.BlockSpec((16, DEG), lambda i, x: (0, 0)),
                 pl.BlockSpec((16, DEG), lambda i, x: (0, 0)),
             ],
             scratch_shapes=[pltpu.VMEM((256, 128), F32), pltpu.VMEM((32, DEG), F32)],
         ),
         out_shape=[
-            jax.ShapeDtypeStruct((8, 32, DEG), dtype),
+            jax.ShapeDtypeStruct((2, 32, DEG), F32),
+            jax.ShapeDtypeStruct((2, 32, DEG), dtype),
+            jax.ShapeDtypeStruct((2, 32, DEG), dtype),
+            jax.ShapeDtypeStruct((2, 32, DEG), dtype),
             jax.ShapeDtypeStruct((16, DEG), BF16),
             jax.ShapeDtypeStruct((16, DEG), BF16),
         ],
@@ -217,15 +227,46 @@
     )(idx, received, legendre, other, *after)
 
 
-def synth_kernel(idx, sc_ref, own_ref, rcv_ref, mid_ref, prev_ref, next_ref, *rest):
-    out_ref, t_ref, u_ref = rest[-3:]
+def add_kernel(idx, own_ref, a_ref, b_ref, c_ref, *outs):
+    for k, out_ref in enumerate(outs):
+        z = (idx[4] + k) & 3
+        total = own_ref[z] + a_ref[z].astype(F32) + b_ref[z].astype(F32) + c_ref[z].astype(F32)
+        out_ref[...] = total.astype(out_ref.dtype)
+
+
+def add_bands(idx, own, others, dtype):
+    part = pl.BlockSpec((4, 16, DEG), lambda i, x: (0, 0, 0))
+    return pl.pallas_call(
+        add_kernel,
+        grid_spec=pltpu.PrefetchScalarGridSpec(
+            num_scalar_prefetch=1,
+            grid=(1,),
+            in_specs=[part] * 4,
+            out_specs=[pl.BlockSpec((16, DEG), lambda i, x: (0, 0))] * 4,
+        ),
+        out_shape=[jax.ShapeDtypeStruct((16, DEG), t) for t in (F32, dtype, dtype, dtype)],
+        compiler_params=params(),
+        name="add_bands",
+    )(idx, own.reshape(4, 16, DEG), *[x.reshape(4, 16, DEG) for x in others])
+
+
+def synth_kernel(idx, w0_ref, w1_ref, w2_ref, w3_ref, own_ref, rcv_ref, mid_ref, prev_ref, next_ref, out_ref, sc_ref, t_ref, u_ref):
     edges = jnp.concatenate([mid_ref[...], prev_ref[...], next_ref[...]], axis=0)
     i = pl.program_id(0)
+    pair = (idx[3] - i) & 3
+    for k, w_ref in enumerate((w0_ref, w1_ref, w2_ref, w3_ref)):
+
+        @pl.when(i == k)
+        def _():
+            for z in range(4):
+                sc_ref[16 * z : 16 * z + 16, :] = w_ref[(idx[4] - z) & 3]
+
     for s in range(2):
         table = jnp.concatenate([own_ref[s], rcv_ref[s]], axis=0)
-        row = pl.multiple_of(64 * i, 64) + 32 * s
-        t_ref[pl.ds(row, 32), :] = lax.dot_general(sc_ref[s], table, NT, preferred_element_type=F32)
-        u_ref[2 * i + s, :, :32] = lax.dot_general(edges, sc_ref[s], NT, preferred_element_type=F32)
+        row = pl.multiple_of(64 * pair, 64) + 32 * s
+        scaled = sc_ref[32 * s : 32 * s + 32, :]
+        t_ref[pl.ds(row, 32), :] = lax.dot_general(scaled, table, NT, preferred_element_type=F32)
+        u_ref[2 * pair + s, :, :32] = lax.dot_general(edges, scaled, NT, preferred_element_type=F32)
 
     @pl.when(i == 3)
     def _():
@@ -264,27 +305,32 @@
                 out_ref[2 * d + half, :, 1024:] = edge
 
 
-def synthesise(idx, scaled, legendre, other, edges, after, dtype):
-    table = pl.BlockSpec((2, ROWS, DEG), lambda i, x: (4 * x[2] + i, 0, 0))
+def synthesise(idx, parts, legendre, other, edges, dtype):
+    def whole(shape):
+        return pl.BlockSpec(shape, lambda i, x: (0,) * len(shape))
+
     return pl.pallas_call(
         synth_kernel,
         grid_spec=pltpu.PrefetchScalarGridSpec(
             num_scalar_prefetch=1,
             grid=(4,),
-            in_specs=[
-                pl.BlockSpec((2, 32, DEG), lambda i, x: (i, 0, 0)),
-                table,
-                pl.BlockSpec((2, ROWS, DEG), lambda i, x: (i, 0, 0)),
+            in_specs=[whole((4, 16, DEG))] * 4
+            + [
+                pl.BlockSpec((2, ROWS, DEG), lambda i, x: (4 * x[2] + ((x[3] - i) & 3), 0, 0)),
+                pl.BlockSpec((2, ROWS, DEG), lambda i, x: ((x[3] - i) & 3, 0, 0)),
             ]
-            + [pl.BlockSpec((16, DEG), lambda i, x: (0, 0))] * 3
-            + [pl.BlockSpec(memory_space=pl.ANY)] * len(after),
-            out_specs=pl.BlockSpec((16, 16, 1152), lambda i, x: (0, 0, 0)),
-            scratch_shapes=[pltpu.VMEM((256, 128), F32), pltpu.VMEM((8, 48, 128), F32)],
+            + [whole((16, DEG))] * 3,
+            out_specs=whole((16, 16, 1152)),
+            scratch_shapes=[
+                pltpu.VMEM((64, DEG), BF16),
+                pltpu.VMEM((256, 128), F32),
+                pltpu.VMEM((8, 48, 128), F32),
+            ],
         ),
         out_shape=jax.ShapeDtypeStruct((16, 16, 1152), dtype),
         compiler_params=params(),
         name="synthesise",
-    )(idx, scaled, legendre, other, *edges, *after)
+    )(idx, *parts, legendre, other, *edges)
 
 
 def lat_of(row):
@@ -322,19 +368,16 @@
 
         def invert(cols):
             part = g_ref[:, cols]
-            hi = lax.dot_general(part, harm_ref[:256, :], TN, preferred_element_type=F32)
-            lo = lax.dot_general(part, harm_ref[256:, :], TN, preferred_element_type=F32)
+            hi = lax.dot_general(part, harm_ref[272:, :], TN, preferred_element_type=F32)
+            lo = lax.dot_general(part, harm_ref[:256, :], TN, preferred_element_type=F32)
             return hi + lo
 
-        sub = lax.broadcasted_iota(jnp.int32, (8, 128), 0)
-        lane = lax.broadcasted_iota(jnp.int32, (8, 128), 1)
-        to_low = jnp.where((sub == 1) & (lane < 64), 1.0, 0.0).astype(F32)
-        to_high = jnp.where((sub == 0) & (lane >= 64), 1.0, 0.0).astype(F32)
-
-        def place(x, sel):
-            return lax.dot_general(x, sel, TN, precision=lax.Precision.HIGHEST, preferred_element_type=F32)
-
-        beside = place(west_ref[...], to_low) + place(east_ref[...], to_high)
+        sub = lax.broadcasted_iota(jnp.int32, (32, 128), 0) & 15
+        lane = lax.broadcasted_iota(jnp.int32, (32, 128), 1)
+        place = ((sub == 1) & (lane < 64)) | ((sub == 8) & (lane >= 64))
+        place = jnp.where(place, 1.0, 0.0).astype(BF16)
+        hi, lo = split(jnp.concatenate([west_ref[...], east_ref[...]], axis=0))
+        beside = lax.dot_general(jnp.concatenate([hi, lo], axis=0), place, TN, preferred_element_type=F32)
         for ch in range(18):
             lonh_all[ch] = beside[64 * ch : 64 * ch + 64]
         edge = invert(slice(1024, 1152))
@@ -447,7 +490,7 @@
 
     def stacked(parts):
         hi, lo = split(jnp.concatenate(parts, axis=0))
-        return jnp.concatenate([hi, lo, hi], axis=0)
+        return jnp.concatenate([hi, lo], axis=0)
 
     xe, xn = stacked(ecell), stacked(ncell)
     total = jnp.zeros((8, COLS), F32)
@@ -472,9 +515,8 @@
     phases = time * np.asarray(FREQUENCIES, np.float32)[None, :]
     table = np.stack([np.cos(phases), np.sin(phases)], axis=2).reshape(SAMPLES, CH).astype(np.float32)
     hi = table.astype(jnp.bfloat16)
-    lo = (table - hi.astype(np.float32)).astype(jnp.bfloat16)
     eye = np.eye(8, dtype=np.float32)
-    wide = [np.kron(x.astype(np.float32), eye) for x in (hi, hi, lo)]
+    wide = [np.kron(x.astype(np.float32), eye) for x in (hi, hi)]
     return jnp.asarray(np.concatenate(wide, axis=1), BF16)
 
 
@@ -489,7 +531,7 @@
             grid=(8,),
             in_specs=[
                 whole((256, 1152)),
-                whole((512, COLS + 128)),
+                whole((528, COLS + 128)),
                 whole((CH, ROWS, COLS)),
                 whole((ROWS, COLS)),
                 whole((ROWS, COLS)),
@@ -498,7 +540,7 @@
                 whole((24, COLS)),
                 whole((8, 1152)),
                 whole((8, 1152)),
-                whole((512, 384)),
+                whole((512, 256)),
             ],
             out_specs=[
                 pl.BlockSpec((CH, 8, COLS), lambda i, x: (0, i, 0)),
@@ -533,6 +575,14 @@
     return lax.ppermute(value, axes, [(i, (i + step) % size) for i in range(size)])
 
 
+def shift_lat(value, step):
+    return lax.ppermute(value, LAT, [(i, i + step) for i in range(32) if 0 <= i + step < 32])
+
+
+def all_shifts(values, axis):
+    return [shift(value, axis, 4, k + 1) for k, value in enumerate(values)]
+
+
 def swap(x, axis):
     return lax.all_to_all(x, axis, 0, 0, tiled=True)
 
@@ -541,27 +591,30 @@
     lat = lax.axis_index(LAT)
     lon = lax.axis_index(LON)
     core = lax.axis_index("c")
-    idx = jnp.stack([lat, lon, core, core]).astype(jnp.int32)
+    x, z = lax.axis_index("x"), lax.axis_index("zh")
+    idx = jnp.stack([lat, lon, core, x, z]).astype(jnp.int32)
 
     part, harm, half, first_row, last_row, ends = dft(
         idx, order_map[None, :], elevation, land_mask, depth, friction, legendre
     )
     received = swap(part.astype(jnp.float16), ("y", "zl", "c"))
     other = shift(half, "c", 2, 1)
-    before = shift(last_row, LAT, 32, 1)
-    after = shift(first_row, LAT, 32, -1)
+    before = shift_lat(last_row, 1)
+    after = shift_lat(first_row, -1)
     west = shift(ends, LON, 8, 1)
     east = shift(ends, LON, 8, -1)
     fourier = jnp.sum(received.reshape(8, 2, 16, 1024).astype(F32), axis=0) * (1.0 / PART_SCALE)
-    coeffs, mid, outer = analyse(idx, fourier, legendre, other, (before, after), BF16)
-    prior = shift(outer, LAT, 32, 2)
-    later = shift(outer, LAT, 32, -2)
-
-    by_band = swap(coeffs.reshape(16, 16, DEG), ("zh", "x"))
-    total = jnp.sum(by_band.astype(F32), axis=0)
+    own, *parts, mid, outer = analyse(idx, fourier, legendre, other, (before, after, west, east), BF16)
+    prior = shift_lat(outer, 2)
+    later = shift_lat(outer, -2)
+
+    own, *parts = add_bands(idx, own, all_shifts(parts, "x"), BF16)
+    total = own + sum(part.astype(F32) for part in all_shifts(parts, "zh"))
     scaled = (total * load[None, :]).astype(BF16)
-    every = swap(jnp.broadcast_to(scaled[None], (16, 16, DEG)), ("zh", "x"))
-    spread = synthesise(idx, every.reshape(8, 32, DEG), legendre, other, (mid, prior, later), (west, east), BF16)
+    by_z = jnp.stack([scaled, *all_shifts([scaled] * 3, "zh")])
+    spread = synthesise(
+        idx, [by_z, *all_shifts([by_z] * 3, "x")], legendre, other, (mid, prior, later), BF16
+    )
     g = swap(spread, ("y", "zl", "c"))
     new, sal, fnew = sweep(
         idx, g.reshape(256, 1152), harm, elevation, depth, friction, land_mask,

time: 140 us -> 130 us (0.929); the launches traced: 137 us -> 130 us
  blocking collectives: 45 us -> 20 us
  starting transfers between devices: 27.4 us -> 48.4 us
  Pallas kernels: 31.8 us -> 24.2 us
  waiting for transfers between devices: 28 us -> 30.8 us
  local copies, waits for them, and re-layouts: 1.14 us -> 2.9 us
    all_to_all x2 -> x1, blocking collectives: 45 us -> 20 us  [swap(): return lax.all_to_all(x, axis, 0, 0, tiled=True)]
    ppermute x7 -> x15, starting transfers between devices: 12.7 us -> 31.1 us  [shift(): lax.ppermute(value, axes, [(i, (i + step) % size) for i in range(size)])]
    ppermute x0 -> x4, starting transfers between devices: none -> 11.3 us  [shift_lat(): lax.ppermute(value, LAT, [(i, i + step) for i in range(32) if 0 <= i + st...]
    all_to_all x2 -> x1, starting transfers between devices: 14.7 us -> 5.95 us  [swap(): return lax.all_to_all(x, axis, 0, 0, tiled=True)]
    all_to_all x2 -> x1, waiting for transfers between devices: 8.51 us -> 0.62 us  [swap(): return lax.all_to_all(x, axis, 0, 0, tiled=True)]
    ppermute x0 -> x4, waiting for transfers between devices: none -> 7.2 us  [shift_lat(): lax.ppermute(value, LAT, [(i, i + step) for i in range(32) if 0 <= i + st...]
    pallas_call x1, Pallas kernels: 15.6 us -> 10.9 us  [sweep(): pl.pallas_call(sweep_kernel, grid_spec=pltpu.PrefetchScalarGridSpec(num_s...]
    ppermute x7 -> x15, waiting for transfers between devices: 19.5 us -> 23 us  [shift(): lax.ppermute(value, axes, [(i, (i + step) % size) for i in range(size)])]
  transfers between devices with their start and end apart: 9 -> 20, of which waited for: 3 -> 11; matrix products, arithmetic and copies ran while one was open for 2% -> 2% of each run, Pallas kernels for 0% -> 0%
where the time goes in v3:
time: 130 us
  starting transfers between devices  48.4 us (37%)
  waiting for transfers between devices  30.8 us (24%)
  Pallas kernels  24.2 us (19%)
  blocking collectives  20 us (15%)
  local copies, waits for them, and re-layouts  2.9 us (2%)
  other arithmetic  2.29 us (2%)
    ppermute x15, starting transfers between devices, shift(): lax.ppermute(value, axes, [(i, (i + step) % size) for i in range(size)])  31.1 us
    ppermute x15, waiting for transfers between devices, shift(): lax.ppermute(value, axes, [(i, (i + step) % size) for i in range(size)])  23 us
    all_to_all x1, blocking collectives, swap(): return lax.all_to_all(x, axis, 0, 0, tiled=True)  20 us
    ppermute x4, starting transfers between devices, shift_lat(): lax.ppermute(value, LAT, [(i, i + step) for i in range(32) if 0 <= i + st...  11.3 us
    pallas_call x1, Pallas kernels, sweep(): pl.pallas_call(sweep_kernel, grid_spec=pltpu.PrefetchScalarGridSpec(num_s...  10.9 us
    ppermute x4, waiting for transfers between devices, shift_lat(): lax.ppermute(value, LAT, [(i, i + step) for i in range(32) if 0 <= i + st...  7.2 us
    pallas_call x1, Pallas kernels, dft(): pl.pallas_call(dft_kernel, grid_spec=pltpu.PrefetchScalarGridSpec(num_sca...  6.79 us
    all_to_all x1, starting transfers between devices, swap(): return lax.all_to_all(x, axis, 0, 0, tiled=True)  5.95 us
  transfers between devices with their start and end apart: 20, of which 11 were waited for; matrix products, arithmetic and copies ran while one was open for 2% of the time, Pallas kernels for 0%

profile of v3, /device:TPU:65, one launch (start us, length us, event | category | flops | bytes accessed | tf_op | source)
XLA Modules:
  0.0 129.6 jit_solution(10751349520300680981)
XLA Ops:
  1.3 6.8 %dft.1 = (f32[16,16,1024]{2,1,0:T(8,128)}, bf16[528,640]{1,0:T(8,128)(2,1)}, bf16[8,64,2048]{2,1,0:T(8,128)(2,1)}, f32[24,512]{1,0:T(8,128)}, f32[24,512]{1,0:T(8,128)}, /*index=5*/f32[8,1152]{1,0:T(8,128)}) custom-call(s32[5]{0:T(128)} %stack.38.idx, s32[1,128]{1,0:T(1,128)} %bitcast.27, f32[16,64,512]{2,1,0:T(8,128)} %elev_ref.3, s32[64,512]{1,0:T(8,128)} %mask_ref.3, ...), custom_call_target="tpu_custom_call" | custom-call | tf_op jit(solution)/shard_map/dft/pallas_call | solution.py:117
  8.9 2.1 %convert_element_type.21 = f16[16,16,1024]{2,1,0:T(8,128)(2,1)} convert(f32[16,16,1024]{2,1,0:T(8,128)} %get-tuple-element.19) | non-fusion elementwise | flops 262144 | bytes 1572864 | tf_op jit(solution)/shard_map/convert_element_type | solution.py:600
  11.0 5.9 %all-to-all-start = ((f16[16,16,1024]{2,1,0:T(8,128)(2,1)}), f16[16,16,1024]{2,1,0:T(8,128)(2,1)S(1)}, u32[]{:S(2)}, u32[]{:S(2)}) async-start(f16[16,16,1024]{2,1,0:T(8,128)(2,1)} %convert_element_type.21), calls=%async_computation | async-start | bytes 1048576 | tf_op jit(solution)/shard_map/all_to_all | solution.py:587
  17.0 3.6 %collective-permute-start.4 = (f32[8,1152]{1,0:T(8,128)S(1)}, f32[8,1152]{1,0:T(8,128)S(1)}, u32[]{:S(2)}, u32[]{:S(2)}) collective-permute-start(f32[8,1152]{1,0:T(8,128)S(1)} %copy-done.12), channel_id=1, source_target_pairs={{0,7},{1,0},{2,1},{3,2},{4,3},{5,4},{6,5},{7,6},{8,15},{9,8},{10,9... | collective-permute-start | bytes 110600 | tf_op jit(solution)/shard_map/ppermute | solution.py:575
  20.5 3.6 %collective-permute-start.1 = (f32[24,512]{1,0:T(8,128)S(1)}, f32[24,512]{1,0:T(8,128)S(1)}, u32[]{:S(2)}, u32[]{:S(2)}) collective-permute-start(f32[24,512]{1,0:T(8,128)S(1)} %copy-done.11), channel_id=1, source_target_pairs={{0,8},{8,16},{16,24},{24,32},{32,40},{40,48},{48,56},{56,64},{64,7... | collective-permute-start | bytes 147464 | tf_op jit(solution)/shard_map/ppermute | solution.py:579
  24.2 1.9 %collective-permute-start.2 = (f32[24,512]{1,0:T(8,128)S(1)}, f32[24,512]{1,0:T(8,128)S(1)}, u32[]{:S(2)}, u32[]{:S(2)}) collective-permute-start(f32[24,512]{1,0:T(8,128)S(1)} %copy-done.10), channel_id=1, source_target_pairs={{8,0},{16,8},{24,16},{32,24},{40,32},{48,40},{56,48},{64,56},{72,6... | collective-permute-start | bytes 147464 | tf_op jit(solution)/shard_map/ppermute | solution.py:579
  29.6 2.2 %copy-done = bf16[16,64,2048]{2,1,0:T(8,128)(2,1)S(1)} copy-done((bf16[16,64,2048]{2,1,0:T(8,128)(2,1)S(1)}, bf16[16,64,2048]{2,1,0:T(8,128)(2,1)}, u32[]{:S(2)}) %copy-start) | copy-done | bytes 4194328
  31.8 2.8 %analyse.1 = (f32[2,32,2048]{2,1,0:T(8,128)S(1)}, bf16[2,32,2048]{2,1,0:T(8,128)(2,1)S(1)}, bf16[2,32,2048]{2,1,0:T(8,128)(2,1)S(1)}, bf16[2,32,2048]{2,1,0:T(8,...) custom-call(s32[5]{0:T(128)S(1)} %copy-done.8, ...), custom_call_target="tpu_custom_call" | custom-call | tf_op jit(solution)/shard_map/analyse/pallas_call | solution.py:196
  35.9 9.2 %collective-permute-start.6 = (bf16[2,32,2048]{2,1,0:T(8,128)(2,1)S(1)}, bf16[2,32,2048]{2,1,0:T(8,128)(2,1)S(1)}, u32[]{:S(2)}, u32[]{:S(2)}) collective-permute-start(bf16[2,32,2048]{2,1,0:T(8,128)(2,1)S(1)} %get-tuple-element.26), channel_id=1, source_target_pairs={{0,32},{16,48},{32,0},{48,16},{1,33},{17,49},{33,1},{49,17},{2,34}... | collective-permute-start | bytes 786440 | tf_op jit(solution)/shard_map/ppermute | solution.py:575
  45.1 7.2 %collective-permute-done.5 = bf16[2,32,2048]{2,1,0:T(8,128)(2,1)S(1)} collective-permute-done((bf16[2,32,2048]{2,1,0:T(8,128)(2,1)S(1)}, bf16[2,32,2048]{2,1,0:T(8,128)(2,1)S(1)}, u32[]{:S(2)}, u32[]{:S(2)}) %collective-permute-start.5) | collective-permute-done | bytes 262176 | tf_op jit(solution)/shard_map/ppermute | solution.py:575
  53.9 3.4 %collective-permute-start.8 = (bf16[16,2048]{1,0:T(8,128)(2,1)S(1)}, bf16[16,2048]{1,0:T(8,128)(2,1)S(1)}, u32[]{:S(2)}, u32[]{:S(2)}) collective-permute-start(bf16[16,2048]{1,0:T(8,128)(2,1)S(1)} %get-tuple-element.29), channel_id=1, source_target_pairs={{0,64},{64,128},{128,192},{192,0},{1,65},{65,129},{129,193},{193,1... | collective-permute-start | bytes 196616 | tf_op jit(solution)/shard_map/ppermute | solution.py:575
  57.3 2.2 %collective-permute-start.10 = (bf16[16,2048]{1,0:T(8,128)(2,1)S(1)}, bf16[16,2048]{1,0:T(8,128)(2,1)S(1)}, u32[]{:S(2)}, u32[]{:S(2)}) collective-permute-start(bf16[16,2048]{1,0:T(8,128)(2,1)S(1)} %get-tuple-element.31), channel_id=1, source_target_pairs={{0,192},{64,0},{128,64},{192,128},{1,193},{65,1},{129,65},{193,129... | collective-permute-start | bytes 196616 | tf_op jit(solution)/shard_map/ppermute | solution.py:575
  59.5 5.3 %collective-permute-done.9 = bf16[16,2048]{1,0:T(8,128)(2,1)S(1)} collective-permute-done((bf16[16,2048]{1,0:T(8,128)(2,1)S(1)}, bf16[16,2048]{1,0:T(8,128)(2,1)S(1)}, u32[]{:S(2)}, u32[]{:S(2)}) %collective-permute-start.9) | collective-permute-done | bytes 65568 | tf_op jit(solution)/shard_map/ppermute | solution.py:575
  66.2 5.1 %collective-permute-start.12 = (bf16[16,2048]{1,0:T(8,128)(2,1)S(1)}, bf16[16,2048]{1,0:T(8,128)(2,1)S(1)}, u32[]{:S(2)}, u32[]{:S(2)}) collective-permute-start(bf16[16,2048]{1,0:T(8,128)(2,1)S(1)} %multiply_convert_fusion), channel_id=1, source_target_pairs={{0,128},{64,192},{128,0},{192,64},{1,129},{65,193},{129,1},{193,65... | collective-permute-start | bytes 196616 | tf_op jit(solution)/shard_map/ppermute | solution.py:575
  73.4 3.7 %collective-permute-done.11 = bf16[16,2048]{1,0:T(8,128)(2,1)S(1)} collective-permute-done((bf16[16,2048]{1,0:T(8,128)(2,1)S(1)}, bf16[16,2048]{1,0:T(8,128)(2,1)S(1)}, u32[]{:S(2)}, u32[]{:S(2)}) %collective-permute-start.11) | collective-permute-done | bytes 65568 | tf_op jit(solution)/shard_map/ppermute | solution.py:575
  77.1 3.0 %collective-permute-start.16 = (bf16[4,16,2048]{2,1,0:T(8,128)(2,1)S(1)}, bf16[4,16,2048]{2,1,0:T(8,128)(2,1)S(1)}, u32[]{:S(2)}, u32[]{:S(2)}) collective-permute-start(bf16[4,16,2048]{2,1,0:T(8,128)(2,1)S(1)} %pad_maximum_fusion.w0_ref), channel_id=1, source_target_pairs={{0,48},{16,0},{32,16},{48,32},{1,49},{17,1},{33,17},{49,33},{2,50}... | collective-permute-start | bytes 786440 | tf_op jit(solution)/shard_map/ppermute | solution.py:575
  80.7 3.6 %collective-permute-start.18 = (bf16[16,2048]{1,0:T(8,128)(2,1)S(1)}, bf16[16,2048]{1,0:T(8,128)(2,1)S(1)}, u32[]{:S(2)}, u32[]{:S(2)}) collective-permute-start(bf16[16,2048]{1,0:T(8,128)(2,1)S(1)} %get-tuple-element.33), channel_id=1, source_target_pairs={{16,0},{24,8},{32,16},{40,24},{48,32},{56,40},{64,48},{72,56},{80,... | collective-permute-start | bytes 196616 | tf_op jit(solution)/shard_map/ppermute | solution.py:579
  84.4 2.1 %collective-permute-start.17 = (bf16[16,2048]{1,0:T(8,128)(2,1)S(1)}, bf16[16,2048]{1,0:T(8,128)(2,1)S(1)}, u32[]{:S(2)}, u32[]{:S(2)}) collective-permute-start(bf16[16,2048]{1,0:T(8,128)(2,1)S(1)} %get-tuple-element.33), channel_id=1, source_target_pairs={{0,16},{8,24},{16,32},{24,40},{32,48},{40,56},{48,64},{56,72},{64,... | collective-permute-start | bytes 196616 | tf_op jit(solution)/shard_map/ppermute | solution.py:579
  86.5 4.2 %collective-permute-done.18.next_ref = bf16[16,2048]{1,0:T(8,128)(2,1)S(1)} collective-permute-done((bf16[16,2048]{1,0:T(8,128)(2,1)S(1)}, bf16[16,2048]{1,0:T(8,128)(2,1)S(1)}, u32[]{:S(2)}, u32[]{:S(2)}) %collective-permute-start.18) | collective-permute-done | bytes 65568 | tf_op jit(solution)/shard_map/ppermute | solution.py:579
  90.7 1.8 %collective-permute-done.17.prev_ref = bf16[16,2048]{1,0:T(8,128)(2,1)S(1)} collective-permute-done((bf16[16,2048]{1,0:T(8,128)(2,1)S(1)}, bf16[16,2048]{1,0:T(8,128)(2,1)S(1)}, u32[]{:S(2)}, u32[]{:S(2)}) %collective-permute-start.17) | collective-permute-done | bytes 65568 | tf_op jit(solution)/shard_map/ppermute | solution.py:579
  92.5 3.0 %collective-permute-done.14.w1_ref = bf16[4,16,2048]{2,1,0:T(8,128)(2,1)S(1)} collective-permute-done((bf16[4,16,2048]{2,1,0:T(8,128)(2,1)S(1)}, bf16[4,16,2048]{2,1,0:T(8,128)(2,1)S(1)}, u32[]{:S(2)}, u32[]{:S(2)}) %collective-permute-start.14) | collective-permute-done | bytes 262176 | tf_op jit(solution)/shard_map/ppermute | solution.py:575
  95.5 3.0 %synthesise.1 = bf16[16,16,1152]{2,1,0:T(8,128)(2,1)S(1)} custom-call(s32[5]{0:T(128)S(1)} %copy-done.8, bf16[4,16,2048]{2,1,0:T(8,128)(2,1)S(1)} %pad_maximum_fusion.w0_ref, bf16[4,16,2048]{2,1,0:T(8,128)(2,1)S(1)} %collective-permute-done.14.w1_ref, bf16[4,16,2048]{2,1,0:T(8,128)(2,1)S(1)} %collective-permute-done.15.w2_ref, ...), custom_call_target="tpu_custom_call" | custom-call | tf_op jit(solution)/shard_map/synthesise/pallas_call | solution.py:312
  98.6 20.0 %all_to_all.10 = bf16[16,16,1152]{2,1,0:T(8,128)(2,1)S(1)} all-to-all(bf16[16,16,1152]{2,1,0:T(8,128)(2,1)S(1)} %synthesise.1), channel_id=1, replica_groups=mesh['zh'=4,'x'=4,'c'=2,'y'=4,'zl'=2] {'y','zl','c'}, dimensions={0} | all-to-all | bytes 1179648 | tf_op jit(solution)/shard_map/all_to_all | solution.py:587
  118.6 10.9 %sweep.1 = (f32[16,64,512]{2,1,0:T(8,128)}, f32[16,64,512]{2,1,0:T(8,128)}, f32[64,512]{1,0:T(8,128)}) custom-call(s32[5]{0:T(128)S(1)} %copy-done.8, bf16[256,1152]{1,0:T(8,128)(2,1)S(1)} %bitcast.17, bf16[528,640]{1,0:T(8,128)(2,1)S(1)} %copy-done.3, f32[16,64,512]{2,1,0:T(8,128)S(1)} %copy-done.2, f32[64,512]{1,0:T(8,128)S(1)} %copy-done.5, ...), custom_call_target="tpu_custom_call" | custom-call | tf_op jit(solution)/shard_map/sweep/pallas_call | solution.py:527
  (54 shorter events, 11.9 us)
Async XLA Ops:
  8.1 21.5 %collective-permute-start = (bf16[8,64,2048]{2,1,0:T(8,128)(2,1)}, bf16[8,64,2048]{2,1,0:T(8,128)(2,1)S(1)}, u32[]{:S(2)}, u32[]{:S(2)}) collective-permute-start(bf16[8,64,2048]{2,1,0:T(8,128)(2,1)} %get-tuple-element.20), channel_id=1, source_target_pairs={{0,8},{8,0},{1,9},{9,1},{2,10},{10,2},{3,11},{11,3},{4,12},{12,4},... | collective-permute-start | bytes 6291464 | tf_op jit(solution)/shard_map/ppermute | solution.py:575
  11.0 15.7 %all-to-all-start = ((f16[16,16,1024]{2,1,0:T(8,128)(2,1)}), f16[16,16,1024]{2,1,0:T(8,128)(2,1)S(1)}, u32[]{:S(2)}, u32[]{:S(2)}) async-start(f16[16,16,1024]{2,1,0:T(8,128)(2,1)} %convert_element_type.21), calls=%async_computation | async-start | bytes 1048576 | tf_op jit(solution)/shard_map/all_to_all | solution.py:587
  17.0 9.9 %collective-permute-start.4 = (f32[8,1152]{1,0:T(8,128)S(1)}, f32[8,1152]{1,0:T(8,128)S(1)}, u32[]{:S(2)}, u32[]{:S(2)}) collective-permute-start(f32[8,1152]{1,0:T(8,128)S(1)} %copy-done.12), channel_id=1, source_target_pairs={{0,7},{1,0},{2,1},{3,2},{4,3},{5,4},{6,5},{7,6},{8,15},{9,8},{10,9... | collective-permute-start | bytes 110600 | tf_op jit(solution)/shard_map/ppermute | solution.py:575
  20.5 7.8 %collective-permute-start.3 = (f32[8,1152]{1,0:T(8,128)S(1)}, f32[8,1152]{1,0:T(8,128)S(1)}, u32[]{:S(2)}, u32[]{:S(2)}) collective-permute-start(f32[8,1152]{1,0:T(8,128)S(1)} %copy-done.12), channel_id=1, source_target_pairs={{0,1},{1,2},{2,3},{3,4},{4,5},{5,6},{6,7},{7,0},{8,9},{9,10},{10,1... | collective-permute-start | bytes 110600 | tf_op jit(solution)/shard_map/ppermute | solution.py:575
  20.5 7.8 %collective-permute-start.1 = (f32[24,512]{1,0:T(8,128)S(1)}, f32[24,512]{1,0:T(8,128)S(1)}, u32[]{:S(2)}, u32[]{:S(2)}) collective-permute-start(f32[24,512]{1,0:T(8,128)S(1)} %copy-done.11), channel_id=1, source_target_pairs={{0,8},{8,16},{16,24},{24,32},{32,40},{40,48},{48,56},{56,64},{64,7... | collective-permute-start | bytes 147464 | tf_op jit(solution)/shard_map/ppermute | solution.py:579
  24.2 5.4 %collective-permute-start.2 = (f32[24,512]{1,0:T(8,128)S(1)}, f32[24,512]{1,0:T(8,128)S(1)}, u32[]{:S(2)}, u32[]{:S(2)}) collective-permute-start(f32[24,512]{1,0:T(8,128)S(1)} %copy-done.10), channel_id=1, source_target_pairs={{8,0},{16,8},{24,16},{32,24},{40,32},{48,40},{56,48},{64,56},{72,6... | collective-permute-start | bytes 147464 | tf_op jit(solution)/shard_map/ppermute | solution.py:579
  26.8 38.0 %copy-start.9 = (f32[2048]{0:T(1024)S(1)}, f32[2048]{0:T(1024)}, u32[]{:S(2)}) copy-start(f32[2048]{0:T(1024)} %param.14) | copy-start | bytes 24580
  31.8 63.7 %copy-start.1 = (bf16[16,64,2048]{2,1,0:T(8,128)(2,1)S(1)}, bf16[16,64,2048]{2,1,0:T(8,128)(2,1)}, u32[]{:S(2)}) copy-start(bf16[16,64,2048]{2,1,0:T(8,128)(2,1)} %own_ref.3) | copy-start | bytes 12582916
  34.7 17.7 %collective-permute-start.5 = (bf16[2,32,2048]{2,1,0:T(8,128)(2,1)S(1)}, bf16[2,32,2048]{2,1,0:T(8,128)(2,1)S(1)}, u32[]{:S(2)}, u32[]{:S(2)}) collective-permute-start(bf16[2,32,2048]{2,1,0:T(8,128)(2,1)S(1)} %get-tuple-element.25), channel_id=1, source_target_pairs={{0,16},{16,32},{32,48},{48,0},{1,17},{17,33},{33,49},{49,1},{2,18}... | collective-permute-start | bytes 786440 | tf_op jit(solution)/shard_map/ppermute | solution.py:575
  35.9 16.4 %collective-permute-start.6 = (bf16[2,32,2048]{2,1,0:T(8,128)(2,1)S(1)}, bf16[2,32,2048]{2,1,0:T(8,128)(2,1)S(1)}, u32[]{:S(2)}, u32[]{:S(2)}) collective-permute-start(bf16[2,32,2048]{2,1,0:T(8,128)(2,1)S(1)} %get-tuple-element.26), channel_id=1, source_target_pairs={{0,32},{16,48},{32,0},{48,16},{1,33},{17,49},{33,1},{49,17},{2,34}... | collective-permute-start | bytes 786440 | tf_op jit(solution)/shard_map/ppermute | solution.py:575
  45.1 8.1 %collective-permute-start.7 = (bf16[2,32,2048]{2,1,0:T(8,128)(2,1)S(1)}, bf16[2,32,2048]{2,1,0:T(8,128)(2,1)S(1)}, u32[]{:S(2)}, u32[]{:S(2)}) collective-permute-start(bf16[2,32,2048]{2,1,0:T(8,128)(2,1)S(1)} %get-tuple-element.27), channel_id=1, source_target_pairs={{0,48},{16,0},{32,16},{48,32},{1,49},{17,1},{33,17},{49,33},{2,50}... | collective-permute-start | bytes 786440 | tf_op jit(solution)/shard_map/ppermute | solution.py:575
  53.9 5.6 %collective-permute-start.8 = (bf16[16,2048]{1,0:T(8,128)(2,1)S(1)}, bf16[16,2048]{1,0:T(8,128)(2,1)S(1)}, u32[]{:S(2)}, u32[]{:S(2)}) collective-permute-start(bf16[16,2048]{1,0:T(8,128)(2,1)S(1)} %get-tuple-element.29), channel_id=1, source_target_pairs={{0,64},{64,128},{128,192},{192,0},{1,65},{65,129},{129,193},{193,1... | collective-permute-start | bytes 196616 | tf_op jit(solution)/shard_map/ppermute | solution.py:575
  57.3 7.5 %collective-permute-start.9 = (bf16[16,2048]{1,0:T(8,128)(2,1)S(1)}, bf16[16,2048]{1,0:T(8,128)(2,1)S(1)}, u32[]{:S(2)}, u32[]{:S(2)}) collective-permute-start(bf16[16,2048]{1,0:T(8,128)(2,1)S(1)} %get-tuple-element.30), channel_id=1, source_target_pairs={{0,128},{64,192},{128,0},{192,64},{1,129},{65,193},{129,1},{193,65... | collective-permute-start | bytes 196616 | tf_op jit(solution)/shard_map/ppermute | solution.py:575
  57.3 7.5 %collective-permute-start.10 = (bf16[16,2048]{1,0:T(8,128)(2,1)S(1)}, bf16[16,2048]{1,0:T(8,128)(2,1)S(1)}, u32[]{:S(2)}, u32[]{:S(2)}) collective-permute-start(bf16[16,2048]{1,0:T(8,128)(2,1)S(1)} %get-tuple-element.31), channel_id=1, source_target_pairs={{0,192},{64,0},{128,64},{192,128},{1,193},{65,1},{129,65},{193,129... | collective-permute-start | bytes 196616 | tf_op jit(solution)/shard_map/ppermute | solution.py:575
  64.9 7.1 %collective-permute-start.13 = (bf16[16,2048]{1,0:T(8,128)(2,1)S(1)}, bf16[16,2048]{1,0:T(8,128)(2,1)S(1)}, u32[]{:S(2)}, u32[]{:S(2)}) collective-permute-start(bf16[16,2048]{1,0:T(8,128)(2,1)S(1)} %multiply_convert_fusion), channel_id=1, source_target_pairs={{0,192},{64,0},{128,64},{192,128},{1,193},{65,1},{129,65},{193,129... | collective-permute-start | bytes 196616 | tf_op jit(solution)/shard_map/ppermute | solution.py:575
  66.2 7.1 %collective-permute-start.12 = (bf16[16,2048]{1,0:T(8,128)(2,1)S(1)}, bf16[16,2048]{1,0:T(8,128)(2,1)S(1)}, u32[]{:S(2)}, u32[]{:S(2)}) collective-permute-start(bf16[16,2048]{1,0:T(8,128)(2,1)S(1)} %multiply_convert_fusion), channel_id=1, source_target_pairs={{0,128},{64,192},{128,0},{192,64},{1,129},{65,193},{129,1},{193,65... | collective-permute-start | bytes 196616 | tf_op jit(solution)/shard_map/ppermute | solution.py:575
  71.4 5.7 %collective-permute-start.11 = (bf16[16,2048]{1,0:T(8,128)(2,1)S(1)}, bf16[16,2048]{1,0:T(8,128)(2,1)S(1)}, u32[]{:S(2)}, u32[]{:S(2)}) collective-permute-start(bf16[16,2048]{1,0:T(8,128)(2,1)S(1)} %multiply_convert_fusion), channel_id=1, source_target_pairs={{0,64},{64,128},{128,192},{192,0},{1,65},{65,129},{129,193},{193,1... | collective-permute-start | bytes 196616 | tf_op jit(solution)/shard_map/ppermute | solution.py:575
  77.1 15.4 %collective-permute-start.16 = (bf16[4,16,2048]{2,1,0:T(8,128)(2,1)S(1)}, bf16[4,16,2048]{2,1,0:T(8,128)(2,1)S(1)}, u32[]{:S(2)}, u32[]{:S(2)}) collective-permute-start(bf16[4,16,2048]{2,1,0:T(8,128)(2,1)S(1)} %pad_maximum_fusion.w0_ref), channel_id=1, source_target_pairs={{0,48},{16,0},{32,16},{48,32},{1,49},{17,1},{33,17},{49,33},{2,50}... | collective-permute-start | bytes 786440 | tf_op jit(solution)/shard_map/ppermute | solution.py:575
  80.1 12.4 %collective-permute-start.15 = (bf16[4,16,2048]{2,1,0:T(8,128)(2,1)S(1)}, bf16[4,16,2048]{2,1,0:T(8,128)(2,1)S(1)}, u32[]{:S(2)}, u32[]{:S(2)}) collective-permute-start(bf16[4,16,2048]{2,1,0:T(8,128)(2,1)S(1)} %pad_maximum_fusion.w0_ref), channel_id=1, source_target_pairs={{0,32},{16,48},{32,0},{48,16},{1,33},{17,49},{33,1},{49,17},{2,34}... | collective-permute-start | bytes 786440 | tf_op jit(solution)/shard_map/ppermute | solution.py:575
  80.1 15.4 %collective-permute-start.14 = (bf16[4,16,2048]{2,1,0:T(8,128)(2,1)S(1)}, bf16[4,16,2048]{2,1,0:T(8,128)(2,1)S(1)}, u32[]{:S(2)}, u32[]{:S(2)}) collective-permute-start(bf16[4,16,2048]{2,1,0:T(8,128)(2,1)S(1)} %pad_maximum_fusion.w0_ref), channel_id=1, source_target_pairs={{0,16},{16,32},{32,48},{48,0},{1,17},{17,33},{33,49},{49,1},{2,18}... | collective-permute-start | bytes 786440 | tf_op jit(solution)/shard_map/ppermute | solution.py:575
  80.7 10.0 %collective-permute-start.18 = (bf16[16,2048]{1,0:T(8,128)(2,1)S(1)}, bf16[16,2048]{1,0:T(8,128)(2,1)S(1)}, u32[]{:S(2)}, u32[]{:S(2)}) collective-permute-start(bf16[16,2048]{1,0:T(8,128)(2,1)S(1)} %get-tuple-element.33), channel_id=1, source_target_pairs={{16,0},{24,8},{32,16},{40,24},{48,32},{56,40},{64,48},{72,56},{80,... | collective-permute-start | bytes 196616 | tf_op jit(solution)/shard_map/ppermute | solution.py:579
  84.4 8.1 %collective-permute-start.17 = (bf16[16,2048]{1,0:T(8,128)(2,1)S(1)}, bf16[16,2048]{1,0:T(8,128)(2,1)S(1)}, u32[]{:S(2)}, u32[]{:S(2)}) collective-permute-start(bf16[16,2048]{1,0:T(8,128)(2,1)S(1)} %get-tuple-element.33), channel_id=1, source_target_pairs={{0,16},{8,24},{16,32},{24,40},{32,48},{40,56},{48,64},{56,72},{64,... | collective-permute-start | bytes 196616 | tf_op jit(solution)/shard_map/ppermute | solution.py:579
  95.5 23.1 %copy-start.3 = (bf16[528,640]{1,0:T(8,128)(2,1)S(1)}, bf16[528,640]{1,0:T(8,128)(2,1)}, u32[]{:S(2)}) copy-start(bf16[528,640]{1,0:T(8,128)(2,1)} %get-tuple-element.34.harm_ref) | copy-start | bytes 2027524
  95.5 23.1 %copy-start.4 = (s32[64,512]{1,0:T(8,128)S(1)}, s32[64,512]{1,0:T(8,128)}, u32[]{:S(2)}) copy-start(s32[64,512]{1,0:T(8,128)} %mask_ref.3) | copy-start | bytes 393220
  (9 other events, 153.3 us)

commit v4 on v3

--- a/solution.py
+++ b/solution.py
@@ -422,89 +422,94 @@
                 nf[2 * k, lo : lo + 8, :] = rc * dr - ic * di
                 nf[2 * k + 1, lo : lo + 8, :] = rc * di + ic * dr
 
-    base = pl.multiple_of(8 * b, 8)
-    own = pl.ds(base + 8, 8)
-    row = (lat0 + base).astype(F32) + lax.broadcasted_iota(jnp.int32, (8, 128), 0).astype(F32)
-    phi = lat_of(row + 0.5)
-    rcos1 = 1.0 / jnp.cos(phi)
-    rcos = jnp.tile(rcos1, (1, 4))
-    lane = lax.broadcasted_iota(jnp.int32, (8, COLS), 1)
-    last = lane == COLS - 1
-    first = lane == 0
-    tile_lane = lax.broadcasted_iota(jnp.int32, (8, 128), 1)
-    col = idx[1] * COLS + jnp.where(tile_lane < 64, -1, COLS)
-    c1, s1 = unit_circle(col)
-    c2, s2 = unit_circle(2 * col)
-    waves = (c2, s2, c1, s1)
-    cosphi = jnp.cos(phi)
-    sq, s2phi = cosphi * cosphi, jnp.sin(2.0 * phi)
-
-    def east_of(x, halo):
-        wide = jnp.tile(halo, (1, 4))
-        return jnp.where(last, wide, pltpu.roll(x, COLS - 1, 1))
-
-    d = dpad[own, :]
-    f = fpad[own, :]
-    dh = lonh_all[16, pl.ds(base, 8), :]
-    fh = lonh_all[17, pl.ds(base, 8), :]
-    hh = d * east_of(d, dh)
-    h = jnp.sqrt(hh)
-    r = 0.5 * (f + east_of(f, fh))
-    hhw = d[:, :128] * dh
-    hw = jnp.sqrt(hhw)
-    rw = 0.5 * (f[:, :128] + fh)
-    mask = mask_ref[pl.ds(base, 8), :].astype(F32)
-    ecell, ncell = [], []
-    for k in range(8):
-        om = FREQUENCIES[k]
-        inv = -hh / (r * r + (om * om) * hh)
-        rc = inv * r * rcos
-        ic = inv * h * om * rcos
-        invw = -hhw / (rw * rw + (om * om) * hhw)
-        rcw = invw * rw * rcos1
-        icw = invw * hw * om * rcos1
-        diffs, wdiffs = [], []
-        for ch in (2 * k, 2 * k + 1):
-            s = spad[ch, own, :]
-            eq = EQ_AMPS[k] * (sq if k < 4 else s2phi) * waves[(0 if k < 4 else 2) + ch % 2]
-            sh = lonh_all[ch, pl.ds(base, 8), :] - eq
-            diffs.append(east_of(s, sh) - s)
-            wdiffs.append(s[:, :128] - sh)
-        flux = (rc * diffs[0] - ic * diffs[1], rc * diffs[1] + ic * diffs[0])
-        fluxw = (rcw * wdiffs[0] - icw * wdiffs[1], rcw * wdiffs[1] + icw * wdiffs[0])
-        div = []
-        for p in range(2):
-            ch = 2 * k + p
-            west = jnp.where(first, jnp.tile(fluxw[p], (1, 4)), pltpu.roll(flux[p], 1, 1))
-            south = nf[ch, pl.ds(base, 8), :]
-            below = nf[ch, pl.ds(base + 8, 8), :]
-            sub = lax.broadcasted_iota(jnp.int32, (8, COLS), 0)
-            north = pltpu.roll(jnp.where(sub == 0, below, south), 7, 0)
-            div.append((flux[p] - west + (north - south)) * rcos)
-            ecell.append(0.5 * (flux[p] + west))
-            ncell.append(0.5 * (north + south))
-        cr = elev_ref[2 * k, pl.ds(base, 8), :]
-        ci = elev_ref[2 * k + 1, pl.ds(base, 8), :]
-        new_ref[2 * k] = (cr - RELAX_RATE * (div[0] + om * ci)) * mask
-        new_ref[2 * k + 1] = (ci - RELAX_RATE * (div[1] - om * cr)) * mask
-
-    def stacked(parts):
-        hi, lo = split(jnp.concatenate(parts, axis=0))
-        return jnp.concatenate([hi, lo], axis=0)
-
-    xe, xn = stacked(ecell), stacked(ncell)
-    total = jnp.zeros((8, COLS), F32)
-    for q in range(4):
-        w = w_ref[128 * q : 128 * q + 128, :]
-        u = jnp.dot(w, xe, preferred_element_type=F32)
-        v = jnp.dot(w, xn, preferred_element_type=F32)
-        x = u * u + v * v + SPEED_EPS * SPEED_EPS
-        speed = x * lax.rsqrt(x)
-        for s in range(16):
-            total = total + speed[8 * s : 8 * s + 8, :]
-    fnew_ref[...] = BASE_FRICTION + DRAG_COEFF * total / SAMPLES
-
-    @pl.when(b == 7)
+    def sweep_rows(sub_block):
+        out = slice(8 * sub_block, 8 * sub_block + 8)
+        base = pl.multiple_of(8 * (2 * b + sub_block), 8)
+        own = pl.ds(base + 8, 8)
+        row = (lat0 + base).astype(F32) + lax.broadcasted_iota(jnp.int32, (8, 128), 0).astype(F32)
+        phi = lat_of(row + 0.5)
+        rcos1 = 1.0 / jnp.cos(phi)
+        rcos = jnp.tile(rcos1, (1, 4))
+        lane = lax.broadcasted_iota(jnp.int32, (8, COLS), 1)
+        last = lane == COLS - 1
+        first = lane == 0
+        tile_lane = lax.broadcasted_iota(jnp.int32, (8, 128), 1)
+        col = idx[1] * COLS + jnp.where(tile_lane < 64, -1, COLS)
+        c1, s1 = unit_circle(col)
+        c2, s2 = unit_circle(2 * col)
+        waves = (c2, s2, c1, s1)
+        cosphi = jnp.cos(phi)
+        sq, s2phi = cosphi * cosphi, jnp.sin(2.0 * phi)
+
+        def east_of(x, halo):
+            wide = jnp.tile(halo, (1, 4))
+            return jnp.where(last, wide, pltpu.roll(x, COLS - 1, 1))
+
+        d = dpad[own, :]
+        f = fpad[own, :]
+        dh = lonh_all[16, pl.ds(base, 8), :]
+        fh = lonh_all[17, pl.ds(base, 8), :]
+        hh = d * east_of(d, dh)
+        h = jnp.sqrt(hh)
+        r = 0.5 * (f + east_of(f, fh))
+        hhw = d[:, :128] * dh
+        hw = jnp.sqrt(hhw)
+        rw = 0.5 * (f[:, :128] + fh)
+        mask = mask_ref[pl.ds(base, 8), :].astype(F32)
+        ecell, ncell = [], []
+        for k in range(8):
+            om = FREQUENCIES[k]
+            inv = -hh / (r * r + (om * om) * hh)
+            rc = inv * r * rcos
+            ic = inv * h * om * rcos
+            invw = -hhw / (rw * rw + (om * om) * hhw)
+            rcw = invw * rw * rcos1
+            icw = invw * hw * om * rcos1
+            diffs, wdiffs = [], []
+            for ch in (2 * k, 2 * k + 1):
+                s = spad[ch, own, :]
+                eq = EQ_AMPS[k] * (sq if k < 4 else s2phi) * waves[(0 if k < 4 else 2) + ch % 2]
+                sh = lonh_all[ch, pl.ds(base, 8), :] - eq
+                diffs.append(east_of(s, sh) - s)
+                wdiffs.append(s[:, :128] - sh)
+            flux = (rc * diffs[0] - ic * diffs[1], rc * diffs[1] + ic * diffs[0])
+            fluxw = (rcw * wdiffs[0] - icw * wdiffs[1], rcw * wdiffs[1] + icw * wdiffs[0])
+            div = []
+            for p in range(2):
+                ch = 2 * k + p
+                west = jnp.where(first, jnp.tile(fluxw[p], (1, 4)), pltpu.roll(flux[p], 1, 1))
+                south = nf[ch, pl.ds(base, 8), :]
+                below = nf[ch, pl.ds(base + 8, 8), :]
+                sub = lax.broadcasted_iota(jnp.int32, (8, COLS), 0)
+                north = pltpu.roll(jnp.where(sub == 0, below, south), 7, 0)
+                div.append((flux[p] - west + (north - south)) * rcos)
+                ecell.append(0.5 * (flux[p] + west))
+                ncell.append(0.5 * (north + south))
+            cr = elev_ref[2 * k, pl.ds(base, 8), :]
+            ci = elev_ref[2 * k + 1, pl.ds(base, 8), :]
+            new_ref[2 * k, out] = (cr - RELAX_RATE * (div[0] + om * ci)) * mask
+            new_ref[2 * k + 1, out] = (ci - RELAX_RATE * (div[1] - om * cr)) * mask
+
+        def stacked(parts):
+            hi, lo = split(jnp.concatenate(parts, axis=0))
+            return jnp.concatenate([hi, lo], axis=0)
+
+        xe, xn = stacked(ecell), stacked(ncell)
+        total = jnp.zeros((8, COLS), F32)
+        for q in range(4):
+            w = w_ref[128 * q : 128 * q + 128, :]
+            u = jnp.dot(w, xe, preferred_element_type=F32)
+            v = jnp.dot(w, xn, preferred_element_type=F32)
+            x = u * u + v * v + SPEED_EPS * SPEED_EPS
+            speed = x * lax.rsqrt(x)
+            for s in range(16):
+                total = total + speed[8 * s : 8 * s + 8, :]
+        fnew_ref[out, :] = BASE_FRICTION + DRAG_COEFF * total / SAMPLES
+
+    for sub_block in range(2):
+        sweep_rows(sub_block)
+
+    @pl.when(b == 3)
     def _():
         for c in range(4):
             send(c).wait()
@@ -528,7 +533,7 @@
         sweep_kernel,
         grid_spec=pltpu.PrefetchScalarGridSpec(
             num_scalar_prefetch=1,
-            grid=(8,),
+            grid=(4,),
             in_specs=[
                 whole((256, 1152)),
                 whole((528, COLS + 128)),
@@ -543,9 +548,9 @@
                 whole((512, 256)),
             ],
             out_specs=[
-                pl.BlockSpec((CH, 8, COLS), lambda i, x: (0, i, 0)),
+                pl.BlockSpec((CH, 16, COLS), lambda i, x: (0, i, 0)),
                 pl.BlockSpec(memory_space=pl.ANY),
-                pl.BlockSpec((8, COLS), lambda i, x: (i, 0)),
+                pl.BlockSpec((16, COLS), lambda i, x: (i, 0)),
             ],
             scratch_shapes=[
                 pltpu.VMEM((CH, 80, COLS), F32),

time: 130 us -> 129 us (level)
  no operation moved by 1% of the time
where the time goes in v4:
time: 129 us
  starting transfers between devices  48.4 us (38%)
  waiting for transfers between devices  30.8 us (24%)
  Pallas kernels  23.6 us (18%)
  blocking collectives  20 us (16%)
  local copies, waits for them, and re-layouts  2.9 us (2%)
  other arithmetic  2.29 us (2%)
    ppermute x15, starting transfers between devices, shift(): lax.ppermute(value, axes, [(i, (i + step) % size) for i in range(size)])  31.1 us
    ppermute x15, waiting for transfers between devices, shift(): lax.ppermute(value, axes, [(i, (i + step) % size) for i in range(size)])  23 us
    all_to_all x1, blocking collectives, swap(): return lax.all_to_all(x, axis, 0, 0, tiled=True)  20 us
    ppermute x4, starting transfers between devices, shift_lat(): lax.ppermute(value, LAT, [(i, i + step) for i in range(32) if 0 <= i + st...  11.3 us
    pallas_call x1, Pallas kernels, sweep(): pl.pallas_call(sweep_kernel, grid_spec=pltpu.PrefetchScalarGridSpec(num_s...  10.3 us
    ppermute x4, waiting for transfers between devices, shift_lat(): lax.ppermute(value, LAT, [(i, i + step) for i in range(32) if 0 <= i + st...  7.2 us
    pallas_call x1, Pallas kernels, dft(): pl.pallas_call(dft_kernel, grid_spec=pltpu.PrefetchScalarGridSpec(num_sca...  6.79 us
    all_to_all x1, starting transfers between devices, swap(): return lax.all_to_all(x, axis, 0, 0, tiled=True)  5.95 us
  transfers between devices with their start and end apart: 20, of which 11 were waited for; matrix products, arithmetic and copies ran while one was open for 2% of the time, Pallas kernels for 0%

profile of v4, /device:TPU:65, one launch (start us, length us, event | category | flops | bytes accessed | tf_op | source)
XLA Modules:
  0.0 129.0 jit_solution(11389643885332594006)
XLA Ops:
  1.3 6.8 %dft.1 = (f32[16,16,1024]{2,1,0:T(8,128)}, bf16[528,640]{1,0:T(8,128)(2,1)}, bf16[8,64,2048]{2,1,0:T(8,128)(2,1)}, f32[24,512]{1,0:T(8,128)}, f32[24,512]{1,0:T(8,128)}, /*index=5*/f32[8,1152]{1,0:T(8,128)}) custom-call(s32[5]{0:T(128)} %stack.38.idx, s32[1,128]{1,0:T(1,128)} %bitcast.27, f32[16,64,512]{2,1,0:T(8,128)} %elev_ref.3, s32[64,512]{1,0:T(8,128)} %mask_ref.3, ...), custom_call_target="tpu_custom_call" | custom-call | tf_op jit(solution)/shard_map/dft/pallas_call | solution.py:117
  8.9 2.1 %convert_element_type.21 = f16[16,16,1024]{2,1,0:T(8,128)(2,1)} convert(f32[16,16,1024]{2,1,0:T(8,128)} %get-tuple-element.19) | non-fusion elementwise | flops 262144 | bytes 1572864 | tf_op jit(solution)/shard_map/convert_element_type | solution.py:605
  11.0 5.9 %all-to-all-start = ((f16[16,16,1024]{2,1,0:T(8,128)(2,1)}), f16[16,16,1024]{2,1,0:T(8,128)(2,1)S(1)}, u32[]{:S(2)}, u32[]{:S(2)}) async-start(f16[16,16,1024]{2,1,0:T(8,128)(2,1)} %convert_element_type.21), calls=%async_computation | async-start | bytes 1048576 | tf_op jit(solution)/shard_map/all_to_all | solution.py:592
  17.0 3.6 %collective-permute-start.4 = (f32[8,1152]{1,0:T(8,128)S(1)}, f32[8,1152]{1,0:T(8,128)S(1)}, u32[]{:S(2)}, u32[]{:S(2)}) collective-permute-start(f32[8,1152]{1,0:T(8,128)S(1)} %copy-done.12), channel_id=1, source_target_pairs={{0,7},{1,0},{2,1},{3,2},{4,3},{5,4},{6,5},{7,6},{8,15},{9,8},{10,9... | collective-permute-start | bytes 110600 | tf_op jit(solution)/shard_map/ppermute | solution.py:580
  20.5 3.6 %collective-permute-start.1 = (f32[24,512]{1,0:T(8,128)S(1)}, f32[24,512]{1,0:T(8,128)S(1)}, u32[]{:S(2)}, u32[]{:S(2)}) collective-permute-start(f32[24,512]{1,0:T(8,128)S(1)} %copy-done.11), channel_id=1, source_target_pairs={{0,8},{8,16},{16,24},{24,32},{32,40},{40,48},{48,56},{56,64},{64,7... | collective-permute-start | bytes 147464 | tf_op jit(solution)/shard_map/ppermute | solution.py:584
  24.2 1.9 %collective-permute-start.2 = (f32[24,512]{1,0:T(8,128)S(1)}, f32[24,512]{1,0:T(8,128)S(1)}, u32[]{:S(2)}, u32[]{:S(2)}) collective-permute-start(f32[24,512]{1,0:T(8,128)S(1)} %copy-done.10), channel_id=1, source_target_pairs={{8,0},{16,8},{24,16},{32,24},{40,32},{48,40},{56,48},{64,56},{72,6... | collective-permute-start | bytes 147464 | tf_op jit(solution)/shard_map/ppermute | solution.py:584
  29.6 2.2 %copy-done = bf16[16,64,2048]{2,1,0:T(8,128)(2,1)S(1)} copy-done((bf16[16,64,2048]{2,1,0:T(8,128)(2,1)S(1)}, bf16[16,64,2048]{2,1,0:T(8,128)(2,1)}, u32[]{:S(2)}) %copy-start) | copy-done | bytes 4194328
  31.8 2.8 %analyse.1 = (f32[2,32,2048]{2,1,0:T(8,128)S(1)}, bf16[2,32,2048]{2,1,0:T(8,128)(2,1)S(1)}, bf16[2,32,2048]{2,1,0:T(8,128)(2,1)S(1)}, bf16[2,32,2048]{2,1,0:T(8,...) custom-call(s32[5]{0:T(128)S(1)} %copy-done.8, ...), custom_call_target="tpu_custom_call" | custom-call | tf_op jit(solution)/shard_map/analyse/pallas_call | solution.py:196
  35.9 9.2 %collective-permute-start.6 = (bf16[2,32,2048]{2,1,0:T(8,128)(2,1)S(1)}, bf16[2,32,2048]{2,1,0:T(8,128)(2,1)S(1)}, u32[]{:S(2)}, u32[]{:S(2)}) collective-permute-start(bf16[2,32,2048]{2,1,0:T(8,128)(2,1)S(1)} %get-tuple-element.26), channel_id=1, source_target_pairs={{0,32},{16,48},{32,0},{48,16},{1,33},{17,49},{33,1},{49,17},{2,34}... | collective-permute-start | bytes 786440 | tf_op jit(solution)/shard_map/ppermute | solution.py:580
  45.1 7.2 %collective-permute-done.5 = bf16[2,32,2048]{2,1,0:T(8,128)(2,1)S(1)} collective-permute-done((bf16[2,32,2048]{2,1,0:T(8,128)(2,1)S(1)}, bf16[2,32,2048]{2,1,0:T(8,128)(2,1)S(1)}, u32[]{:S(2)}, u32[]{:S(2)}) %collective-permute-start.5) | collective-permute-done | bytes 262176 | tf_op jit(solution)/shard_map/ppermute | solution.py:580
  53.9 3.4 %collective-permute-start.8 = (bf16[16,2048]{1,0:T(8,128)(2,1)S(1)}, bf16[16,2048]{1,0:T(8,128)(2,1)S(1)}, u32[]{:S(2)}, u32[]{:S(2)}) collective-permute-start(bf16[16,2048]{1,0:T(8,128)(2,1)S(1)} %get-tuple-element.29), channel_id=1, source_target_pairs={{0,64},{64,128},{128,192},{192,0},{1,65},{65,129},{129,193},{193,1... | collective-permute-start | bytes 196616 | tf_op jit(solution)/shard_map/ppermute | solution.py:580
  57.3 2.2 %collective-permute-start.10 = (bf16[16,2048]{1,0:T(8,128)(2,1)S(1)}, bf16[16,2048]{1,0:T(8,128)(2,1)S(1)}, u32[]{:S(2)}, u32[]{:S(2)}) collective-permute-start(bf16[16,2048]{1,0:T(8,128)(2,1)S(1)} %get-tuple-element.31), channel_id=1, source_target_pairs={{0,192},{64,0},{128,64},{192,128},{1,193},{65,1},{129,65},{193,129... | collective-permute-start | bytes 196616 | tf_op jit(solution)/shard_map/ppermute | solution.py:580
  59.5 5.3 %collective-permute-done.9 = bf16[16,2048]{1,0:T(8,128)(2,1)S(1)} collective-permute-done((bf16[16,2048]{1,0:T(8,128)(2,1)S(1)}, bf16[16,2048]{1,0:T(8,128)(2,1)S(1)}, u32[]{:S(2)}, u32[]{:S(2)}) %collective-permute-start.9) | collective-permute-done | bytes 65568 | tf_op jit(solution)/shard_map/ppermute | solution.py:580
  66.2 5.1 %collective-permute-start.12 = (bf16[16,2048]{1,0:T(8,128)(2,1)S(1)}, bf16[16,2048]{1,0:T(8,128)(2,1)S(1)}, u32[]{:S(2)}, u32[]{:S(2)}) collective-permute-start(bf16[16,2048]{1,0:T(8,128)(2,1)S(1)} %multiply_convert_fusion), channel_id=1, source_target_pairs={{0,128},{64,192},{128,0},{192,64},{1,129},{65,193},{129,1},{193,65... | collective-permute-start | bytes 196616 | tf_op jit(solution)/shard_map/ppermute | solution.py:580
  73.4 3.7 %collective-permute-done.11 = bf16[16,2048]{1,0:T(8,128)(2,1)S(1)} collective-permute-done((bf16[16,2048]{1,0:T(8,128)(2,1)S(1)}, bf16[16,2048]{1,0:T(8,128)(2,1)S(1)}, u32[]{:S(2)}, u32[]{:S(2)}) %collective-permute-start.11) | collective-permute-done | bytes 65568 | tf_op jit(solution)/shard_map/ppermute | solution.py:580
  77.1 3.0 %collective-permute-start.16 = (bf16[4,16,2048]{2,1,0:T(8,128)(2,1)S(1)}, bf16[4,16,2048]{2,1,0:T(8,128)(2,1)S(1)}, u32[]{:S(2)}, u32[]{:S(2)}) collective-permute-start(bf16[4,16,2048]{2,1,0:T(8,128)(2,1)S(1)} %pad_maximum_fusion.w0_ref), channel_id=1, source_target_pairs={{0,48},{16,0},{32,16},{48,32},{1,49},{17,1},{33,17},{49,33},{2,50}... | collective-permute-start | bytes 786440 | tf_op jit(solution)/shard_map/ppermute | solution.py:580
  80.7 3.6 %collective-permute-start.18 = (bf16[16,2048]{1,0:T(8,128)(2,1)S(1)}, bf16[16,2048]{1,0:T(8,128)(2,1)S(1)}, u32[]{:S(2)}, u32[]{:S(2)}) collective-permute-start(bf16[16,2048]{1,0:T(8,128)(2,1)S(1)} %get-tuple-element.33), channel_id=1, source_target_pairs={{16,0},{24,8},{32,16},{40,24},{48,32},{56,40},{64,48},{72,56},{80,... | collective-permute-start | bytes 196616 | tf_op jit(solution)/shard_map/ppermute | solution.py:584
  84.4 2.1 %collective-permute-start.17 = (bf16[16,2048]{1,0:T(8,128)(2,1)S(1)}, bf16[16,2048]{1,0:T(8,128)(2,1)S(1)}, u32[]{:S(2)}, u32[]{:S(2)}) collective-permute-start(bf16[16,2048]{1,0:T(8,128)(2,1)S(1)} %get-tuple-element.33), channel_id=1, source_target_pairs={{0,16},{8,24},{16,32},{24,40},{32,48},{40,56},{48,64},{56,72},{64,... | collective-permute-start | bytes 196616 | tf_op jit(solution)/shard_map/ppermute | solution.py:584
  86.5 4.2 %collective-permute-done.18.next_ref = bf16[16,2048]{1,0:T(8,128)(2,1)S(1)} collective-permute-done((bf16[16,2048]{1,0:T(8,128)(2,1)S(1)}, bf16[16,2048]{1,0:T(8,128)(2,1)S(1)}, u32[]{:S(2)}, u32[]{:S(2)}) %collective-permute-start.18) | collective-permute-done | bytes 65568 | tf_op jit(solution)/shard_map/ppermute | solution.py:584
  90.7 1.8 %collective-permute-done.17.prev_ref = bf16[16,2048]{1,0:T(8,128)(2,1)S(1)} collective-permute-done((bf16[16,2048]{1,0:T(8,128)(2,1)S(1)}, bf16[16,2048]{1,0:T(8,128)(2,1)S(1)}, u32[]{:S(2)}, u32[]{:S(2)}) %collective-permute-start.17) | collective-permute-done | bytes 65568 | tf_op jit(solution)/shard_map/ppermute | solution.py:584
  92.5 3.0 %collective-permute-done.14.w1_ref = bf16[4,16,2048]{2,1,0:T(8,128)(2,1)S(1)} collective-permute-done((bf16[4,16,2048]{2,1,0:T(8,128)(2,1)S(1)}, bf16[4,16,2048]{2,1,0:T(8,128)(2,1)S(1)}, u32[]{:S(2)}, u32[]{:S(2)}) %collective-permute-start.14) | collective-permute-done | bytes 262176 | tf_op jit(solution)/shard_map/ppermute | solution.py:580
  95.5 3.0 %synthesise.1 = bf16[16,16,1152]{2,1,0:T(8,128)(2,1)S(1)} custom-call(s32[5]{0:T(128)S(1)} %copy-done.8, bf16[4,16,2048]{2,1,0:T(8,128)(2,1)S(1)} %pad_maximum_fusion.w0_ref, bf16[4,16,2048]{2,1,0:T(8,128)(2,1)S(1)} %collective-permute-done.14.w1_ref, bf16[4,16,2048]{2,1,0:T(8,128)(2,1)S(1)} %collective-permute-done.15.w2_ref, ...), custom_call_target="tpu_custom_call" | custom-call | tf_op jit(solution)/shard_map/synthesise/pallas_call | solution.py:312
  98.6 20.0 %all_to_all.10 = bf16[16,16,1152]{2,1,0:T(8,128)(2,1)S(1)} all-to-all(bf16[16,16,1152]{2,1,0:T(8,128)(2,1)S(1)} %synthesise.1), channel_id=1, replica_groups=mesh['zh'=4,'x'=4,'c'=2,'y'=4,'zl'=2] {'y','zl','c'}, dimensions={0} | all-to-all | bytes 1179648 | tf_op jit(solution)/shard_map/all_to_all | solution.py:592
  118.6 10.3 %sweep.1 = (f32[16,64,512]{2,1,0:T(8,128)}, f32[16,64,512]{2,1,0:T(8,128)}, f32[64,512]{1,0:T(8,128)}) custom-call(s32[5]{0:T(128)S(1)} %copy-done.8, bf16[256,1152]{1,0:T(8,128)(2,1)S(1)} %bitcast.17, bf16[528,640]{1,0:T(8,128)(2,1)S(1)} %copy-done.3, f32[16,64,512]{2,1,0:T(8,128)S(1)} %copy-done.2, f32[64,512]{1,0:T(8,128)S(1)} %copy-done.5, ...), custom_call_target="tpu_custom_call" | custom-call | tf_op jit(solution)/shard_map/sweep/pallas_call | solution.py:532
  (54 shorter events, 11.9 us)
Async XLA Ops:
  8.1 21.5 %collective-permute-start = (bf16[8,64,2048]{2,1,0:T(8,128)(2,1)}, bf16[8,64,2048]{2,1,0:T(8,128)(2,1)S(1)}, u32[]{:S(2)}, u32[]{:S(2)}) collective-permute-start(bf16[8,64,2048]{2,1,0:T(8,128)(2,1)} %get-tuple-element.20), channel_id=1, source_target_pairs={{0,8},{8,0},{1,9},{9,1},{2,10},{10,2},{3,11},{11,3},{4,12},{12,4},... | collective-permute-start | bytes 6291464 | tf_op jit(solution)/shard_map/ppermute | solution.py:580
  11.0 15.7 %all-to-all-start = ((f16[16,16,1024]{2,1,0:T(8,128)(2,1)}), f16[16,16,1024]{2,1,0:T(8,128)(2,1)S(1)}, u32[]{:S(2)}, u32[]{:S(2)}) async-start(f16[16,16,1024]{2,1,0:T(8,128)(2,1)} %convert_element_type.21), calls=%async_computation | async-start | bytes 1048576 | tf_op jit(solution)/shard_map/all_to_all | solution.py:592
  17.0 9.9 %collective-permute-start.4 = (f32[8,1152]{1,0:T(8,128)S(1)}, f32[8,1152]{1,0:T(8,128)S(1)}, u32[]{:S(2)}, u32[]{:S(2)}) collective-permute-start(f32[8,1152]{1,0:T(8,128)S(1)} %copy-done.12), channel_id=1, source_target_pairs={{0,7},{1,0},{2,1},{3,2},{4,3},{5,4},{6,5},{7,6},{8,15},{9,8},{10,9... | collective-permute-start | bytes 110600 | tf_op jit(solution)/shard_map/ppermute | solution.py:580
  20.5 7.8 %collective-permute-start.3 = (f32[8,1152]{1,0:T(8,128)S(1)}, f32[8,1152]{1,0:T(8,128)S(1)}, u32[]{:S(2)}, u32[]{:S(2)}) collective-permute-start(f32[8,1152]{1,0:T(8,128)S(1)} %copy-done.12), channel_id=1, source_target_pairs={{0,1},{1,2},{2,3},{3,4},{4,5},{5,6},{6,7},{7,0},{8,9},{9,10},{10,1... | collective-permute-start | bytes 110600 | tf_op jit(solution)/shard_map/ppermute | solution.py:580
  20.5 7.8 %collective-permute-start.1 = (f32[24,512]{1,0:T(8,128)S(1)}, f32[24,512]{1,0:T(8,128)S(1)}, u32[]{:S(2)}, u32[]{:S(2)}) collective-permute-start(f32[24,512]{1,0:T(8,128)S(1)} %copy-done.11), channel_id=1, source_target_pairs={{0,8},{8,16},{16,24},{24,32},{32,40},{40,48},{48,56},{56,64},{64,7... | collective-permute-start | bytes 147464 | tf_op jit(solution)/shard_map/ppermute | solution.py:584
  24.2 5.4 %collective-permute-start.2 = (f32[24,512]{1,0:T(8,128)S(1)}, f32[24,512]{1,0:T(8,128)S(1)}, u32[]{:S(2)}, u32[]{:S(2)}) collective-permute-start(f32[24,512]{1,0:T(8,128)S(1)} %copy-done.10), channel_id=1, source_target_pairs={{8,0},{16,8},{24,16},{32,24},{40,32},{48,40},{56,48},{64,56},{72,6... | collective-permute-start | bytes 147464 | tf_op jit(solution)/shard_map/ppermute | solution.py:584
  26.8 38.0 %copy-start.9 = (f32[2048]{0:T(1024)S(1)}, f32[2048]{0:T(1024)}, u32[]{:S(2)}) copy-start(f32[2048]{0:T(1024)} %param.14) | copy-start | bytes 24580
  31.8 63.7 %copy-start.1 = (bf16[16,64,2048]{2,1,0:T(8,128)(2,1)S(1)}, bf16[16,64,2048]{2,1,0:T(8,128)(2,1)}, u32[]{:S(2)}) copy-start(bf16[16,64,2048]{2,1,0:T(8,128)(2,1)} %own_ref.3) | copy-start | bytes 12582916
  34.7 17.7 %collective-permute-start.5 = (bf16[2,32,2048]{2,1,0:T(8,128)(2,1)S(1)}, bf16[2,32,2048]{2,1,0:T(8,128)(2,1)S(1)}, u32[]{:S(2)}, u32[]{:S(2)}) collective-permute-start(bf16[2,32,2048]{2,1,0:T(8,128)(2,1)S(1)} %get-tuple-element.25), channel_id=1, source_target_pairs={{0,16},{16,32},{32,48},{48,0},{1,17},{17,33},{33,49},{49,1},{2,18}... | collective-permute-start | bytes 786440 | tf_op jit(solution)/shard_map/ppermute | solution.py:580
  35.9 16.4 %collective-permute-start.6 = (bf16[2,32,2048]{2,1,0:T(8,128)(2,1)S(1)}, bf16[2,32,2048]{2,1,0:T(8,128)(2,1)S(1)}, u32[]{:S(2)}, u32[]{:S(2)}) collective-permute-start(bf16[2,32,2048]{2,1,0:T(8,128)(2,1)S(1)} %get-tuple-element.26), channel_id=1, source_target_pairs={{0,32},{16,48},{32,0},{48,16},{1,33},{17,49},{33,1},{49,17},{2,34}... | collective-permute-start | bytes 786440 | tf_op jit(solution)/shard_map/ppermute | solution.py:580
  45.1 8.1 %collective-permute-start.7 = (bf16[2,32,2048]{2,1,0:T(8,128)(2,1)S(1)}, bf16[2,32,2048]{2,1,0:T(8,128)(2,1)S(1)}, u32[]{:S(2)}, u32[]{:S(2)}) collective-permute-start(bf16[2,32,2048]{2,1,0:T(8,128)(2,1)S(1)} %get-tuple-element.27), channel_id=1, source_target_pairs={{0,48},{16,0},{32,16},{48,32},{1,49},{17,1},{33,17},{49,33},{2,50}... | collective-permute-start | bytes 786440 | tf_op jit(solution)/shard_map/ppermute | solution.py:580
  53.9 5.6 %collective-permute-start.8 = (bf16[16,2048]{1,0:T(8,128)(2,1)S(1)}, bf16[16,2048]{1,0:T(8,128)(2,1)S(1)}, u32[]{:S(2)}, u32[]{:S(2)}) collective-permute-start(bf16[16,2048]{1,0:T(8,128)(2,1)S(1)} %get-tuple-element.29), channel_id=1, source_target_pairs={{0,64},{64,128},{128,192},{192,0},{1,65},{65,129},{129,193},{193,1... | collective-permute-start | bytes 196616 | tf_op jit(solution)/shard_map/ppermute | solution.py:580
  57.3 7.5 %collective-permute-start.9 = (bf16[16,2048]{1,0:T(8,128)(2,1)S(1)}, bf16[16,2048]{1,0:T(8,128)(2,1)S(1)}, u32[]{:S(2)}, u32[]{:S(2)}) collective-permute-start(bf16[16,2048]{1,0:T(8,128)(2,1)S(1)} %get-tuple-element.30), channel_id=1, source_target_pairs={{0,128},{64,192},{128,0},{192,64},{1,129},{65,193},{129,1},{193,65... | collective-permute-start | bytes 196616 | tf_op jit(solution)/shard_map/ppermute | solution.py:580
  57.3 7.5 %collective-permute-start.10 = (bf16[16,2048]{1,0:T(8,128)(2,1)S(1)}, bf16[16,2048]{1,0:T(8,128)(2,1)S(1)}, u32[]{:S(2)}, u32[]{:S(2)}) collective-permute-start(bf16[16,2048]{1,0:T(8,128)(2,1)S(1)} %get-tuple-element.31), channel_id=1, source_target_pairs={{0,192},{64,0},{128,64},{192,128},{1,193},{65,1},{129,65},{193,129... | collective-permute-start | bytes 196616 | tf_op jit(solution)/shard_map/ppermute | solution.py:580
  64.9 7.1 %collective-permute-start.13 = (bf16[16,2048]{1,0:T(8,128)(2,1)S(1)}, bf16[16,2048]{1,0:T(8,128)(2,1)S(1)}, u32[]{:S(2)}, u32[]{:S(2)}) collective-permute-start(bf16[16,2048]{1,0:T(8,128)(2,1)S(1)} %multiply_convert_fusion), channel_id=1, source_target_pairs={{0,192},{64,0},{128,64},{192,128},{1,193},{65,1},{129,65},{193,129... | collective-permute-start | bytes 196616 | tf_op jit(solution)/shard_map/ppermute | solution.py:580
  66.2 7.1 %collective-permute-start.12 = (bf16[16,2048]{1,0:T(8,128)(2,1)S(1)}, bf16[16,2048]{1,0:T(8,128)(2,1)S(1)}, u32[]{:S(2)}, u32[]{:S(2)}) collective-permute-start(bf16[16,2048]{1,0:T(8,128)(2,1)S(1)} %multiply_convert_fusion), channel_id=1, source_target_pairs={{0,128},{64,192},{128,0},{192,64},{1,129},{65,193},{129,1},{193,65... | collective-permute-start | bytes 196616 | tf_op jit(solution)/shard_map/ppermute | solution.py:580
  71.4 5.7 %collective-permute-start.11 = (bf16[16,2048]{1,0:T(8,128)(2,1)S(1)}, bf16[16,2048]{1,0:T(8,128)(2,1)S(1)}, u32[]{:S(2)}, u32[]{:S(2)}) collective-permute-start(bf16[16,2048]{1,0:T(8,128)(2,1)S(1)} %multiply_convert_fusion), channel_id=1, source_target_pairs={{0,64},{64,128},{128,192},{192,0},{1,65},{65,129},{129,193},{193,1... | collective-permute-start | bytes 196616 | tf_op jit(solution)/shard_map/ppermute | solution.py:580
  77.1 15.4 %collective-permute-start.16 = (bf16[4,16,2048]{2,1,0:T(8,128)(2,1)S(1)}, bf16[4,16,2048]{2,1,0:T(8,128)(2,1)S(1)}, u32[]{:S(2)}, u32[]{:S(2)}) collective-permute-start(bf16[4,16,2048]{2,1,0:T(8,128)(2,1)S(1)} %pad_maximum_fusion.w0_ref), channel_id=1, source_target_pairs={{0,48},{16,0},{32,16},{48,32},{1,49},{17,1},{33,17},{49,33},{2,50}... | collective-permute-start | bytes 786440 | tf_op jit(solution)/shard_map/ppermute | solution.py:580
  80.1 12.4 %collective-permute-start.15 = (bf16[4,16,2048]{2,1,0:T(8,128)(2,1)S(1)}, bf16[4,16,2048]{2,1,0:T(8,128)(2,1)S(1)}, u32[]{:S(2)}, u32[]{:S(2)}) collective-permute-start(bf16[4,16,2048]{2,1,0:T(8,128)(2,1)S(1)} %pad_maximum_fusion.w0_ref), channel_id=1, source_target_pairs={{0,32},{16,48},{32,0},{48,16},{1,33},{17,49},{33,1},{49,17},{2,34}... | collective-permute-start | bytes 786440 | tf_op jit(solution)/shard_map/ppermute | solution.py:580
  80.1 15.4 %collective-permute-start.14 = (bf16[4,16,2048]{2,1,0:T(8,128)(2,1)S(1)}, bf16[4,16,2048]{2,1,0:T(8,128)(2,1)S(1)}, u32[]{:S(2)}, u32[]{:S(2)}) collective-permute-start(bf16[4,16,2048]{2,1,0:T(8,128)(2,1)S(1)} %pad_maximum_fusion.w0_ref), channel_id=1, source_target_pairs={{0,16},{16,32},{32,48},{48,0},{1,17},{17,33},{33,49},{49,1},{2,18}... | collective-permute-start | bytes 786440 | tf_op jit(solution)/shard_map/ppermute | solution.py:580
  80.7 10.0 %collective-permute-start.18 = (bf16[16,2048]{1,0:T(8,128)(2,1)S(1)}, bf16[16,2048]{1,0:T(8,128)(2,1)S(1)}, u32[]{:S(2)}, u32[]{:S(2)}) collective-permute-start(bf16[16,2048]{1,0:T(8,128)(2,1)S(1)} %get-tuple-element.33), channel_id=1, source_target_pairs={{16,0},{24,8},{32,16},{40,24},{48,32},{56,40},{64,48},{72,56},{80,... | collective-permute-start | bytes 196616 | tf_op jit(solution)/shard_map/ppermute | solution.py:584
  84.4 8.1 %collective-permute-start.17 = (bf16[16,2048]{1,0:T(8,128)(2,1)S(1)}, bf16[16,2048]{1,0:T(8,128)(2,1)S(1)}, u32[]{:S(2)}, u32[]{:S(2)}) collective-permute-start(bf16[16,2048]{1,0:T(8,128)(2,1)S(1)} %get-tuple-element.33), channel_id=1, source_target_pairs={{0,16},{8,24},{16,32},{24,40},{32,48},{40,56},{48,64},{56,72},{64,... | collective-permute-start | bytes 196616 | tf_op jit(solution)/shard_map/ppermute | solution.py:584
  95.5 23.1 %copy-start.3 = (bf16[528,640]{1,0:T(8,128)(2,1)S(1)}, bf16[528,640]{1,0:T(8,128)(2,1)}, u32[]{:S(2)}) copy-start(bf16[528,640]{1,0:T(8,128)(2,1)} %get-tuple-element.34.harm_ref) | copy-start | bytes 2027524
  95.5 23.1 %copy-start.4 = (s32[64,512]{1,0:T(8,128)S(1)}, s32[64,512]{1,0:T(8,128)}, u32[]{:S(2)}) copy-start(s32[64,512]{1,0:T(8,128)} %mask_ref.3) | copy-start | bytes 393220
  (9 other events, 153.3 us)

commit v5 on v4

--- a/solution.py
+++ b/solution.py
@@ -98,16 +98,16 @@
         edge = edge + lax.dot_general(pick, lo, NT, preferred_element_type=F32)
         cols_ref[:, 1024:] = edge[:8]
 
-    field = jnp.concatenate([elev_ref[c] * mask for c in range(4)], axis=0)
+    field = jnp.concatenate([elev_ref[c] * mask for c in range(8)], axis=0)
     hi, lo = split(field)
     both = lax.dot_general(harm_ref[:, :COLS], hi, NT, preferred_element_type=F32)
     small = lax.dot_general(harm_ref[256:, :COLS], lo, NT, preferred_element_type=F32)
     out = both[272:] + (both[:256] + small[16:])
-    part_ref[...] = (out * PART_SCALE).reshape(16, 16, 256).astype(part_ref.dtype)
-    for c in range(4):
-        first_ref[pl.ds(4 * i + c, 1), :] = field[64 * c : 64 * c + 1]
-        last_ref[pl.ds(4 * i + c, 1), :] = field[64 * c + 63 : 64 * c + 64]
-    cols_ref[:, pl.ds(pl.multiple_of(256 * i, 256), 256)] = both[256:264] + small[:8]
+    part_ref[...] = (out * PART_SCALE).reshape(16, 16, 512).astype(part_ref.dtype)
+    for c in range(8):
+        first_ref[pl.ds(8 * i + c, 1), :] = field[64 * c : 64 * c + 1]
+        last_ref[pl.ds(8 * i + c, 1), :] = field[64 * c + 63 : 64 * c + 64]
+    cols_ref[:, pl.ds(pl.multiple_of(512 * i, 512), 512)] = both[256:264] + small[:8]
 
 
 def dft(idx, om, elevation, mask, depth, friction, legendre):
@@ -118,19 +118,19 @@
         dft_kernel,
         grid_spec=pltpu.PrefetchScalarGridSpec(
             num_scalar_prefetch=1,
-            grid=(4,),
+            grid=(2,),
             in_specs=[
                 whole((1, 128)),
-                pl.BlockSpec((4, ROWS, COLS), lambda i, x: (i, 0, 0)),
+                pl.BlockSpec((8, ROWS, COLS), lambda i, x: (i, 0, 0)),
                 whole((ROWS, COLS)),
                 whole((ROWS, COLS)),
                 whole((ROWS, COLS)),
-                pl.BlockSpec((2, ROWS, DEG), lambda i, x: (4 - 4 * x[2] + i, 0, 0)),
+                pl.BlockSpec((4, ROWS, DEG), lambda i, x: (2 - 2 * x[2] + i, 0, 0)),
             ],
             out_specs=[
-                pl.BlockSpec((16, 16, 256), lambda i, x: (0, 0, i)),
+                pl.BlockSpec((16, 16, 512), lambda i, x: (0, 0, i)),
                 whole((528, COLS + 128)),
-                pl.BlockSpec((2, ROWS, DEG), lambda i, x: (i, 0, 0)),
+                pl.BlockSpec((4, ROWS, DEG), lambda i, x: (i, 0, 0)),
                 whole((24, COLS)),
                 whole((24, COLS)),
                 whole((8, 1152)),

time: 129 us -> 128 us (level)
  no operation moved by 1% of the time
where the time goes in v5:
time: 128 us
  starting transfers between devices  48.5 us (38%)
  waiting for transfers between devices  30.8 us (24%)
  Pallas kernels  22.5 us (18%)
  blocking collectives  20 us (16%)
  local copies, waits for them, and re-layouts  2.9 us (2%)
  other arithmetic  2.29 us (2%)
    ppermute x15, starting transfers between devices, shift(): lax.ppermute(value, axes, [(i, (i + step) % size) for i in range(size)])  31.4 us
    ppermute x15, waiting for transfers between devices, shift(): lax.ppermute(value, axes, [(i, (i + step) % size) for i in range(size)])  23 us
    all_to_all x1, blocking collectives, swap(): return lax.all_to_all(x, axis, 0, 0, tiled=True)  20 us
    ppermute x4, starting transfers between devices, shift_lat(): lax.ppermute(value, LAT, [(i, i + step) for i in range(32) if 0 <= i + st...  11.2 us
    pallas_call x1, Pallas kernels, sweep(): pl.pallas_call(sweep_kernel, grid_spec=pltpu.PrefetchScalarGridSpec(num_s...  10.3 us
    ppermute x4, waiting for transfers between devices, shift_lat(): lax.ppermute(value, LAT, [(i, i + step) for i in range(32) if 0 <= i + st...  7.16 us
    all_to_all x1, starting transfers between devices, swap(): return lax.all_to_all(x, axis, 0, 0, tiled=True)  5.95 us
    pallas_call x1, Pallas kernels, dft(): pl.pallas_call(dft_kernel, grid_spec=pltpu.PrefetchScalarGridSpec(num_sca...  5.75 us
  transfers between devices with their start and end apart: 20, of which 11 were waited for; matrix products, arithmetic and copies ran while one was open for 2% of the time, Pallas kernels for 0%

profile of v5, /device:TPU:65, one launch (start us, length us, event | category | flops | bytes accessed | tf_op | source)
XLA Modules:
  0.0 128.0 jit_solution(4611810253063207393)
XLA Ops:
  1.3 5.7 %dft.1 = (f32[16,16,1024]{2,1,0:T(8,128)}, bf16[528,640]{1,0:T(8,128)(2,1)}, bf16[8,64,2048]{2,1,0:T(8,128)(2,1)}, f32[24,512]{1,0:T(8,128)}, f32[24,512]{1,0:T(8,128)}, /*index=5*/f32[8,1152]{1,0:T(8,128)}) custom-call(s32[5]{0:T(128)} %stack.38.idx, s32[1,128]{1,0:T(1,128)} %bitcast.27, f32[16,64,512]{2,1,0:T(8,128)} %elev_ref.3, s32[64,512]{1,0:T(8,128)} %mask_ref.3, ...), custom_call_target="tpu_custom_call" | custom-call | tf_op jit(solution)/shard_map/dft/pallas_call | solution.py:117
  7.8 2.1 %convert_element_type.21 = f16[16,16,1024]{2,1,0:T(8,128)(2,1)} convert(f32[16,16,1024]{2,1,0:T(8,128)} %get-tuple-element.19) | non-fusion elementwise | flops 262144 | bytes 1572864 | tf_op jit(solution)/shard_map/convert_element_type | solution.py:605
  10.0 6.0 %all-to-all-start = ((f16[16,16,1024]{2,1,0:T(8,128)(2,1)}), f16[16,16,1024]{2,1,0:T(8,128)(2,1)S(1)}, u32[]{:S(2)}, u32[]{:S(2)}) async-start(f16[16,16,1024]{2,1,0:T(8,128)(2,1)} %convert_element_type.21), calls=%async_computation | async-start | bytes 1048576 | tf_op jit(solution)/shard_map/all_to_all | solution.py:592
  15.9 3.6 %collective-permute-start.4 = (f32[8,1152]{1,0:T(8,128)S(1)}, f32[8,1152]{1,0:T(8,128)S(1)}, u32[]{:S(2)}, u32[]{:S(2)}) collective-permute-start(f32[8,1152]{1,0:T(8,128)S(1)} %copy-done.12), channel_id=1, source_target_pairs={{0,7},{1,0},{2,1},{3,2},{4,3},{5,4},{6,5},{7,6},{8,15},{9,8},{10,9... | collective-permute-start | bytes 110600 | tf_op jit(solution)/shard_map/ppermute | solution.py:580
  19.5 3.6 %collective-permute-start.1 = (f32[24,512]{1,0:T(8,128)S(1)}, f32[24,512]{1,0:T(8,128)S(1)}, u32[]{:S(2)}, u32[]{:S(2)}) collective-permute-start(f32[24,512]{1,0:T(8,128)S(1)} %copy-done.11), channel_id=1, source_target_pairs={{0,8},{8,16},{16,24},{24,32},{32,40},{40,48},{48,56},{56,64},{64,7... | collective-permute-start | bytes 147464 | tf_op jit(solution)/shard_map/ppermute | solution.py:584
  23.2 1.9 %collective-permute-start.2 = (f32[24,512]{1,0:T(8,128)S(1)}, f32[24,512]{1,0:T(8,128)S(1)}, u32[]{:S(2)}, u32[]{:S(2)}) collective-permute-start(f32[24,512]{1,0:T(8,128)S(1)} %copy-done.10), channel_id=1, source_target_pairs={{8,0},{16,8},{24,16},{32,24},{40,32},{48,40},{56,48},{64,56},{72,6... | collective-permute-start | bytes 147464 | tf_op jit(solution)/shard_map/ppermute | solution.py:584
  28.6 2.2 %copy-done = bf16[16,64,2048]{2,1,0:T(8,128)(2,1)S(1)} copy-done((bf16[16,64,2048]{2,1,0:T(8,128)(2,1)S(1)}, bf16[16,64,2048]{2,1,0:T(8,128)(2,1)}, u32[]{:S(2)}) %copy-start) | copy-done | bytes 4194328
  30.8 2.8 %analyse.1 = (f32[2,32,2048]{2,1,0:T(8,128)S(1)}, bf16[2,32,2048]{2,1,0:T(8,128)(2,1)S(1)}, bf16[2,32,2048]{2,1,0:T(8,128)(2,1)S(1)}, bf16[2,32,2048]{2,1,0:T(8,...) custom-call(s32[5]{0:T(128)S(1)} %copy-done.8, ...), custom_call_target="tpu_custom_call" | custom-call | tf_op jit(solution)/shard_map/analyse/pallas_call | solution.py:196
  34.9 9.2 %collective-permute-start.6 = (bf16[2,32,2048]{2,1,0:T(8,128)(2,1)S(1)}, bf16[2,32,2048]{2,1,0:T(8,128)(2,1)S(1)}, u32[]{:S(2)}, u32[]{:S(2)}) collective-permute-start(bf16[2,32,2048]{2,1,0:T(8,128)(2,1)S(1)} %get-tuple-element.26), channel_id=1, source_target_pairs={{0,32},{16,48},{32,0},{48,16},{1,33},{17,49},{33,1},{49,17},{2,34}... | collective-permute-start | bytes 786440 | tf_op jit(solution)/shard_map/ppermute | solution.py:580
  44.1 7.2 %collective-permute-done.5 = bf16[2,32,2048]{2,1,0:T(8,128)(2,1)S(1)} collective-permute-done((bf16[2,32,2048]{2,1,0:T(8,128)(2,1)S(1)}, bf16[2,32,2048]{2,1,0:T(8,128)(2,1)S(1)}, u32[]{:S(2)}, u32[]{:S(2)}) %collective-permute-start.5) | collective-permute-done | bytes 262176 | tf_op jit(solution)/shard_map/ppermute | solution.py:580
  52.9 3.4 %collective-permute-start.8 = (bf16[16,2048]{1,0:T(8,128)(2,1)S(1)}, bf16[16,2048]{1,0:T(8,128)(2,1)S(1)}, u32[]{:S(2)}, u32[]{:S(2)}) collective-permute-start(bf16[16,2048]{1,0:T(8,128)(2,1)S(1)} %get-tuple-element.29), channel_id=1, source_target_pairs={{0,64},{64,128},{128,192},{192,0},{1,65},{65,129},{129,193},{193,1... | collective-permute-start | bytes 196616 | tf_op jit(solution)/shard_map/ppermute | solution.py:580
  56.3 2.2 %collective-permute-start.10 = (bf16[16,2048]{1,0:T(8,128)(2,1)S(1)}, bf16[16,2048]{1,0:T(8,128)(2,1)S(1)}, u32[]{:S(2)}, u32[]{:S(2)}) collective-permute-start(bf16[16,2048]{1,0:T(8,128)(2,1)S(1)} %get-tuple-element.31), channel_id=1, source_target_pairs={{0,192},{64,0},{128,64},{192,128},{1,193},{65,1},{129,65},{193,129... | collective-permute-start | bytes 196616 | tf_op jit(solution)/shard_map/ppermute | solution.py:580
  58.5 5.3 %collective-permute-done.9 = bf16[16,2048]{1,0:T(8,128)(2,1)S(1)} collective-permute-done((bf16[16,2048]{1,0:T(8,128)(2,1)S(1)}, bf16[16,2048]{1,0:T(8,128)(2,1)S(1)}, u32[]{:S(2)}, u32[]{:S(2)}) %collective-permute-start.9) | collective-permute-done | bytes 65568 | tf_op jit(solution)/shard_map/ppermute | solution.py:580
  65.2 5.1 %collective-permute-start.12 = (bf16[16,2048]{1,0:T(8,128)(2,1)S(1)}, bf16[16,2048]{1,0:T(8,128)(2,1)S(1)}, u32[]{:S(2)}, u32[]{:S(2)}) collective-permute-start(bf16[16,2048]{1,0:T(8,128)(2,1)S(1)} %multiply_convert_fusion), channel_id=1, source_target_pairs={{0,128},{64,192},{128,0},{192,64},{1,129},{65,193},{129,1},{193,65... | collective-permute-start | bytes 196616 | tf_op jit(solution)/shard_map/ppermute | solution.py:580
  72.3 3.7 %collective-permute-done.11 = bf16[16,2048]{1,0:T(8,128)(2,1)S(1)} collective-permute-done((bf16[16,2048]{1,0:T(8,128)(2,1)S(1)}, bf16[16,2048]{1,0:T(8,128)(2,1)S(1)}, u32[]{:S(2)}, u32[]{:S(2)}) %collective-permute-start.11) | collective-permute-done | bytes 65568 | tf_op jit(solution)/shard_map/ppermute | solution.py:580
  76.0 3.0 %collective-permute-start.16 = (bf16[4,16,2048]{2,1,0:T(8,128)(2,1)S(1)}, bf16[4,16,2048]{2,1,0:T(8,128)(2,1)S(1)}, u32[]{:S(2)}, u32[]{:S(2)}) collective-permute-start(bf16[4,16,2048]{2,1,0:T(8,128)(2,1)S(1)} %pad_maximum_fusion.w0_ref), channel_id=1, source_target_pairs={{0,48},{16,0},{32,16},{48,32},{1,49},{17,1},{33,17},{49,33},{2,50}... | collective-permute-start | bytes 786440 | tf_op jit(solution)/shard_map/ppermute | solution.py:580
  79.9 3.4 %collective-permute-start.18 = (bf16[16,2048]{1,0:T(8,128)(2,1)S(1)}, bf16[16,2048]{1,0:T(8,128)(2,1)S(1)}, u32[]{:S(2)}, u32[]{:S(2)}) collective-permute-start(bf16[16,2048]{1,0:T(8,128)(2,1)S(1)} %get-tuple-element.33), channel_id=1, source_target_pairs={{16,0},{24,8},{32,16},{40,24},{48,32},{56,40},{64,48},{72,56},{80,... | collective-permute-start | bytes 196616 | tf_op jit(solution)/shard_map/ppermute | solution.py:584
  83.4 2.2 %collective-permute-start.17 = (bf16[16,2048]{1,0:T(8,128)(2,1)S(1)}, bf16[16,2048]{1,0:T(8,128)(2,1)S(1)}, u32[]{:S(2)}, u32[]{:S(2)}) collective-permute-start(bf16[16,2048]{1,0:T(8,128)(2,1)S(1)} %get-tuple-element.33), channel_id=1, source_target_pairs={{0,16},{8,24},{16,32},{24,40},{32,48},{40,56},{48,64},{56,72},{64,... | collective-permute-start | bytes 196616 | tf_op jit(solution)/shard_map/ppermute | solution.py:584
  85.5 4.1 %collective-permute-done.18.next_ref = bf16[16,2048]{1,0:T(8,128)(2,1)S(1)} collective-permute-done((bf16[16,2048]{1,0:T(8,128)(2,1)S(1)}, bf16[16,2048]{1,0:T(8,128)(2,1)S(1)}, u32[]{:S(2)}, u32[]{:S(2)}) %collective-permute-start.18) | collective-permute-done | bytes 65568 | tf_op jit(solution)/shard_map/ppermute | solution.py:584
  89.7 1.8 %collective-permute-done.17.prev_ref = bf16[16,2048]{1,0:T(8,128)(2,1)S(1)} collective-permute-done((bf16[16,2048]{1,0:T(8,128)(2,1)S(1)}, bf16[16,2048]{1,0:T(8,128)(2,1)S(1)}, u32[]{:S(2)}, u32[]{:S(2)}) %collective-permute-start.17) | collective-permute-done | bytes 65568 | tf_op jit(solution)/shard_map/ppermute | solution.py:584
  91.4 3.0 %collective-permute-done.14.w1_ref = bf16[4,16,2048]{2,1,0:T(8,128)(2,1)S(1)} collective-permute-done((bf16[4,16,2048]{2,1,0:T(8,128)(2,1)S(1)}, bf16[4,16,2048]{2,1,0:T(8,128)(2,1)S(1)}, u32[]{:S(2)}, u32[]{:S(2)}) %collective-permute-start.14) | collective-permute-done | bytes 262176 | tf_op jit(solution)/shard_map/ppermute | solution.py:580
  94.5 3.0 %synthesise.1 = bf16[16,16,1152]{2,1,0:T(8,128)(2,1)S(1)} custom-call(s32[5]{0:T(128)S(1)} %copy-done.8, bf16[4,16,2048]{2,1,0:T(8,128)(2,1)S(1)} %pad_maximum_fusion.w0_ref, bf16[4,16,2048]{2,1,0:T(8,128)(2,1)S(1)} %collective-permute-done.14.w1_ref, bf16[4,16,2048]{2,1,0:T(8,128)(2,1)S(1)} %collective-permute-done.15.w2_ref, ...), custom_call_target="tpu_custom_call" | custom-call | tf_op jit(solution)/shard_map/synthesise/pallas_call | solution.py:312
  97.6 20.0 %all_to_all.10 = bf16[16,16,1152]{2,1,0:T(8,128)(2,1)S(1)} all-to-all(bf16[16,16,1152]{2,1,0:T(8,128)(2,1)S(1)} %synthesise.1), channel_id=1, replica_groups=mesh['zh'=4,'x'=4,'c'=2,'y'=4,'zl'=2] {'y','zl','c'}, dimensions={0} | all-to-all | bytes 1179648 | tf_op jit(solution)/shard_map/all_to_all | solution.py:592
  117.5 10.3 %sweep.1 = (f32[16,64,512]{2,1,0:T(8,128)}, f32[16,64,512]{2,1,0:T(8,128)}, f32[64,512]{1,0:T(8,128)}) custom-call(s32[5]{0:T(128)S(1)} %copy-done.8, bf16[256,1152]{1,0:T(8,128)(2,1)S(1)} %bitcast.17, bf16[528,640]{1,0:T(8,128)(2,1)S(1)} %copy-done.3, f32[16,64,512]{2,1,0:T(8,128)S(1)} %copy-done.2, f32[64,512]{1,0:T(8,128)S(1)} %copy-done.5, ...), custom_call_target="tpu_custom_call" | custom-call | tf_op jit(solution)/shard_map/sweep/pallas_call | solution.py:532
  (54 shorter events, 12.1 us)
Async XLA Ops:
  7.1 21.5 %collective-permute-start = (bf16[8,64,2048]{2,1,0:T(8,128)(2,1)}, bf16[8,64,2048]{2,1,0:T(8,128)(2,1)S(1)}, u32[]{:S(2)}, u32[]{:S(2)}) collective-permute-start(bf16[8,64,2048]{2,1,0:T(8,128)(2,1)} %get-tuple-element.20), channel_id=1, source_target_pairs={{0,8},{8,0},{1,9},{9,1},{2,10},{10,2},{3,11},{11,3},{4,12},{12,4},... | collective-permute-start | bytes 6291464 | tf_op jit(solution)/shard_map/ppermute | solution.py:580
  10.0 15.8 %all-to-all-start = ((f16[16,16,1024]{2,1,0:T(8,128)(2,1)}), f16[16,16,1024]{2,1,0:T(8,128)(2,1)S(1)}, u32[]{:S(2)}, u32[]{:S(2)}) async-start(f16[16,16,1024]{2,1,0:T(8,128)(2,1)} %convert_element_type.21), calls=%async_computation | async-start | bytes 1048576 | tf_op jit(solution)/shard_map/all_to_all | solution.py:592
  15.9 9.9 %collective-permute-start.4 = (f32[8,1152]{1,0:T(8,128)S(1)}, f32[8,1152]{1,0:T(8,128)S(1)}, u32[]{:S(2)}, u32[]{:S(2)}) collective-permute-start(f32[8,1152]{1,0:T(8,128)S(1)} %copy-done.12), channel_id=1, source_target_pairs={{0,7},{1,0},{2,1},{3,2},{4,3},{5,4},{6,5},{7,6},{8,15},{9,8},{10,9... | collective-permute-start | bytes 110600 | tf_op jit(solution)/shard_map/ppermute | solution.py:580
  19.5 7.8 %collective-permute-start.3 = (f32[8,1152]{1,0:T(8,128)S(1)}, f32[8,1152]{1,0:T(8,128)S(1)}, u32[]{:S(2)}, u32[]{:S(2)}) collective-permute-start(f32[8,1152]{1,0:T(8,128)S(1)} %copy-done.12), channel_id=1, source_target_pairs={{0,1},{1,2},{2,3},{3,4},{4,5},{5,6},{6,7},{7,0},{8,9},{9,10},{10,1... | collective-permute-start | bytes 110600 | tf_op jit(solution)/shard_map/ppermute | solution.py:580
  19.5 7.8 %collective-permute-start.1 = (f32[24,512]{1,0:T(8,128)S(1)}, f32[24,512]{1,0:T(8,128)S(1)}, u32[]{:S(2)}, u32[]{:S(2)}) collective-permute-start(f32[24,512]{1,0:T(8,128)S(1)} %copy-done.11), channel_id=1, source_target_pairs={{0,8},{8,16},{16,24},{24,32},{32,40},{40,48},{48,56},{56,64},{64,7... | collective-permute-start | bytes 147464 | tf_op jit(solution)/shard_map/ppermute | solution.py:584
  23.2 5.4 %collective-permute-start.2 = (f32[24,512]{1,0:T(8,128)S(1)}, f32[24,512]{1,0:T(8,128)S(1)}, u32[]{:S(2)}, u32[]{:S(2)}) collective-permute-start(f32[24,512]{1,0:T(8,128)S(1)} %copy-done.10), channel_id=1, source_target_pairs={{8,0},{16,8},{24,16},{32,24},{40,32},{48,40},{56,48},{64,56},{72,6... | collective-permute-start | bytes 147464 | tf_op jit(solution)/shard_map/ppermute | solution.py:584
  25.8 38.0 %copy-start.9 = (f32[2048]{0:T(1024)S(1)}, f32[2048]{0:T(1024)}, u32[]{:S(2)}) copy-start(f32[2048]{0:T(1024)} %param.14) | copy-start | bytes 24580
  30.8 63.7 %copy-start.1 = (bf16[16,64,2048]{2,1,0:T(8,128)(2,1)S(1)}, bf16[16,64,2048]{2,1,0:T(8,128)(2,1)}, u32[]{:S(2)}) copy-start(bf16[16,64,2048]{2,1,0:T(8,128)(2,1)} %own_ref.3) | copy-start | bytes 12582916
  33.6 17.7 %collective-permute-start.5 = (bf16[2,32,2048]{2,1,0:T(8,128)(2,1)S(1)}, bf16[2,32,2048]{2,1,0:T(8,128)(2,1)S(1)}, u32[]{:S(2)}, u32[]{:S(2)}) collective-permute-start(bf16[2,32,2048]{2,1,0:T(8,128)(2,1)S(1)} %get-tuple-element.25), channel_id=1, source_target_pairs={{0,16},{16,32},{32,48},{48,0},{1,17},{17,33},{33,49},{49,1},{2,18}... | collective-permute-start | bytes 786440 | tf_op jit(solution)/shard_map/ppermute | solution.py:580
  34.9 16.4 %collective-permute-start.6 = (bf16[2,32,2048]{2,1,0:T(8,128)(2,1)S(1)}, bf16[2,32,2048]{2,1,0:T(8,128)(2,1)S(1)}, u32[]{:S(2)}, u32[]{:S(2)}) collective-permute-start(bf16[2,32,2048]{2,1,0:T(8,128)(2,1)S(1)} %get-tuple-element.26), channel_id=1, source_target_pairs={{0,32},{16,48},{32,0},{48,16},{1,33},{17,49},{33,1},{49,17},{2,34}... | collective-permute-start | bytes 786440 | tf_op jit(solution)/shard_map/ppermute | solution.py:580
  44.1 8.1 %collective-permute-start.7 = (bf16[2,32,2048]{2,1,0:T(8,128)(2,1)S(1)}, bf16[2,32,2048]{2,1,0:T(8,128)(2,1)S(1)}, u32[]{:S(2)}, u32[]{:S(2)}) collective-permute-start(bf16[2,32,2048]{2,1,0:T(8,128)(2,1)S(1)} %get-tuple-element.27), channel_id=1, source_target_pairs={{0,48},{16,0},{32,16},{48,32},{1,49},{17,1},{33,17},{49,33},{2,50}... | collective-permute-start | bytes 786440 | tf_op jit(solution)/shard_map/ppermute | solution.py:580
  52.9 5.6 %collective-permute-start.8 = (bf16[16,2048]{1,0:T(8,128)(2,1)S(1)}, bf16[16,2048]{1,0:T(8,128)(2,1)S(1)}, u32[]{:S(2)}, u32[]{:S(2)}) collective-permute-start(bf16[16,2048]{1,0:T(8,128)(2,1)S(1)} %get-tuple-element.29), channel_id=1, source_target_pairs={{0,64},{64,128},{128,192},{192,0},{1,65},{65,129},{129,193},{193,1... | collective-permute-start | bytes 196616 | tf_op jit(solution)/shard_map/ppermute | solution.py:580
  56.3 7.5 %collective-permute-start.9 = (bf16[16,2048]{1,0:T(8,128)(2,1)S(1)}, bf16[16,2048]{1,0:T(8,128)(2,1)S(1)}, u32[]{:S(2)}, u32[]{:S(2)}) collective-permute-start(bf16[16,2048]{1,0:T(8,128)(2,1)S(1)} %get-tuple-element.30), channel_id=1, source_target_pairs={{0,128},{64,192},{128,0},{192,64},{1,129},{65,193},{129,1},{193,65... | collective-permute-start | bytes 196616 | tf_op jit(solution)/shard_map/ppermute | solution.py:580
  56.3 7.5 %collective-permute-start.10 = (bf16[16,2048]{1,0:T(8,128)(2,1)S(1)}, bf16[16,2048]{1,0:T(8,128)(2,1)S(1)}, u32[]{:S(2)}, u32[]{:S(2)}) collective-permute-start(bf16[16,2048]{1,0:T(8,128)(2,1)S(1)} %get-tuple-element.31), channel_id=1, source_target_pairs={{0,192},{64,0},{128,64},{192,128},{1,193},{65,1},{129,65},{193,129... | collective-permute-start | bytes 196616 | tf_op jit(solution)/shard_map/ppermute | solution.py:580
  63.8 7.1 %collective-permute-start.13 = (bf16[16,2048]{1,0:T(8,128)(2,1)S(1)}, bf16[16,2048]{1,0:T(8,128)(2,1)S(1)}, u32[]{:S(2)}, u32[]{:S(2)}) collective-permute-start(bf16[16,2048]{1,0:T(8,128)(2,1)S(1)} %multiply_convert_fusion), channel_id=1, source_target_pairs={{0,192},{64,0},{128,64},{192,128},{1,193},{65,1},{129,65},{193,129... | collective-permute-start | bytes 196616 | tf_op jit(solution)/shard_map/ppermute | solution.py:580
  65.2 7.1 %collective-permute-start.12 = (bf16[16,2048]{1,0:T(8,128)(2,1)S(1)}, bf16[16,2048]{1,0:T(8,128)(2,1)S(1)}, u32[]{:S(2)}, u32[]{:S(2)}) collective-permute-start(bf16[16,2048]{1,0:T(8,128)(2,1)S(1)} %multiply_convert_fusion), channel_id=1, source_target_pairs={{0,128},{64,192},{128,0},{192,64},{1,129},{65,193},{129,1},{193,65... | collective-permute-start | bytes 196616 | tf_op jit(solution)/shard_map/ppermute | solution.py:580
  70.4 5.7 %collective-permute-start.11 = (bf16[16,2048]{1,0:T(8,128)(2,1)S(1)}, bf16[16,2048]{1,0:T(8,128)(2,1)S(1)}, u32[]{:S(2)}, u32[]{:S(2)}) collective-permute-start(bf16[16,2048]{1,0:T(8,128)(2,1)S(1)} %multiply_convert_fusion), channel_id=1, source_target_pairs={{0,64},{64,128},{128,192},{192,0},{1,65},{65,129},{129,193},{193,1... | collective-permute-start | bytes 196616 | tf_op jit(solution)/shard_map/ppermute | solution.py:580
  76.0 15.4 %collective-permute-start.16 = (bf16[4,16,2048]{2,1,0:T(8,128)(2,1)S(1)}, bf16[4,16,2048]{2,1,0:T(8,128)(2,1)S(1)}, u32[]{:S(2)}, u32[]{:S(2)}) collective-permute-start(bf16[4,16,2048]{2,1,0:T(8,128)(2,1)S(1)} %pad_maximum_fusion.w0_ref), channel_id=1, source_target_pairs={{0,48},{16,0},{32,16},{48,32},{1,49},{17,1},{33,17},{49,33},{2,50}... | collective-permute-start | bytes 786440 | tf_op jit(solution)/shard_map/ppermute | solution.py:580
  79.1 12.4 %collective-permute-start.15 = (bf16[4,16,2048]{2,1,0:T(8,128)(2,1)S(1)}, bf16[4,16,2048]{2,1,0:T(8,128)(2,1)S(1)}, u32[]{:S(2)}, u32[]{:S(2)}) collective-permute-start(bf16[4,16,2048]{2,1,0:T(8,128)(2,1)S(1)} %pad_maximum_fusion.w0_ref), channel_id=1, source_target_pairs={{0,32},{16,48},{32,0},{48,16},{1,33},{17,49},{33,1},{49,17},{2,34}... | collective-permute-start | bytes 786440 | tf_op jit(solution)/shard_map/ppermute | solution.py:580
  79.1 15.4 %collective-permute-start.14 = (bf16[4,16,2048]{2,1,0:T(8,128)(2,1)S(1)}, bf16[4,16,2048]{2,1,0:T(8,128)(2,1)S(1)}, u32[]{:S(2)}, u32[]{:S(2)}) collective-permute-start(bf16[4,16,2048]{2,1,0:T(8,128)(2,1)S(1)} %pad_maximum_fusion.w0_ref), channel_id=1, source_target_pairs={{0,16},{16,32},{32,48},{48,0},{1,17},{17,33},{33,49},{49,1},{2,18}... | collective-permute-start | bytes 786440 | tf_op jit(solution)/shard_map/ppermute | solution.py:580
  79.9 9.7 %collective-permute-start.18 = (bf16[16,2048]{1,0:T(8,128)(2,1)S(1)}, bf16[16,2048]{1,0:T(8,128)(2,1)S(1)}, u32[]{:S(2)}, u32[]{:S(2)}) collective-permute-start(bf16[16,2048]{1,0:T(8,128)(2,1)S(1)} %get-tuple-element.33), channel_id=1, source_target_pairs={{16,0},{24,8},{32,16},{40,24},{48,32},{56,40},{64,48},{72,56},{80,... | collective-permute-start | bytes 196616 | tf_op jit(solution)/shard_map/ppermute | solution.py:584
  83.4 8.1 %collective-permute-start.17 = (bf16[16,2048]{1,0:T(8,128)(2,1)S(1)}, bf16[16,2048]{1,0:T(8,128)(2,1)S(1)}, u32[]{:S(2)}, u32[]{:S(2)}) collective-permute-start(bf16[16,2048]{1,0:T(8,128)(2,1)S(1)} %get-tuple-element.33), channel_id=1, source_target_pairs={{0,16},{8,24},{16,32},{24,40},{32,48},{40,56},{48,64},{56,72},{64,... | collective-permute-start | bytes 196616 | tf_op jit(solution)/shard_map/ppermute | solution.py:584
  94.5 23.0 %copy-start.3 = (bf16[528,640]{1,0:T(8,128)(2,1)S(1)}, bf16[528,640]{1,0:T(8,128)(2,1)}, u32[]{:S(2)}) copy-start(bf16[528,640]{1,0:T(8,128)(2,1)} %get-tuple-element.34.harm_ref) | copy-start | bytes 2027524
  94.5 23.0 %copy-start.4 = (s32[64,512]{1,0:T(8,128)S(1)}, s32[64,512]{1,0:T(8,128)}, u32[]{:S(2)}) copy-start(s32[64,512]{1,0:T(8,128)} %mask_ref.3) | copy-start | bytes 393220
  (9 other events, 153.2 us)
